TPU v7x, 512 devices: a whole 4x4x16 slice. The times are simulated.
512 devices in a mesh: sky: 128 (over z, x, core), tm: 4 (over y).
Axes of the slice: x: 4, y: 4, z: 16, core: 2. Of those that a mesh axis runs over, the one named last changes fastest.
Arguments:
- star_pos: float32 [1024, 3, 512], P(('sky', 'tm'))
- noise_var: float32 [1024, 512], P(('sky', 'tm')), may hold values from 0.5 to 2
- targets: float32 [1024, 64, 512], P(('sky', 'tm'))
- pair_list: int32 [1024, 14], P(('sky', 'tm')), may hold values from -1 to 1023, as said below
Outputs:
- solution: float32 [1024, 64, 512], P(('sky', 'tm'))
- residual: float32 [1024, 64, 512], P(('sky', 'tm'))
Inputs may be any that keep to these rules, and one draw needn't show every extreme that they name: `pair_list`: row g lists first the ids of the blocks whose pair with g is evaluated at g, then -1 in the remaining slots. Each evaluated pair of distinct blocks is listed exactly once, at one of its two blocks, and only the listed pairs take part in the operator; a listed partner lies on the same device or on a device adjacent along sky, along tm or both.
All inputs are finite; a program needn't handle non-finite values.
Results may differ from a plain program's by a relative error of at most 0.00035.
Values sent between devices are 32-bit elements; how exact they have to be, the bound alone decides.
No kernel may reach another device: no remote copies, remote signals or barrier semaphores. Data moves between devices by JAX's collectives and lax.ppermute only.
A program may use at most 64 MiB of HBM per device.

v0:
```python
import jax
import jax.numpy as jnp
from jax import lax
from jax.sharding import PartitionSpec as P

ITERS = 2


def with_halo(block, sides, width):
    for axis, dim in sides:
        count = lax.axis_size(axis)
        forward = [(i, i + 1) for i in range(count - 1)]
        backward = [(target, source) for source, target in forward]
        low = lax.ppermute(
            lax.slice_in_dim(block, block.shape[dim] - width, None, axis=dim), axis, forward
        )
        high = lax.ppermute(lax.slice_in_dim(block, 0, width, axis=dim), axis, backward)
        block = jnp.concatenate([low, block, high], axis=dim)
    return block


def from_behind(shard, axis, by):
    length = lax.axis_size(axis)
    pairs = [(i, i + by) for i in range(length) if 0 <= i + by < length]
    return lax.ppermute(shard, axis, pairs)


def kernel_tile(left_pos, right_pos):
    squared = jnp.zeros((left_pos.shape[1], right_pos.shape[1]), jnp.float32)
    for component in range(3):
        offset = left_pos[component][:, None] - right_pos[component][None, :]
        squared = squared + offset * offset
    radius = jnp.sqrt(squared)
    margin = jnp.maximum(1.0 - radius, 0.0)
    margin_sq = margin * margin
    return margin_sq * margin_sq * (4.0 * radius + 1.0) * 0.3


def pull(vector, panel):
    return lax.dot_general(vector, panel, (((1,), (1,)), ((), ())), precision=lax.Precision.HIGHEST)


def push(vector, panel):
    return lax.dot_general(vector, panel, (((1,), (0,)), ((), ())), precision=lax.Precision.HIGHEST)


def local(star_pos, noise_var, targets, pair_list):
    sky_index = lax.axis_index("sky")
    epoch_index = lax.axis_index("tm")
    epochs = lax.axis_size("tm")
    blocks, width, stars = targets.shape
    places = with_halo(star_pos[None, None], (("sky", 0), ("tm", 1)), 1)
    counts = jnp.sum((pair_list >= 0).astype(jnp.int32), axis=1)
    self_tiles = jax.vmap(kernel_tile)(star_pos, star_pos)

    def locate(partner):
        owner = partner // blocks
        return (owner // epochs - sky_index + 1, owner % epochs - epoch_index + 1, partner % blocks)

    solution = jnp.zeros_like(targets)
    residual = targets
    direction = targets
    norm_now = lax.psum(jnp.sum(residual * residual, axis=(0, 2)), ("sky", "tm"))
    for iteration in range(ITERS):
        vector = direction
        rim_vec = with_halo(vector[None, None], (("sky", 0), ("tm", 1)), 1)
        selfpart = lax.dot_general(
            vector, self_tiles, (((2,), (2,)), ((0,), (0,))), precision=lax.Precision.HIGHEST
        )
        result = noise_var[:, None, :] * vector + selfpart
        returned = jnp.zeros((3, 3, blocks, width, stars), jnp.float32)

        def per_block(block_at, totals):

            def per_slot(slot_at, totals):
                partial_value, returned = totals
                partner = pair_list[block_at, slot_at]
                row_slot, col_slot, block_slot = locate(partner)
                panel = kernel_tile(star_pos[block_at], places[row_slot, col_slot, block_slot])
                partial_value = partial_value.at[block_at].add(
                    pull(rim_vec[row_slot, col_slot, block_slot], panel)
                )
                returned = returned.at[row_slot, col_slot, block_slot].add(
                    push(vector[block_at], panel)
                )
                return (partial_value, returned)

            return lax.fori_loop(0, counts[block_at], per_slot, totals)

        result, returned = lax.fori_loop(0, blocks, per_block, (result, returned))
        rows_sum = returned[:, 1]
        for offset_by, col_slot in ((1, 2), (-1, 0)):
            rows_sum = rows_sum + from_behind(returned[:, col_slot], "tm", offset_by)
        gathered = rows_sum[1]
        for offset_by, row_slot in ((1, 2), (-1, 0)):
            gathered = gathered + from_behind(rows_sum[row_slot], "sky", offset_by)
        image = result + gathered
        curve = lax.psum(jnp.sum(direction * image, axis=(0, 2)), ("sky", "tm"))
        alpha = norm_now / curve
        solution = solution + alpha[None, :, None] * direction
        residual = residual - alpha[None, :, None] * image
        norm_next = lax.psum(jnp.sum(residual * residual, axis=(0, 2)), ("sky", "tm"))
        if iteration + 1 < ITERS:
            direction = residual + (norm_next / norm_now)[None, :, None] * direction
        norm_now = norm_next
    return (solution, residual)


def solution(mesh):
    in_specs = (
        P(("sky", "tm"), None, None),
        P(("sky", "tm"), None),
        P(("sky", "tm"), None, None),
        P(("sky", "tm"), None),
    )
    out_specs = (P(("sky", "tm"), None, None), P(("sky", "tm"), None, None))
    return jax.shard_map(local, mesh=mesh, in_specs=in_specs, out_specs=out_specs, check_vma=False)
```

profile of v0, /device:TPU:1, one launch (start us, length us, event | category | flops | bytes accessed | tf_op | source)
XLA Modules:
  0.0 794.1 jit_solution(5982830872285919936)
XLA Ops:
  0.6 4.5 collective-permute-start
  5.1 5.6 collective-permute-start.1
  11.5 1.9 collective-permute-start.4
  13.4 2.4 collective-permute-start.5
  15.8 1.0 pad_maximum_fusion.2
  16.8 1.3 collective-permute-start.2
  18.2 1.3 collective-permute-start.3
  19.5 0.7 slice_bitcast_fusion.14
  20.2 5.7 fusion.36
  26.0 4.0 collective-permute-start.6
  29.9 1.3 collective-permute-start.7
  31.4 4.7 collective-permute-done.6
  36.1 4.3 collective-permute-done.7
  40.4 1.7 pad_maximum_fusion
  43.1 34.5 %while.103 = (s32[]{:T(128)}, f32[2,64,512]{2,1,0:T(8,128)S(1)}, f32[3,3,2,64,512]{4,3,2,1,0:T(8,128)S(1)}, s32[2]{0:T(128)S(1)}, f32[2,3,512]{2,1,0:T(4,128)S(1...) while((s32[]{:T(128)}, f32[2,64,512]{2,1,0:T(8,128)S(1)}, ...), condition=%wide.region_8.9_spmd, body=%wide.region_3.8_spmd.sunk | while | flops 411172928 | bytes 1114029 | solution.py:90
  43.8 11.2 %while.106 = (s32[]{:T(128)}, f32[2,64,512]{2,1,0:T(8,128)S(1)}, f32[3,3,2,64,512]{4,3,2,1,0:T(8,128)S(1)}, s32[]{:T(128)}, s32[3]{0:T(128)S(1)}, /*index=5*/pre...) while((s32[]{:T(128)}, f32[2,64,512]{2,1,0:T(8,128)S(1)}, ...), condition=%wide.region_7.7_spmd, body=%wide.region_4.6_spmd.sunk | while | flops 411172928 | bytes 839089 | solution.py:88
  48.2 2.2 fusion.91
  51.0 3.4 fusion.90
  55.8 21.8 %while.106 = (s32[]{:T(128)}, f32[2,64,512]{2,1,0:T(8,128)S(1)}, f32[3,3,2,64,512]{4,3,2,1,0:T(8,128)S(1)}, s32[]{:T(128)}, s32[3]{0:T(128)S(1)}, /*index=5*/pre...) while((s32[]{:T(128)}, f32[2,64,512]{2,1,0:T(8,128)S(1)}, ...), condition=%wide.region_7.7_spmd, body=%wide.region_4.6_spmd.sunk | while | flops 411172928 | bytes 839089 | solution.py:88
  60.1 2.2 fusion.91
  63.0 3.4 fusion.90
  70.7 2.2 fusion.91
  73.6 3.4 fusion.90
  77.8 75.8 %collective-permute-start.8 = (f32[3,2,64,512]{3,2,1,0:T(8,128)S(1)}, f32[3,2,64,512]{3,2,1,0:T(8,128)S(1)}, u32[]{:S(2)}, u32[]{:S(2)}) collective-permute-start(f32[3,2,64,512]{3,2,1,0:T(8,128)S(1)} %get-tuple-element.1305), channel_id=1, source_target_pairs={{0,1},{1,2},{2,3},{4,5},{5,6},{6,7},{8,9},{9,10},{10,11},{12,13},{... | collective-permute-start | bytes 2359304 | tf_op jit(solution)/shard_map/ppermute | solution.py:25
  153.5 1.3 collective-permute-start.9
  154.8 7.6 collective-permute-done.8
  162.4 3.9 collective-permute-done.9
  166.6 6.3 collective-permute-start.10
  172.9 1.9 collective-permute-start.11
  174.8 1.4 collective-permute-done.10
  176.2 4.4 collective-permute-done.11
  180.7 167.5 %all-reduce = (f32[64]{0:T(128)S(1)}, f32[64]{0:T(128)S(1)}) all-reduce(f32[64]{0:T(128)S(1)} %get-tuple-element.1181, f32[64]{0:T(128)S(1)} %get-tuple-element.1180), channel_id=1, replica_groups=mesh['sky'=128,'tm'=4] {'sky','tm'}, use_global_device_ids=true, to_apply=%region_1.0 | all-reduce | flops 128 | bytes 1024 | tf_op jit(solution)/shard_map/psum | solution.py:63
  348.4 101.3 %psum.30 = f32[64]{0:T(128)S(1)} all-reduce(f32[64]{0:T(128)S(1)} %multiply_reduce_fusion.1), channel_id=1, replica_groups=mesh['sky'=128,'tm'=4] {'sky','tm'}, use_global_device_ids=true, to_apply=%region_12.13 | all-reduce | flops 64 | bytes 512 | tf_op jit(solution)/shard_map/psum | solution.py:102
  449.9 3.3 collective-permute-start.12
  453.1 1.9 collective-permute-start.13
  455.1 1.4 collective-permute-done.12
  456.4 4.4 collective-permute-done.13
  460.8 0.9 pad_maximum_fusion.3
  461.8 1.4 collective-permute-start.14
  463.1 1.5 collective-permute-start.15
  464.6 4.4 convolution_add_fusion
  469.1 8.4 %collective-permute-done.14 = f32[3,1,2,64,512]{4,3,2,1,0:T(8,128)S(1)} collective-permute-done((f32[3,1,2,64,512]{4,3,2,1,0:T(8,128)}, f32[3,1,2,64,512]{4,3,2,1,0:T(8,128)S(1)}, u32[]{:S(2)}, u32[]{:S(2)}) %collective-permute-start.14) | collective-permute-done | bytes 786464 | tf_op jit(solution)/shard_map/ppermute | solution.py:14
  477.5 4.0 collective-permute-done.15
  481.5 1.7 pad_maximum_fusion.1
  483.5 36.7 %while.105 = (s32[]{:T(128)}, f32[2,64,512]{2,1,0:T(8,128)}, f32[3,3,2,64,512]{4,3,2,1,0:T(8,128)S(1)}, s32[2]{0:T(128)S(1)}, f32[2,3,512]{2,1,0:T(4,128)S(1)}, ...) while((s32[]{:T(128)}, f32[2,64,512]{2,1,0:T(8,128)}, ...), condition=%wide.region_18.19_spmd, body=%wide.region_13.18_spmd.sunk | while | flops 411172928 | bytes 1114013 | solution.py:90
  484.3 11.9 %while.107 = (s32[]{:T(128)}, f32[2,64,512]{2,1,0:T(8,128)}, f32[3,3,2,64,512]{4,3,2,1,0:T(8,128)S(1)}, s32[]{:T(128)}, s32[3]{0:T(128)S(1)}, /*index=5*/pred[3]...) while((s32[]{:T(128)}, f32[2,64,512]{2,1,0:T(8,128)}, ...), condition=%wide.region_17.17_spmd, body=%wide.region_14.16_spmd.sunk | while | flops 411172928 | bytes 839089 | solution.py:88
  488.6 2.2 fusion.86
  491.4 4.1 fusion.85
  496.9 23.2 %while.107 = (s32[]{:T(128)}, f32[2,64,512]{2,1,0:T(8,128)}, f32[3,3,2,64,512]{4,3,2,1,0:T(8,128)S(1)}, s32[]{:T(128)}, s32[3]{0:T(128)S(1)}, /*index=5*/pred[3]...) while((s32[]{:T(128)}, f32[2,64,512]{2,1,0:T(8,128)}, ...), condition=%wide.region_17.17_spmd, body=%wide.region_14.16_spmd.sunk | while | flops 411172928 | bytes 839089 | solution.py:88
  501.3 2.2 fusion.86
  504.1 4.1 fusion.85
  512.6 2.2 fusion.86
  515.4 4.1 fusion.85
  520.3 82.3 %collective-permute-start.16 = (f32[3,2,64,512]{3,2,1,0:T(8,128)S(1)}, f32[3,2,64,512]{3,2,1,0:T(8,128)S(1)}, u32[]{:S(2)}, u32[]{:S(2)}) collective-permute-start(f32[3,2,64,512]{3,2,1,0:T(8,128)S(1)} %get-tuple-element.1303), channel_id=1, source_target_pairs={{0,1},{1,2},{2,3},{4,5},{5,6},{6,7},{8,9},{9,10},{10,11},{12,13},{... | collective-permute-start | bytes 2359304 | tf_op jit(solution)/shard_map/ppermute | solution.py:25
  602.7 1.3 collective-permute-start.17
  604.0 7.6 collective-permute-done.16
  611.5 3.9 collective-permute-done.17
  615.7 7.5 collective-permute-start.18
  623.2 1.9 collective-permute-start.19
  625.1 1.4 collective-permute-done.18
  626.5 4.4 collective-permute-done.19
  630.9 1.1 multiply_reduce_fusion
  632.0 161.1 %psum.31 = f32[64]{0:T(128)S(1)} all-reduce(f32[64]{0:T(128)S(1)} %get-tuple-element.1288), channel_id=1, replica_groups=mesh['sky'=128,'tm'=4] {'sky','tm'}, use_global_device_ids=true, to_apply=%region_20.21 | all-reduce | flops 64 | bytes 512 | tf_op jit(solution)/shard_map/psum | solution.py:98
  793.2 0.9 multiply_subtract_fusion
  (88 shorter events, 18.2 us)
Async XLA Ops:
  0.6 15.2 %collective-permute-start = (f32[1,1,2,64,512]{4,3,2,1,0:T(8,128)}, f32[1,1,2,64,512]{4,3,2,1,0:T(8,128)S(1)}, u32[]{:S(2)}, u32[]{:S(2)}) collective-permute-start(f32[1,1,2,64,512]{4,3,2,1,0:T(8,128)} %bitcast.199), channel_id=1, source_target_pairs={{0,4},{4,8},{8,12},{12,16},{16,20},{20,24},{24,28},{28,32},{32,36}... | collective-permute-start | bytes 786440 | tf_op jit(solution)/shard_map/ppermute | solution.py:14
  5.1 10.6 %collective-permute-start.1 = (f32[1,1,2,64,512]{4,3,2,1,0:T(8,128)}, f32[1,1,2,64,512]{4,3,2,1,0:T(8,128)S(1)}, u32[]{:S(2)}, u32[]{:S(2)}) collective-permute-start(f32[1,1,2,64,512]{4,3,2,1,0:T(8,128)} %bitcast.200), channel_id=1, source_target_pairs={{4,0},{8,4},{12,8},{16,12},{20,16},{24,20},{28,24},{32,28},{36,32}... | collective-permute-start | bytes 786440 | tf_op jit(solution)/shard_map/ppermute | solution.py:17
  11.5 14.5 %collective-permute-start.4 = (f32[1,1,2,3,512]{4,3,2,1,0:T(4,128)S(1)}, f32[1,1,2,3,512]{4,3,2,1,0:T(4,128)S(1)}, u32[]{:S(2)}, u32[]{:S(2)}) collective-permute-start(f32[1,1,2,3,512]{4,3,2,1,0:T(4,128)S(1)} %bitcast.231), channel_id=1, source_target_pairs={{0,4},{4,8},{8,12},{12,16},{16,20},{20,24},{24,28},{28,32},{32,36}... | collective-permute-start | bytes 36872 | tf_op jit(solution)/shard_map/ppermute | solution.py:14
  13.4 12.6 %collective-permute-start.5 = (f32[1,1,2,3,512]{4,3,2,1,0:T(4,128)S(1)}, f32[1,1,2,3,512]{4,3,2,1,0:T(4,128)S(1)}, u32[]{:S(2)}, u32[]{:S(2)}) collective-permute-start(f32[1,1,2,3,512]{4,3,2,1,0:T(4,128)S(1)} %bitcast.232), channel_id=1, source_target_pairs={{4,0},{8,4},{12,8},{16,12},{20,16},{24,20},{28,24},{32,28},{36,32}... | collective-permute-start | bytes 36872 | tf_op jit(solution)/shard_map/ppermute | solution.py:17
  16.8 23.6 %collective-permute-start.2 = (f32[3,1,2,64,512]{4,3,2,1,0:T(8,128)S(1)}, f32[3,1,2,64,512]{4,3,2,1,0:T(8,128)S(1)}, u32[]{:S(2)}, u32[]{:S(2)}) collective-permute-start(f32[3,1,2,64,512]{4,3,2,1,0:T(8,128)S(1)} %pad_maximum_fusion.2), channel_id=1, source_target_pairs={{0,1},{1,2},{2,3},{4,5},{5,6},{6,7},{8,9},{9,10},{10,11},{12,13},{... | collective-permute-start | bytes 2359304 | tf_op jit(solution)/shard_map/ppermute | solution.py:14
  18.2 22.2 %collective-permute-start.3 = (f32[3,1,2,64,512]{4,3,2,1,0:T(8,128)S(1)}, f32[3,1,2,64,512]{4,3,2,1,0:T(8,128)S(1)}, u32[]{:S(2)}, u32[]{:S(2)}) collective-permute-start(f32[3,1,2,64,512]{4,3,2,1,0:T(8,128)S(1)} %pad_maximum_fusion.2), channel_id=1, source_target_pairs={{1,0},{2,1},{3,2},{5,4},{6,5},{7,6},{9,8},{10,9},{11,10},{13,12},{... | collective-permute-start | bytes 2359304 | tf_op jit(solution)/shard_map/ppermute | solution.py:17
  20.2 11.1 %copy-start.1 = (s32[2,14]{1,0:T(2,128)S(1)}, s32[2,14]{1,0:T(2,128)}, u32[]{:S(2)}) copy-start(s32[2,14]{1,0:T(2,128)} %param.23) | copy-start | bytes 340
  20.2 20.2 %copy-start = (f32[2,64,512]{2,1,0:T(8,128)S(1)}, f32[2,64,512]{2,1,0:T(8,128)}, u32[]{:S(2)}) copy-start(f32[2,64,512]{2,1,0:T(8,128)} %param.22) | copy-start | bytes 786436
  26.0 10.1 %collective-permute-start.6 = (f32[3,1,2,3,512]{4,3,2,1,0:T(4,128)S(1)}, f32[3,1,2,3,512]{4,3,2,1,0:T(4,128)S(1)}, u32[]{:S(2)}, u32[]{:S(2)}) collective-permute-start(f32[3,1,2,3,512]{4,3,2,1,0:T(4,128)S(1)} %pad_maximum_fusion.5), channel_id=1, source_target_pairs={{0,1},{1,2},{2,3},{4,5},{5,6},{6,7},{8,9},{9,10},{10,11},{12,13},{... | collective-permute-start | bytes 110600 | tf_op jit(solution)/shard_map/ppermute | solution.py:14
  29.9 10.4 %collective-permute-start.7 = (f32[3,1,2,3,512]{4,3,2,1,0:T(4,128)S(1)}, f32[3,1,2,3,512]{4,3,2,1,0:T(4,128)S(1)}, u32[]{:S(2)}, u32[]{:S(2)}) collective-permute-start(f32[3,1,2,3,512]{4,3,2,1,0:T(4,128)S(1)} %pad_maximum_fusion.5), channel_id=1, source_target_pairs={{1,0},{2,1},{3,2},{5,4},{6,5},{7,6},{9,8},{10,9},{11,10},{13,12},{... | collective-permute-start | bytes 110600 | tf_op jit(solution)/shard_map/ppermute | solution.py:17
  42.2 0.9 copy-start.2
  42.2 1.0 copy-start.3
  42.2 1.0 copy-start.5
  77.8 84.6 %collective-permute-start.8 = (f32[3,2,64,512]{3,2,1,0:T(8,128)S(1)}, f32[3,2,64,512]{3,2,1,0:T(8,128)S(1)}, u32[]{:S(2)}, u32[]{:S(2)}) collective-permute-start(f32[3,2,64,512]{3,2,1,0:T(8,128)S(1)} %get-tuple-element.1305), channel_id=1, source_target_pairs={{0,1},{1,2},{2,3},{4,5},{5,6},{6,7},{8,9},{9,10},{10,11},{12,13},{... | collective-permute-start | bytes 2359304 | tf_op jit(solution)/shard_map/ppermute | solution.py:25
  153.5 12.7 %collective-permute-start.9 = (f32[3,2,64,512]{3,2,1,0:T(8,128)S(1)}, f32[3,2,64,512]{3,2,1,0:T(8,128)S(1)}, u32[]{:S(2)}, u32[]{:S(2)}) collective-permute-start(f32[3,2,64,512]{3,2,1,0:T(8,128)S(1)} %get-tuple-element.1306), channel_id=1, source_target_pairs={{1,0},{2,1},{3,2},{5,4},{6,5},{7,6},{9,8},{10,9},{11,10},{13,12},{... | collective-permute-start | bytes 2359304 | tf_op jit(solution)/shard_map/ppermute | solution.py:25
  166.6 298.0 %copy-start.4 = (f32[2,512]{1,0:T(2,128)S(1)}, f32[2,512]{1,0:T(2,128)}, u32[]{:S(2)}) copy-start(f32[2,512]{1,0:T(2,128)} %param.21) | copy-start | bytes 12292
  166.6 9.6 %collective-permute-start.10 = (f32[2,64,512]{2,1,0:T(8,128)S(1)}, f32[2,64,512]{2,1,0:T(8,128)S(1)}, u32[]{:S(2)}, u32[]{:S(2)}) collective-permute-start(f32[2,64,512]{2,1,0:T(8,128)S(1)} %get-tuple-element.1309), channel_id=1, source_target_pairs={{0,4},{4,8},{8,12},{12,16},{16,20},{20,24},{24,28},{28,32},{32,36}... | collective-permute-start | bytes 786440 | tf_op jit(solution)/shard_map/ppermute | solution.py:25
  172.9 7.7 collective-permute-start.11
  449.9 6.6 collective-permute-start.12
  453.1 7.7 collective-permute-start.13
  461.8 15.7 %collective-permute-start.14 = (f32[3,1,2,64,512]{4,3,2,1,0:T(8,128)}, f32[3,1,2,64,512]{4,3,2,1,0:T(8,128)S(1)}, u32[]{:S(2)}, u32[]{:S(2)}) collective-permute-start(f32[3,1,2,64,512]{4,3,2,1,0:T(8,128)} %pad_maximum_fusion.3), channel_id=1, source_target_pairs={{0,1},{1,2},{2,3},{4,5},{5,6},{6,7},{8,9},{9,10},{10,11},{12,13},{... | collective-permute-start | bytes 2359304 | tf_op jit(solution)/shard_map/ppermute | solution.py:14
  463.1 18.4 %collective-permute-start.15 = (f32[3,1,2,64,512]{4,3,2,1,0:T(8,128)}, f32[3,1,2,64,512]{4,3,2,1,0:T(8,128)S(1)}, u32[]{:S(2)}, u32[]{:S(2)}) collective-permute-start(f32[3,1,2,64,512]{4,3,2,1,0:T(8,128)} %pad_maximum_fusion.3), channel_id=1, source_target_pairs={{1,0},{2,1},{3,2},{5,4},{6,5},{7,6},{9,8},{10,9},{11,10},{13,12},{... | collective-permute-start | bytes 2359304 | tf_op jit(solution)/shard_map/ppermute | solution.py:17
  520.3 91.2 %collective-permute-start.16 = (f32[3,2,64,512]{3,2,1,0:T(8,128)S(1)}, f32[3,2,64,512]{3,2,1,0:T(8,128)S(1)}, u32[]{:S(2)}, u32[]{:S(2)}) collective-permute-start(f32[3,2,64,512]{3,2,1,0:T(8,128)S(1)} %get-tuple-element.1303), channel_id=1, source_target_pairs={{0,1},{1,2},{2,3},{4,5},{5,6},{6,7},{8,9},{9,10},{10,11},{12,13},{... | collective-permute-start | bytes 2359304 | tf_op jit(solution)/shard_map/ppermute | solution.py:25
  602.7 12.7 %collective-permute-start.17 = (f32[3,2,64,512]{3,2,1,0:T(8,128)S(1)}, f32[3,2,64,512]{3,2,1,0:T(8,128)S(1)}, u32[]{:S(2)}, u32[]{:S(2)}) collective-permute-start(f32[3,2,64,512]{3,2,1,0:T(8,128)S(1)} %get-tuple-element.1304), channel_id=1, source_target_pairs={{1,0},{2,1},{3,2},{5,4},{6,5},{7,6},{9,8},{10,9},{11,10},{13,12},{... | collective-permute-start | bytes 2359304 | tf_op jit(solution)/shard_map/ppermute | solution.py:25
  615.7 10.8 %collective-permute-start.18 = (f32[2,64,512]{2,1,0:T(8,128)S(1)}, f32[2,64,512]{2,1,0:T(8,128)S(1)}, u32[]{:S(2)}, u32[]{:S(2)}) collective-permute-start(f32[2,64,512]{2,1,0:T(8,128)S(1)} %get-tuple-element.1307), channel_id=1, source_target_pairs={{0,4},{4,8},{8,12},{12,16},{16,20},{20,24},{24,28},{28,32},{32,36}... | collective-permute-start | bytes 786440 | tf_op jit(solution)/shard_map/ppermute | solution.py:25
  623.2 7.7 collective-permute-start.19
where the time goes:
time: 798 us; the launch traced here: 794 us
  blocking collectives  430 us (54%)
  starting transfers between devices  209 us (26%)
  waiting for transfers between devices  61.6 us (8%)
  matrix products  46 us (6%)
  loops' own time  20.5 us (3%)
  other arithmetic  16.7 us (2%)
  local copies, waits for them, and re-layouts  9.67 us (1%)
    psum x2, blocking collectives, local(): lax.psum(jnp.sum(residual * residual, axis=(0, 2)), ('sky', 'tm'))  269 us
    ppermute x8, starting transfers between devices, from_behind(): return lax.ppermute(shard, axis, pairs)  178 us
    psum x1, blocking collectives, local(): curve = lax.psum(jnp.sum(direction * image, axis=(0, 2)), ('sky', 'tm'))  161 us
    ppermute x8, waiting for transfers between devices, from_behind(): return lax.ppermute(shard, axis, pairs)  34.4 us
    dot_general x6, matrix products, pull(): lax.dot_general(vector, panel, (((1,), (1,)), ((), ())), precision=lax.Pr...  22.5 us
    another operation x4, loops' own time, per_block(): return lax.fori_loop(0, counts[block_at], per_slot, totals)  20.4 us
    ppermute x6, starting transfers between devices, with_halo(): lax.ppermute(lax.slice_in_dim(block, block.shape[dim] - width, None, axis...  16.4 us
  transfers between devices with their start and end apart: 20, of which 14 were waited for; matrix products, arithmetic and copies ran while one was open for 2% of the time, Pallas kernels for 0%

commit v1 on v0

v1 whole, which is shorter than its diff:
```python
import functools

import jax
import jax.numpy as jnp
from jax import lax
from jax.experimental import pallas as pl
from jax.experimental.pallas import tpu as pltpu
from jax.sharding import Mesh, PartitionSpec as P

F32 = jnp.float32
BF16 = jnp.bfloat16
BLOCKS, WIDTH, STARS, LANES = 2, 64, 512, 128
CHUNKS = STARS // LANES
POS, NOISE, LIST, IDENT, ROWS = 64, 67, 68, 69, 72
NEAR = 18
OWN = 8
TABLE_ROWS = 24
LONG, SHORT = 256, 64
PADDED = STARS + LONG
VMEM = pl.BlockSpec(memory_space=pltpu.VMEM)
SMEM = pl.BlockSpec(memory_space=pltpu.SMEM)
LIMIT = 48 * 1024 * 1024


def nt(left, right):
    return lax.dot_general(left, right, (((1,), (1,)), ((), ())), preferred_element_type=F32)


def nn(left, right):
    return lax.dot_general(left, right, (((1,), (0,)), ((), ())), preferred_element_type=F32)


def iota(shape, dim):
    return lax.broadcasted_iota(jnp.int32, shape, dim)


def column(row):
    return jnp.transpose(jnp.broadcast_to(row, (LANES, LANES)))


def lanes(chunk):
    return slice(chunk * LANES, (chunk + 1) * LANES)


def split_three(x):
    top = x.astype(BF16)
    rest = x - top.astype(F32)
    middle = rest.astype(BF16)
    return top, middle, (rest - middle.astype(F32)).astype(BF16)


def split_two(x):
    top = x.astype(BF16)
    return top, (x - top.astype(F32)).astype(BF16)


def one_hot(rank):
    same = iota((STARS, STARS), 0) == rank.astype(jnp.int32)
    return jnp.where(same, 1.0, 0.0).astype(BF16)


def unsort(x, rank):
    parts = nn(jnp.concatenate(split_three(x), axis=0), one_hot(rank))
    return (parts[:WIDTH] + parts[WIDTH : 2 * WIDTH]) + parts[2 * WIDTH :]


def sort_kernel(ident_ref, pos_ref, noise_ref, targets_ref, list_ref, packed_ref, rank_ref, stage):
    height = stage.shape[0]
    for b in range(BLOCKS):
        times = pos_ref[b, 2:3, :]
        counts = [jnp.zeros((1, LANES), F32) for _ in range(CHUNKS)]
        for jc in range(CHUNKS):
            other = column(times[:, lanes(jc)])
            for ic in range(CHUNKS):
                mine = times[:, lanes(ic)]
                if jc < ic:
                    before = other <= mine
                elif jc > ic:
                    before = other < mine
                else:
                    earlier = iota((LANES, LANES), 0) < iota((LANES, LANES), 1)
                    before = (other < mine) | ((other == mine) & earlier)
                counts[ic] += jnp.sum(jnp.where(before, 1.0, 0.0), axis=0, keepdims=True)
        rank = jnp.concatenate(counts, axis=1)
        rank_ref[b : b + 1, :] = rank
        stage[0:WIDTH, :] = targets_ref[b]
        stage[WIDTH:, :] = jnp.zeros((height - WIDTH, STARS), F32)
        stage[POS : POS + 3, :] = pos_ref[b]
        stage[NOISE : NOISE + 1, :] = noise_ref[b : b + 1, :]
        parts = nt(jnp.concatenate(split_three(stage[...]), axis=0), one_hot(rank))
        placed = (parts[:height] + parts[height : 2 * height]) + parts[2 * height :]
        packed_ref[b] = placed[:ROWS]
        listed = list_ref[b : b + 1, :].astype(F32) + 1.0
        packed_ref[b, LIST : LIST + 1, 0 : listed.shape[1]] = listed
        packed_ref[b, IDENT : IDENT + 1, :] = jnp.full((1, STARS), (ident_ref[0] + b + 1).astype(F32))


def build_table(near, table, times, lists, idents):
    for scratch in (times, lists, idents):
        scratch[...] = jnp.zeros(scratch.shape, F32)
    for k in range(NEAR):
        block = near(k)
        times[k : k + 1, :] = block[POS + 2 : POS + 3, :]
        lists[k : k + 1, :] = block[LIST : LIST + 1, 0:LANES]
        idents[k : k + 1, :] = block[IDENT : IDENT + 1, 0:LANES]
    place = iota((TABLE_ROWS, LANES), 1)
    out = jnp.zeros((TABLE_ROWS, LANES), jnp.int32)
    ident = idents[:, 0:1]
    for o in range(BLOCKS):
        own_ident = idents[OWN + o : OWN + o + 1, 0:1]
        own_list = lists[OWN + o : OWN + o + 1, :]
        own_list = jnp.where(own_list == 0.0, -5.0, own_list)
        hit = jnp.where((lists[...] == own_ident) | (own_list == ident), 1.0, 0.0)
        linked = (jnp.max(hit, axis=1, keepdims=True) > 0.0) | (ident == own_ident)
        mine = times[OWN + o : OWN + o + 1, :]
        total = jnp.zeros((TABLE_ROWS, 1), jnp.int32)
        for jc in range(CHUNKS):
            first = times[:, jc * LANES : jc * LANES + 1]
            last = times[:, (jc + 1) * LANES - 1 : (jc + 1) * LANES]
            skipped = jnp.sum(jnp.where(first - mine >= 1.0, 1.0, 0.0), axis=1, keepdims=True)
            beyond = jnp.sum(jnp.where(mine - last >= 1.0, 1.0, 0.0), axis=1, keepdims=True)
            start = skipped.astype(jnp.int32)
            end = STARS - beyond.astype(jnp.int32)
            aligned = start - (start & 7)
            count = jnp.where(linked & (end > start), end - aligned, 0)
            total = total + count
            col = 2 * (o * CHUNKS + jc)
            out = jnp.where(place == col, aligned, out)
            out = jnp.where(place == col + 1, count, out)
        out = jnp.where(place == 4 * CHUNKS + o, total, out)
    table[...] = out


def stage_weights(values, weights):
    def one(k, _):
        top, rest = split_two(values(k))
        for jc in range(CHUNKS):
            at = k * CHUNKS + jc
            weights[at, 0:WIDTH, 0:LANES] = top[:, lanes(jc)]
            weights[at, 0:WIDTH, LANES:] = top[:, lanes(jc)]
            weights[at, WIDTH:, 0:LANES] = rest[:, lanes(jc)]
            weights[at, WIDTH:, LANES:] = jnp.zeros((WIDTH, LANES), BF16)
        return 0

    return one


def tile_step(o, at, start, rows, own_pos, places, weights, total):
    start = pl.multiple_of(start, 8)
    squared = None
    for c in range(3):
        offset = own_pos[o, c, pl.ds(start, rows), :] - places[at, c : c + 1, :]
        squared = offset * offset if squared is None else squared + offset * offset
    radius = squared * lax.rsqrt(jnp.maximum(squared, 1e-30))
    margin = jnp.maximum(1.0 - radius, 0.0)
    margin_sq = margin * margin
    tile = (margin_sq * margin_sq) * (1.2 * radius + 0.3)
    both = jnp.concatenate(split_two(tile), axis=1)
    total[o, pl.ds(start, rows), :] += nt(both, weights[at])


def run_pairs(table, own_pos, places, weights, total):
    for o in range(BLOCKS):
        for c in range(3):
            for ic in range(CHUNKS):
                row = places[(OWN + o) * CHUNKS + ic, c : c + 1, :]
                own_pos[o, c, lanes(ic), :] = column(row)
            own_pos[o, c, STARS:, :] = jnp.zeros((PADDED - STARS, LANES), F32)
    total[...] = jnp.zeros(total.shape, F32)

    def per_block(k, _):
        for o in range(BLOCKS):

            @pl.when(table[k, 4 * CHUNKS + o] > 0)
            def _():
                for jc in range(CHUNKS):
                    col = 2 * (o * CHUNKS + jc)
                    start, count = table[k, col], table[k, col + 1]
                    at = k * CHUNKS + jc
                    whole = (count + (LONG - SHORT - 1)) // LONG

                    def step(i, _):
                        tile_step(o, at, start + LONG * i, LONG, own_pos, places, weights, total)
                        return 0

                    lax.fori_loop(0, whole, step, 0)

                    @pl.when(count > LONG * whole)
                    def _():
                        tile_step(o, at, start + LONG * whole, SHORT, own_pos, places, weights, total)

        return 0

    lax.fori_loop(0, NEAR, per_block, 0)


def image_of(o, total, places, vector):
    folded = jnp.transpose(total[o, 0:STARS, :])
    noise = jnp.concatenate(
        [places[(OWN + o) * CHUNKS + ic, NOISE - POS : NOISE - POS + 1, :] for ic in range(CHUNKS)], axis=1
    )
    return noise * vector + (folded[:WIDTH] + folded[WIDTH:])


def first_kernel(
    low, mid, high, image_ref, places, table, weights, own_pos, total, times, lists, idents, scalars, sem
):
    groups = (low, mid, high)

    def near(k):
        return groups[k // 6].at[k % 6]

    build_table(near, table, times, lists, idents)
    copy = pltpu.make_async_copy(table, scalars, sem)
    copy.start()
    for g, group in enumerate(groups):

        def one(i, _):
            k = 6 * g + i
            for jc in range(CHUNKS):
                places[k * CHUNKS + jc] = group[i, POS:ROWS, lanes(jc)]
            return stage_weights(lambda at: group[i, 0:WIDTH, :], weights)(k, 0)

        lax.fori_loop(0, 6, one, 0)
    copy.wait()
    run_pairs(scalars, own_pos, places, weights, total)
    for o in range(BLOCKS):
        image_ref[o] = image_of(o, total, places, mid[2 + o, 0:WIDTH, :])


def second_kernel(
    table, low, mid, high, places, packed, rank, image_ref, moments_ref, weights, own_pos, total, square
):
    groups = (low, mid, high)
    for g, group in enumerate(groups):
        one = stage_weights(lambda k: group[k - 6 * g], weights)
        lax.fori_loop(6 * g, 6 * g + 6, one, 0)
    run_pairs(table, own_pos, places, weights, total)
    sums = [jnp.zeros((WIDTH, LANES), F32) for _ in range(5)]
    for o in range(BLOCKS):
        start, once = packed[o, 0:WIDTH, :], mid[2 + o]
        twice = image_of(o, total, places, once)
        image_ref[o] = unsort(twice, rank[o : o + 1, :])
        products = (start * start, start * once, once * once, start * twice, once * twice)
        for n, product in enumerate(products):
            for ic in range(CHUNKS):
                sums[n] += product[:, lanes(ic)]
    square[...] = jnp.zeros(square.shape, F32)
    for n in range(5):
        square[0:WIDTH, n : n + 1] = jnp.sum(sums[n], axis=1, keepdims=True)
    turned = jnp.transpose(square[...])[0:8, :]
    top, middle, rest = (part.astype(F32) for part in split_three(turned))
    shifted = pltpu.roll(middle, WIDTH, axis=1)
    left = iota((8, LANES), 1) < WIDTH
    moments_ref[...] = jnp.where(left, top, shifted)
    rolled = pltpu.roll(rest, WIDTH, axis=1)
    low_half = iota((1, LANES), 1) < WIDTH
    for n in range(3):
        second = rolled[2 * n + 1 : 2 * n + 2, :]
        moments_ref[5 + n : 6 + n, :] = jnp.where(low_half, rest[2 * n : 2 * n + 1, :], second)


def unsort_kernel(x_ref, rank_ref, out_ref):
    for b in range(BLOCKS):
        out_ref[b] = unsort(x_ref[b], rank_ref[b : b + 1, :])


def two_sum(a, b):
    s = a + b
    back = s - a
    return s, (a - (s - back)) + (b - back)


def halves(a):
    scaled = 4097.0 * a
    top = scaled - (scaled - a)
    return top, a - top


def two_product(a, b):
    p = a * b
    a1, a2 = halves(a)
    b1, b2 = halves(b)
    return p, ((a1 * b1 - p) + a1 * b2 + a2 * b1) + a2 * b2


def pair_add(a, b):
    s, e = two_sum(a[0], b[0])
    return two_sum(s, e + (a[1] + b[1]))


def pair_mul(a, b):
    p, e = two_product(a[0], b[0])
    return two_sum(p, e + (a[0] * b[1] + a[1] * b[0]))


def final_kernel(moments_ref, start_ref, once_ref, twice_ref, solution_ref, residual_ref):
    gathered = moments_ref[...]
    rolled = pltpu.roll(gathered, WIDTH, axis=1)
    left = iota((1, LANES), 1) < WIDTH
    moments = []
    for n in range(5):
        source = gathered if n % 2 == 0 else rolled
        last = source[5 + n // 2 : 6 + n // 2, :]
        s, e = two_sum(gathered[n : n + 1, :], rolled[n : n + 1, :])
        s, e = two_sum(s, e + last)
        moments.append((jnp.where(left, s, 1.0), jnp.where(left, e, 0.0)))
    norm, curve, square, cross, cube = moments
    alpha = norm[0] / curve[0]
    step = (alpha, jnp.zeros_like(alpha))
    minus = (-alpha, jnp.zeros_like(alpha))
    step_sq = pair_mul(step, step)
    by_curve = pair_mul(minus, curve)
    norm_next = pair_add(pair_add(norm, pair_add(by_curve, by_curve)), pair_mul(step_sq, square))
    beta = norm_next[0] / norm[0]
    gamma = two_sum(jnp.ones_like(beta), beta)
    curve_next = pair_add(
        pair_mul(pair_mul(gamma, gamma), curve),
        pair_add(
            pair_mul(pair_mul(gamma, minus), pair_add(cross, square)),
            pair_mul(step_sq, cube),
        ),
    )
    alpha_next = norm_next[0] / curve_next[0]
    alpha, beta, alpha_next = (column(row)[0:WIDTH] for row in (alpha, beta, alpha_next))
    for o in range(BLOCKS):
        for ic in range(CHUNKS):
            at = (o, slice(None), lanes(ic))
            start, once, twice = start_ref[at], once_ref[at], twice_ref[at]
            residual = start - alpha * once
            direction = residual + beta * start
            image = (once - alpha * twice) + beta * once
            solution_ref[at] = alpha * start + alpha_next * direction
            residual_ref[at] = residual - alpha_next * image


def shape(*dims, dtype=F32):
    return jax.ShapeDtypeStruct(dims, dtype)


def call(kernel, out_shape, scratch=(), in_specs=None, count=None, flops=0, nbytes=1 << 20):
    outs = jax.tree.map(lambda _: VMEM, out_shape)
    return pl.pallas_call(
        kernel,
        out_shape=out_shape,
        in_specs=in_specs if in_specs is not None else [VMEM] * count,
        out_specs=outs,
        scratch_shapes=list(scratch),
        compiler_params=pltpu.CompilerParams(vmem_limit_bytes=LIMIT),
        cost_estimate=pl.CostEstimate(flops=flops, bytes_accessed=nbytes, transcendentals=0),
    )


def shift(x, axis, by):
    count = lax.axis_size(axis)
    return lax.ppermute(x, axis, [(i, i + by) for i in range(count) if 0 <= i + by < count])


SKY = ("z", "x", "core")


def sky_shift(x, by):
    count = lax.axis_size(SKY)
    return lax.ppermute(x, SKY, [(i, i + by) for i in range(count) if 0 <= i + by < count])


def with_halo(x):
    before, after = shift(x, "tm", 1), shift(x, "tm", -1)
    mid = jnp.concatenate([before, x, after], axis=0)
    return sky_shift(mid, 1), mid, sky_shift(mid, -1)


def local(star_pos, noise_var, targets, pair_list):
    ident = (lax.axis_index(SKY) * lax.axis_size("tm") + lax.axis_index("tm")) * BLOCKS
    block = shape(BLOCKS, WIDTH, STARS)
    pairs_scratch = [
        pltpu.VMEM((NEAR * CHUNKS, LANES, 2 * LANES), BF16),
        pltpu.VMEM((BLOCKS, 3, PADDED, LANES), F32),
        pltpu.VMEM((BLOCKS, PADDED, LANES), F32),
    ]
    packed, rank = call(
        sort_kernel,
        (shape(BLOCKS, ROWS, STARS), shape(BLOCKS, STARS)),
        scratch=[pltpu.VMEM((80, STARS), F32)],
        in_specs=[SMEM, VMEM, VMEM, VMEM, VMEM],
    )(ident.reshape(1), star_pos, noise_var, targets, pair_list)
    low, mid, high = with_halo(packed)
    once, places, table = call(
        first_kernel,
        (block, shape(NEAR * CHUNKS, 8, LANES), shape(TABLE_ROWS, LANES, dtype=jnp.int32)),
        scratch=pairs_scratch
        + [
            pltpu.VMEM((TABLE_ROWS, STARS), F32),
            pltpu.VMEM((TABLE_ROWS, LANES), F32),
            pltpu.VMEM((TABLE_ROWS, LANES), F32),
            pltpu.SMEM((TABLE_ROWS, LANES), jnp.int32),
            pltpu.SemaphoreType.DMA,
        ],
        count=3,
    )(low, mid, high)
    low, mid, high = with_halo(once)
    once_back = call(unsort_kernel, block, count=2)(once, rank)
    twice_back, moments = call(
        second_kernel,
        (block, shape(8, LANES)),
        scratch=pairs_scratch + [pltpu.VMEM((LANES, LANES), F32)],
        in_specs=[SMEM] + [VMEM] * 6,
    )(table, low, mid, high, places, packed, rank)
    moments = lax.psum(moments, ("x", "core"))
    moments = lax.psum(moments, "tm")
    moments = lax.psum(moments, "z")
    return call(final_kernel, (block, block), count=4)(moments, targets, once_back, twice_back)


def solution(mesh):
    sky, tm = mesh.devices.shape
    finer = Mesh(mesh.devices.reshape(sky // 8, 4, 2, tm), SKY + ("tm",))
    both = SKY + ("tm",)
    in_specs = (P(both, None, None), P(both, None), P(both, None, None), P(both, None))
    out_specs = (P(both, None, None), P(both, None, None))
    return jax.shard_map(local, mesh=finer, in_specs=in_specs, out_specs=out_specs, check_vma=False)
```

time: 798 us -> 158 us (0.20)
  the two profiles are of different devices: /device:TPU:1 before, /device:TPU:32 now
where the time goes in v1:
time: 158 us; the launch traced here: 157 us
  blocking collectives  61.6 us (39%)
  waiting for transfers between devices  43.1 us (27%)
  Pallas kernels  28.8 us (18%)
  starting transfers between devices  20.5 us (13%)
  local copies, waits for them, and re-layouts  2.45 us (2%)
    psum x1, blocking collectives, local(): moments = lax.psum(moments, 'z')  34 us
    ppermute x4, waiting for transfers between devices, sky_shift(): lax.ppermute(x, SKY, [(i, i + by) for i in range(count) if 0 <= i + by <...  27.1 us
    ppermute x4, waiting for transfers between devices, shift(): lax.ppermute(x, axis, [(i, i + by) for i in range(count) if 0 <= i + by <...  15.9 us
    psum x1, blocking collectives, local(): moments = lax.psum(moments, 'tm')  15.2 us
    pallas_call x1, Pallas kernels, local(): call(second_kernel, (block, shape(8, LANES)), scratch=pairs_scratch + [pl...  13.3 us
    pallas_call x1, Pallas kernels, local(): call(first_kernel, (block, shape(NEAR * CHUNKS, 8, LANES), shape(TABLE_RO...  13.2 us
    psum x1, blocking collectives, local(): moments = lax.psum(moments, ('x', 'core'))  12.4 us
    ppermute x4, starting transfers between devices, shift(): lax.ppermute(x, axis, [(i, i + by) for i in range(count) if 0 <= i + by <...  11.8 us
  transfers between devices with their start and end apart: 8, of which 8 were waited for; matrix products, arithmetic and copies ran while one was open for 0% of the time, Pallas kernels for 0%

profile of v1, /device:TPU:32, one launch (start us, length us, event | category | flops | bytes accessed | tf_op | source)
XLA Modules:
  0.0 157.2 jit_solution(11430814010318371644)
XLA Ops:
  0.6 0.0 copy-start.4
  0.6 0.7 copy-done.4
  1.3 0.0 copy-start.2
  1.4 0.0 copy-start.3
  1.4 0.7 copy-done.2
  2.0 0.0 copy-done.3
  2.0 0.0 copy-start
  2.0 0.9 copy-done
  3.0 0.8 shard_map.59
  3.8 3.5 %collective-permute-start = (f32[2,72,512]{2,1,0:T(8,128)S(1)}, f32[2,72,512]{2,1,0:T(8,128)S(1)}, u32[]{:S(2)}, u32[]{:S(2)}) collective-permute-start(f32[2,72,512]{2,1,0:T(8,128)S(1)} %get-tuple-element.9.packed), channel_id=1, source_target_pairs={{0,1},{1,2},{2,3},{4,5},{5,6},{6,7},{8,9},{9,10},{10,11},{12,13},{... | collective-permute-start | bytes 884744 | tf_op jit(solution)/shard_map/ppermute | solution.py:356
  7.3 1.3 collective-permute-start.1
  8.6 4.9 %collective-permute-done = f32[2,72,512]{2,1,0:T(8,128)S(1)} collective-permute-done((f32[2,72,512]{2,1,0:T(8,128)S(1)}, f32[2,72,512]{2,1,0:T(8,128)S(1)}, u32[]{:S(2)}, u32[]{:S(2)}) %collective-permute-start) | collective-permute-done | bytes 294944 | tf_op jit(solution)/shard_map/ppermute | solution.py:356
  13.5 4.1 %collective-permute-done.1 = f32[2,72,512]{2,1,0:T(8,128)S(1)} collective-permute-done((f32[2,72,512]{2,1,0:T(8,128)S(1)}, f32[2,72,512]{2,1,0:T(8,128)S(1)}, u32[]{:S(2)}, u32[]{:S(2)}) %collective-permute-start.1) | collective-permute-done | bytes 294944 | tf_op jit(solution)/shard_map/ppermute | solution.py:356
  17.6 2.5 %collective-permute-start.3 = (f32[6,72,512]{2,1,0:T(8,128)S(1)}, f32[6,72,512]{2,1,0:T(8,128)S(1)}, u32[]{:S(2)}, u32[]{:S(2)}) collective-permute-start(f32[6,72,512]{2,1,0:T(8,128)S(1)} %constant_dynamic-update-slice_fusion.mid), channel_id=1, source_target_pairs={{4,0},{8,4},{12,8},{16,12},{20,16},{24,20},{28,24},{32,28},{36,32}... | collective-permute-start | bytes 2654216 | tf_op jit(solution)/shard_map/ppermute | solution.py:364
  20.1 1.9 %collective-permute-start.2 = (f32[6,72,512]{2,1,0:T(8,128)S(1)}, f32[6,72,512]{2,1,0:T(8,128)S(1)}, u32[]{:S(2)}, u32[]{:S(2)}) collective-permute-start(f32[6,72,512]{2,1,0:T(8,128)S(1)} %constant_dynamic-update-slice_fusion.mid), channel_id=1, source_target_pairs={{0,4},{4,8},{8,12},{12,16},{16,20},{20,24},{24,28},{28,32},{32,36}... | collective-permute-start | bytes 2654216 | tf_op jit(solution)/shard_map/ppermute | solution.py:364
  22.0 8.6 %collective-permute-done.3.high = f32[6,72,512]{2,1,0:T(8,128)S(1)} collective-permute-done((f32[6,72,512]{2,1,0:T(8,128)S(1)}, f32[6,72,512]{2,1,0:T(8,128)S(1)}, u32[]{:S(2)}, u32[]{:S(2)}) %collective-permute-start.3) | collective-permute-done | bytes 884768 | tf_op jit(solution)/shard_map/ppermute | solution.py:364
  30.7 5.9 %collective-permute-done.2.low = f32[6,72,512]{2,1,0:T(8,128)S(1)} collective-permute-done((f32[6,72,512]{2,1,0:T(8,128)S(1)}, f32[6,72,512]{2,1,0:T(8,128)S(1)}, u32[]{:S(2)}, u32[]{:S(2)}) %collective-permute-start.2) | collective-permute-done | bytes 884768 | tf_op jit(solution)/shard_map/ppermute | solution.py:364
  36.6 13.2 %shard_map.60 = (f32[2,64,512]{2,1,0:T(8,128)S(1)}, f32[72,8,128]{2,1,0:T(8,128)S(1)}, s32[24,128]{1,0:T(8,128)S(1)}) custom-call(f32[6,72,512]{2,1,0:T(8,128)S(1)} %collective-permute-done.2.low, f32[6,72,512]{2,1,0:T(8,128)S(1)} %constant_dynamic-update-slice_fusion.mid, f32[6,72,512]{2,1,0:T(8,128)S(1)} %collective-permute-done.3.high), custom_call_target="tpu_custom_call" | custom-call | bytes 1048576 | tf_op jit(solution)/shard_map/pallas_call | solution.py:388
  49.8 5.7 %collective-permute-start.4 = (f32[2,64,512]{2,1,0:T(8,128)S(1)}, f32[2,64,512]{2,1,0:T(8,128)S(1)}, u32[]{:S(2)}, u32[]{:S(2)}) collective-permute-start(f32[2,64,512]{2,1,0:T(8,128)S(1)} %get-tuple-element.11.x_ref), channel_id=1, source_target_pairs={{0,1},{1,2},{2,3},{4,5},{5,6},{6,7},{8,9},{9,10},{10,11},{12,13},{... | collective-permute-start | bytes 786440 | tf_op jit(solution)/shard_map/ppermute | solution.py:356
  55.5 1.3 collective-permute-start.5
  56.8 2.6 %collective-permute-done.4 = f32[2,64,512]{2,1,0:T(8,128)S(1)} collective-permute-done((f32[2,64,512]{2,1,0:T(8,128)S(1)}, f32[2,64,512]{2,1,0:T(8,128)S(1)}, u32[]{:S(2)}, u32[]{:S(2)}) %collective-permute-start.4) | collective-permute-done | bytes 262176 | tf_op jit(solution)/shard_map/ppermute | solution.py:356
  59.4 4.4 %collective-permute-done.5 = f32[2,64,512]{2,1,0:T(8,128)S(1)} collective-permute-done((f32[2,64,512]{2,1,0:T(8,128)S(1)}, f32[2,64,512]{2,1,0:T(8,128)S(1)}, u32[]{:S(2)}, u32[]{:S(2)}) %collective-permute-start.5) | collective-permute-done | bytes 262176 | tf_op jit(solution)/shard_map/ppermute | solution.py:356
  63.8 1.9 %collective-permute-start.7 = (f32[6,64,512]{2,1,0:T(8,128)S(1)}, f32[6,64,512]{2,1,0:T(8,128)S(1)}, u32[]{:S(2)}, u32[]{:S(2)}) collective-permute-start(f32[6,64,512]{2,1,0:T(8,128)S(1)} %constant_dynamic-update-slice_fusion.3.mid), channel_id=1, source_target_pairs={{4,0},{8,4},{12,8},{16,12},{20,16},{24,20},{28,24},{32,28},{36,32}... | collective-permute-start | bytes 2359304 | tf_op jit(solution)/shard_map/ppermute | solution.py:364
  65.7 2.4 %collective-permute-start.6 = (f32[6,64,512]{2,1,0:T(8,128)S(1)}, f32[6,64,512]{2,1,0:T(8,128)S(1)}, u32[]{:S(2)}, u32[]{:S(2)}) collective-permute-start(f32[6,64,512]{2,1,0:T(8,128)S(1)} %constant_dynamic-update-slice_fusion.3.mid), channel_id=1, source_target_pairs={{0,4},{4,8},{8,12},{12,16},{16,20},{20,24},{24,28},{28,32},{32,36}... | collective-permute-start | bytes 2359304 | tf_op jit(solution)/shard_map/ppermute | solution.py:364
  68.2 0.4 shard_map.62.once_ref
  68.6 6.7 %collective-permute-done.7.high = f32[6,64,512]{2,1,0:T(8,128)S(1)} collective-permute-done((f32[6,64,512]{2,1,0:T(8,128)S(1)}, f32[6,64,512]{2,1,0:T(8,128)S(1)}, u32[]{:S(2)}, u32[]{:S(2)}) %collective-permute-start.7) | collective-permute-done | bytes 786464 | tf_op jit(solution)/shard_map/ppermute | solution.py:364
  75.2 5.9 %collective-permute-done.6.low = f32[6,64,512]{2,1,0:T(8,128)S(1)} collective-permute-done((f32[6,64,512]{2,1,0:T(8,128)S(1)}, f32[6,64,512]{2,1,0:T(8,128)S(1)}, u32[]{:S(2)}, u32[]{:S(2)}) %collective-permute-start.6) | collective-permute-done | bytes 786464 | tf_op jit(solution)/shard_map/ppermute | solution.py:364
  81.2 0.0 copy-start.1
  81.2 13.3 %shard_map.61 = (f32[2,64,512]{2,1,0:T(8,128)S(1)}, f32[8,128]{1,0:T(8,128)S(1)}) custom-call(s32[24,128]{1,0:T(8,128)S(1)} %get-tuple-element.10.table, f32[6,64,512]{2,1,0:T(8,128)S(1)} %collective-permute-done.6.low, f32[6,64,512]{2,1,0:T(8,128)S(1)} %constant_dynamic-update-slice_fusion.3.mid, f32[6,64,512]{2,1,0:T(8,128)S(1)} %collective-permute-done.7.high, ...), custom_call_target="tpu_custom_call" | custom-call | bytes 1048576 | tf_op jit(solution)/shard_map/pallas_call | solution.py:403
  94.4 12.4 %psum.21 = f32[8,128]{1,0:T(8,128)S(1)} all-reduce(f32[8,128]{1,0:T(8,128)S(1)} %get-tuple-element.14), channel_id=1, replica_groups=mesh['z'=16,'x'=4,'core'=2,'tm'=4] {'x','core'}, use_global_device_ids=true, to_apply=%region_0.0 | all-reduce | flops 1024 | bytes 8192 | tf_op jit(solution)/shard_map/psum | solution.py:409
  106.8 15.2 %psum.22 = f32[8,128]{1,0:T(8,128)S(1)} all-reduce(f32[8,128]{1,0:T(8,128)S(1)} %psum.21), channel_id=1, replica_groups=mesh['z'=16,'x'=4,'core'=2,'tm'=4] {'tm'}, use_global_device_ids=true, to_apply=%region_1.0 | all-reduce | flops 1024 | bytes 8192 | tf_op jit(solution)/shard_map/psum | solution.py:410
  122.1 34.0 %psum.23.moments_ref = f32[8,128]{1,0:T(8,128)S(1)} all-reduce(f32[8,128]{1,0:T(8,128)S(1)} %psum.22), channel_id=1, replica_groups=mesh['z'=16,'x'=4,'core'=2,'tm'=4] {'z'}, use_global_device_ids=true, to_apply=%region_2.0 | all-reduce | flops 1024 | bytes 8192 | tf_op jit(solution)/shard_map/psum | solution.py:411
  156.1 0.0 copy-done.1
  156.1 1.1 shard_map.63
  (7 shorter events, 0.1 us)
Async XLA Ops:
  0.6 0.7 copy-start.4
  1.3 0.7 copy-start.2
  1.4 0.7 copy-start.3
  2.0 0.9 copy-start
  3.8 9.7 %collective-permute-start = (f32[2,72,512]{2,1,0:T(8,128)S(1)}, f32[2,72,512]{2,1,0:T(8,128)S(1)}, u32[]{:S(2)}, u32[]{:S(2)}) collective-permute-start(f32[2,72,512]{2,1,0:T(8,128)S(1)} %get-tuple-element.9.packed), channel_id=1, source_target_pairs={{0,1},{1,2},{2,3},{4,5},{5,6},{6,7},{8,9},{9,10},{10,11},{12,13},{... | collective-permute-start | bytes 884744 | tf_op jit(solution)/shard_map/ppermute | solution.py:356
  7.3 10.4 %collective-permute-start.1 = (f32[2,72,512]{2,1,0:T(8,128)S(1)}, f32[2,72,512]{2,1,0:T(8,128)S(1)}, u32[]{:S(2)}, u32[]{:S(2)}) collective-permute-start(f32[2,72,512]{2,1,0:T(8,128)S(1)} %get-tuple-element.9.packed), channel_id=1, source_target_pairs={{1,0},{2,1},{3,2},{5,4},{6,5},{7,6},{9,8},{10,9},{11,10},{13,12},{... | collective-permute-start | bytes 884744 | tf_op jit(solution)/shard_map/ppermute | solution.py:356
  17.6 13.0 %collective-permute-start.3 = (f32[6,72,512]{2,1,0:T(8,128)S(1)}, f32[6,72,512]{2,1,0:T(8,128)S(1)}, u32[]{:S(2)}, u32[]{:S(2)}) collective-permute-start(f32[6,72,512]{2,1,0:T(8,128)S(1)} %constant_dynamic-update-slice_fusion.mid), channel_id=1, source_target_pairs={{4,0},{8,4},{12,8},{16,12},{20,16},{24,20},{28,24},{32,28},{36,32}... | collective-permute-start | bytes 2654216 | tf_op jit(solution)/shard_map/ppermute | solution.py:364
  20.1 16.5 %collective-permute-start.2 = (f32[6,72,512]{2,1,0:T(8,128)S(1)}, f32[6,72,512]{2,1,0:T(8,128)S(1)}, u32[]{:S(2)}, u32[]{:S(2)}) collective-permute-start(f32[6,72,512]{2,1,0:T(8,128)S(1)} %constant_dynamic-update-slice_fusion.mid), channel_id=1, source_target_pairs={{0,4},{4,8},{8,12},{12,16},{16,20},{20,24},{24,28},{28,32},{32,36}... | collective-permute-start | bytes 2654216 | tf_op jit(solution)/shard_map/ppermute | solution.py:364
  49.8 9.6 %collective-permute-start.4 = (f32[2,64,512]{2,1,0:T(8,128)S(1)}, f32[2,64,512]{2,1,0:T(8,128)S(1)}, u32[]{:S(2)}, u32[]{:S(2)}) collective-permute-start(f32[2,64,512]{2,1,0:T(8,128)S(1)} %get-tuple-element.11.x_ref), channel_id=1, source_target_pairs={{0,1},{1,2},{2,3},{4,5},{5,6},{6,7},{8,9},{9,10},{10,11},{12,13},{... | collective-permute-start | bytes 786440 | tf_op jit(solution)/shard_map/ppermute | solution.py:356
  55.5 8.3 %collective-permute-start.5 = (f32[2,64,512]{2,1,0:T(8,128)S(1)}, f32[2,64,512]{2,1,0:T(8,128)S(1)}, u32[]{:S(2)}, u32[]{:S(2)}) collective-permute-start(f32[2,64,512]{2,1,0:T(8,128)S(1)} %get-tuple-element.11.x_ref), channel_id=1, source_target_pairs={{1,0},{2,1},{3,2},{5,4},{6,5},{7,6},{9,8},{10,9},{11,10},{13,12},{... | collective-permute-start | bytes 786440 | tf_op jit(solution)/shard_map/ppermute | solution.py:356
  63.8 11.4 %collective-permute-start.7 = (f32[6,64,512]{2,1,0:T(8,128)S(1)}, f32[6,64,512]{2,1,0:T(8,128)S(1)}, u32[]{:S(2)}, u32[]{:S(2)}) collective-permute-start(f32[6,64,512]{2,1,0:T(8,128)S(1)} %constant_dynamic-update-slice_fusion.3.mid), channel_id=1, source_target_pairs={{4,0},{8,4},{12,8},{16,12},{20,16},{24,20},{28,24},{32,28},{36,32}... | collective-permute-start | bytes 2359304 | tf_op jit(solution)/shard_map/ppermute | solution.py:364
  65.7 15.4 %collective-permute-start.6 = (f32[6,64,512]{2,1,0:T(8,128)S(1)}, f32[6,64,512]{2,1,0:T(8,128)S(1)}, u32[]{:S(2)}, u32[]{:S(2)}) collective-permute-start(f32[6,64,512]{2,1,0:T(8,128)S(1)} %constant_dynamic-update-slice_fusion.3.mid), channel_id=1, source_target_pairs={{0,4},{4,8},{8,12},{12,16},{16,20},{20,24},{24,28},{28,32},{32,36}... | collective-permute-start | bytes 2359304 | tf_op jit(solution)/shard_map/ppermute | solution.py:364
  81.2 74.9 %copy-start.1 = (f32[2,64,512]{2,1,0:T(8,128)S(1)}, f32[2,64,512]{2,1,0:T(8,128)}, u32[]{:S(2)}) copy-start(f32[2,64,512]{2,1,0:T(8,128)} %start_ref.1) | copy-start | bytes 786436

commit v2 on v1

v2 whole, which is shorter than its diff:
```python
import functools

import jax
import jax.numpy as jnp
from jax import lax
from jax.experimental import pallas as pl
from jax.experimental.pallas import tpu as pltpu
from jax.sharding import Mesh, PartitionSpec as P

F32 = jnp.float32
BF16 = jnp.bfloat16
BLOCKS, WIDTH, STARS, LANES = 2, 64, 512, 128
CHUNKS = STARS // LANES
NOISE, LIST, IDENT, META = 3, 4, 5, 8
COLUMNS = 16
ROWS = STARS + CHUNKS * BLOCKS * META
NEAR = 18
OWN = 8
LONG, SHORT = 256, 64
AT_ONCE = {LONG: 4, SHORT: 8}
KEPT = {LONG: 40, SHORT: 48}
PADDED = STARS + LONG
NOTHING = STARS
FIRST = {LONG: 8, SHORT: 320}
COUNT = {LONG: 0, SHORT: 1}
LISTS = 512
VMEM = pl.BlockSpec(memory_space=pltpu.VMEM)
SMEM = pl.BlockSpec(memory_space=pltpu.SMEM)
LIMIT = 32 * 1024 * 1024


def nt(left, right):
    return lax.dot_general(left, right, (((1,), (1,)), ((), ())), preferred_element_type=F32)


def nn(left, right):
    return lax.dot_general(left, right, (((1,), (0,)), ((), ())), preferred_element_type=F32)


def iota(shape, dim):
    return lax.broadcasted_iota(jnp.int32, shape, dim)


def column(row):
    return jnp.transpose(jnp.broadcast_to(row, (LANES, LANES)))


def lanes(chunk):
    return slice(chunk * LANES, (chunk + 1) * LANES)


def split_three(x):
    top = x.astype(BF16)
    rest = x - top.astype(F32)
    middle = rest.astype(BF16)
    return top, middle, (rest - middle.astype(F32)).astype(BF16)


def split_two(x):
    top = x.astype(BF16)
    return top, (x - top.astype(F32)).astype(BF16)


def one_hot(rank):
    same = iota((STARS, STARS), 0) == rank.astype(jnp.int32)
    return jnp.where(same, 1.0, 0.0).astype(BF16)


def fold(x):
    return x + pltpu.roll(x, WIDTH, axis=x.ndim - 1)


def left_half(rows):
    return iota((rows, LANES), 1) < WIDTH


def unsort(x, rank_ref, out_ref):
    turned = jnp.concatenate([jnp.transpose(x[lanes(jc), :]) for jc in range(CHUNKS)], axis=1)
    for b in range(BLOCKS):
        block = turned[b * WIDTH : (b + 1) * WIDTH]
        parts = nn(jnp.concatenate(split_three(block), axis=0), one_hot(rank_ref[b : b + 1, :]))
        out_ref[b] = (parts[:WIDTH] + parts[WIDTH : 2 * WIDTH]) + parts[2 * WIDTH :]


def ranks(times):
    counts = [jnp.zeros((1, LANES), F32) for _ in range(CHUNKS)]
    for jc in range(CHUNKS):
        other = column(times[:, lanes(jc)])
        for ic in range(CHUNKS):
            mine = times[:, lanes(ic)]
            if jc < ic:
                before = other <= mine
            elif jc > ic:
                before = other < mine
            else:
                earlier = iota((LANES, LANES), 0) < iota((LANES, LANES), 1)
                before = (other < mine) | ((other == mine) & earlier)
            counts[ic] += jnp.sum(jnp.where(before, 1.0, 0.0), axis=0, keepdims=True)
    return jnp.concatenate(counts, axis=1)


def meta_rows(b, jc):
    first = STARS + (jc * BLOCKS + b) * META
    return slice(first, first + META)


def sort_kernel(ident_ref, pos_ref, noise_ref, targets_ref, list_ref, packed_ref, rank_ref, tall, small):
    values = jnp.zeros((STARS, LANES), F32)
    for b in range(BLOCKS):
        rank = ranks(pos_ref[b, 2:3, :])
        rank_ref[b : b + 1, :] = rank
        where_to = one_hot(rank)
        tall[...] = jnp.zeros(tall.shape, F32)
        tall[b * WIDTH : (b + 1) * WIDTH, :] = targets_ref[b]
        parts = nt(where_to, jnp.concatenate(split_three(tall[...]), axis=0))
        values += (parts[:, lanes(0)] + parts[:, lanes(1)]) + parts[:, lanes(2)]
        small[...] = jnp.zeros(small.shape, F32)
        small[0:3, :] = pos_ref[b]
        small[NOISE : NOISE + 1, :] = noise_ref[b : b + 1, :]
        parts = nt(jnp.concatenate(split_three(small[...]), axis=0), where_to)
        height = small.shape[0]
        meta = ((parts[:height] + parts[height : 2 * height]) + parts[2 * height :])[0:META]
        for jc in range(CHUNKS):
            packed_ref[meta_rows(b, jc), :] = meta[:, lanes(jc)]
            first = STARS + (jc * BLOCKS + b) * META
            ident = jnp.full((1, LANES), (ident_ref[0] + b + 1).astype(F32))
            packed_ref[first + IDENT : first + IDENT + 1, :] = ident
        listed = list_ref[b : b + 1, :].astype(F32) + 1.0
        first = STARS + b * META + LIST
        packed_ref[first : first + 1, 0 : listed.shape[1]] = listed
    packed_ref[0:STARS, :] = values


def build_table(devices, own, chosen, table, times, lists, idents):
    rows = table.shape[0]
    for scratch in (times, lists, idents):
        scratch[...] = jnp.zeros(scratch.shape, F32)
    for d, device in enumerate(devices):
        for b in range(BLOCKS):
            k = BLOCKS * d + b
            for jc in range(CHUNKS):
                first = STARS + (jc * BLOCKS + b) * META
                times[k : k + 1, lanes(jc)] = device[first + 2 : first + 3, :]
            first = STARS + b * META
            lists[k : k + 1, :] = device[first + LIST : first + LIST + 1, :]
            idents[k : k + 1, :] = device[first + IDENT : first + IDENT + 1, :]
    place = iota((rows, LANES), 1)
    block = iota((rows, 1), 0)
    out = jnp.full((rows, LANES), -1, jnp.int32)
    ident = idents[:, 0:1]
    for o in range(BLOCKS):
        own_ident = idents[own + o : own + o + 1, 0:1]
        own_list = lists[own + o : own + o + 1, :]
        own_list = jnp.where(own_list == 0.0, -5.0, own_list)
        hit = jnp.where((lists[...] == own_ident) | (own_list == ident), 1.0, 0.0)
        linked = (jnp.max(hit, axis=1, keepdims=True) > 0.0) | (ident == own_ident)
        linked = linked & chosen(block)
        mine = times[own + o : own + o + 1, :]
        twice = jnp.zeros((rows, 1), jnp.int32)
        for jc in range(CHUNKS):
            first = times[:, jc * LANES : jc * LANES + 1]
            last = times[:, (jc + 1) * LANES - 1 : (jc + 1) * LANES]
            skipped = jnp.sum(jnp.where(first - mine >= 1.0, 1.0, 0.0), axis=1, keepdims=True)
            beyond = jnp.sum(jnp.where(mine - last >= 1.0, 1.0, 0.0), axis=1, keepdims=True)
            start = skipped.astype(jnp.int32)
            end = STARS - beyond.astype(jnp.int32)
            start = start - (start & 7)
            count = jnp.where(linked & (end > start), end - start, 0)
            whole = (count + (LONG - SHORT - 1)) // LONG
            twice = jnp.where(whole > 1, 1, twice)
            code = (block * CHUNKS + jc) * 2048 + (o * PADDED + start)
            steps = (
                jnp.where(whole > 0, code, -1),
                jnp.where(count > whole * LONG, code + whole * LONG, -1),
                jnp.where(whole > 1, code + LONG, -1),
            )
            for n, step in enumerate(steps):
                out = jnp.where(place == COLUMNS * o + n * CHUNKS + jc, step, out)
        flag = linked.astype(jnp.int32) + twice
        out = jnp.where(place == COLUMNS * o + 3 * CHUNKS, flag, out)
    table[...] = out


def list_steps(table, tasks, blocks):
    def per_block(k, counts):
        for o in range(BLOCKS):
            flag = table[k, COLUMNS * o + 3 * CHUNKS]

            def add(counts, o=o):
                counts = list(counts)
                for jc in range(CHUNKS):
                    for n, rows in enumerate((LONG, SHORT)):
                        code = table[k, COLUMNS * o + n * CHUNKS + jc]
                        tasks[FIRST[rows] + counts[n]] = code
                        counts[n] += (code >= 0).astype(jnp.int32)
                return tuple(counts)

            def more(counts, o=o):
                long, short = counts
                for jc in range(CHUNKS):
                    code = table[k, COLUMNS * o + 2 * CHUNKS + jc]
                    tasks[FIRST[LONG] + long] = code
                    long += (code >= 0).astype(jnp.int32)
                return long, short

            counts = lax.cond(flag > 0, add, lambda counts: counts, counts)
            counts = lax.cond(flag > 1, more, lambda counts: counts, counts)
        return counts

    counts = lax.fori_loop(0, blocks, per_block, (jnp.int32(0), jnp.int32(0)))
    for rows, count in zip((LONG, SHORT), counts):
        tasks[COUNT[rows]] = count
        for n in range(AT_ONCE[rows]):
            tasks[FIRST[rows] + count + n] = NOTHING


def stage_weights(device, d, weights):
    left = left_half(LANES)
    for jc in range(CHUNKS):
        x = device[lanes(jc), :]
        top = x.astype(BF16).astype(F32)
        rest = pltpu.roll(x - top, WIDTH, axis=1)
        weights[2 * d * CHUNKS + jc] = jnp.where(left, top, rest).astype(BF16)
        weights[(2 * d + 1) * CHUNKS + jc] = jnp.where(left, rest, top).astype(BF16)


def eval_tile(at, row, rows, own_pos, places, tile):
    step = 64
    for piece in range(rows // step):
        squared = None
        for c in range(3):
            mine = own_pos[c, pl.ds(row + piece * step, step), :]
            offset = mine - places[at, c : c + 1, :]
            squared = offset * offset if squared is None else squared + offset * offset
        radius = squared * lax.rsqrt(jnp.maximum(squared, 1e-30))
        margin = jnp.maximum(1.0 - radius, 0.0)
        margin_sq = margin * margin
        values = (margin_sq * margin_sq) * (1.2 * radius + 0.3)
        top, rest = split_two(values)
        tile[piece * step : (piece + 1) * step, 0:LANES] = top
        tile[piece * step : (piece + 1) * step, LANES:] = rest


def decode(code):
    return code >> 11, pl.multiple_of(code & 2047, 8)


def add_product(at, row, rows, tile, weights, total):
    both = jnp.concatenate([weights[at], weights[at]], axis=0)
    total[pl.ds(row, rows), :] += nn(tile, both)


def run_steps(tasks, own_pos, places, weights, total, tiles, skip=None):
    for rows in (LONG, SHORT):
        width = AT_ONCE[rows]
        begin = skip[rows] // width if skip else 0

        def some(i, _):
            picked = [decode(tasks[FIRST[rows] + width * i + n]) for n in range(width)]
            for n, (at, row) in enumerate(picked):
                eval_tile(at, row, rows, own_pos, places, tiles.at[n, 0:rows])
            for n, (at, row) in enumerate(picked):
                add_product(at, row, rows, tiles[n, 0:rows], weights, total)
            return 0

        lax.fori_loop(begin, (tasks[COUNT[rows]] + (width - 1)) // width, some, 0)


def keep_tiles(tasks, own_pos, places, kept):
    for rows in (LONG, SHORT):
        width = AT_ONCE[rows]

        def some(i, _):
            for n in range(width):
                at, row = decode(tasks[FIRST[rows] + width * i + n])
                eval_tile(at, row, rows, own_pos, places, kept[rows].at[width * i + n])
            return 0

        batches = (tasks[COUNT[rows]] + (width - 1)) // width
        lax.fori_loop(0, jnp.minimum(batches, KEPT[rows] // width), some, 0)


def run_kept(tasks, kept, weights, total):
    for rows in (LONG, SHORT):
        width = AT_ONCE[rows]

        def some(i, _):
            for n in range(width):
                at, row = decode(tasks[FIRST[rows] + width * i + n])
                add_product(at, row, rows, kept[rows][width * i + n], weights, total)
            return 0

        batches = (tasks[COUNT[rows]] + (width - 1)) // width
        lax.fori_loop(0, jnp.minimum(batches, KEPT[rows] // width), some, 0)


def own_rows(o):
    return slice(o * PADDED, o * PADDED + STARS)


def padding(o):
    return slice(o * PADDED + STARS, (o + 1) * PADDED)


def stage_own_sum(own_sum, total):
    for o in range(BLOCKS):
        total[own_rows(o), :] = own_sum[o * STARS : (o + 1) * STARS, :]
        total[padding(o), :] = jnp.zeros((PADDED - STARS, LANES), F32)


def image_of(total, own_pos, vector):
    left = left_half(STARS)
    noise = jnp.where(left, own_pos[NOISE, own_rows(0), :], own_pos[NOISE, own_rows(1), :])
    return noise * vector + jnp.where(left, fold(total[own_rows(0), :]), fold(total[own_rows(1), :]))


def stage_places(device, d, places):
    for b in range(BLOCKS):
        for jc in range(CHUNKS):
            places[(BLOCKS * d + b) * CHUNKS + jc] = device[meta_rows(b, jc), :]


def own_kernel(packed, own_pos, own_sum, places, own_tasks, weights, total, tiles, *scratch):
    times, lists, idents, table, scalars, sem = scratch
    build_table([packed], 0, lambda k: k < BLOCKS, table, times, lists, idents)
    copy = pltpu.make_async_copy(table, scalars, sem)
    copy.start()
    stage_places(packed, 0, places)
    stage_weights(packed, 0, weights)
    for o in range(BLOCKS):
        for c in range(NOISE + 1):
            for ic in range(CHUNKS):
                first = o * PADDED + ic * LANES
                own_pos[c, first : first + LANES, :] = column(places[o * CHUNKS + ic, c : c + 1, :])
            own_pos[c, padding(o), :] = jnp.zeros((PADDED - STARS, LANES), F32)
    total[...] = jnp.zeros(total.shape, F32)
    copy.wait()
    list_steps(scalars, own_tasks, BLOCKS)
    run_steps(own_tasks, own_pos, places, weights, total, tiles)
    for o in range(BLOCKS):
        own_sum[o * STARS : (o + 1) * STARS, :] = total[own_rows(o), :]


def first_kernel(
    low, mid, high, own_pos, own_sum, image_ref, places, tasks, weights, total, tiles, *scratch
):
    times, lists, idents, table, scalars, sem = scratch
    groups = (low, mid, high)
    devices = [groups[d // 3].at[d % 3] for d in range(9)]
    build_table(devices, OWN, lambda k: (k < OWN) | (k >= OWN + BLOCKS), table, times, lists, idents)
    copy = pltpu.make_async_copy(table, scalars, sem)
    copy.start()
    for d, device in enumerate(devices):
        if d != OWN // BLOCKS:
            stage_places(device, d, places)
            stage_weights(device, d, weights)
    stage_own_sum(own_sum, total)
    copy.wait()
    list_steps(scalars, tasks, NEAR)
    run_steps(tasks, own_pos, places, weights, total, tiles)
    image_ref[...] = image_of(total, own_pos, mid[1, 0:STARS, :])


def between_kernel(
    own_tasks, tasks, once, own_pos, own_places, places, own_sum, kept_long, kept_short, weights, total, tiles
):
    stage_weights(once, 0, weights)
    total[...] = jnp.zeros(total.shape, F32)
    run_steps(own_tasks, own_pos, own_places, weights, total, tiles)
    for o in range(BLOCKS):
        own_sum[o * STARS : (o + 1) * STARS, :] = total[own_rows(o), :]
    keep_tiles(tasks, own_pos, places, {LONG: kept_long, SHORT: kept_short})


def second_kernel(
    tasks,
    low,
    mid,
    high,
    own_pos,
    own_sum,
    places,
    kept_long,
    kept_short,
    packed,
    rank,
    image_ref,
    moments_ref,
    weights,
    total,
    tiles,
    sums,
):
    groups = (low, mid, high)
    for d in range(9):
        if d != OWN // BLOCKS:
            stage_weights(groups[d // 3].at[d % 3], d, weights)
    stage_own_sum(own_sum, total)
    run_kept(tasks, {LONG: kept_long, SHORT: kept_short}, weights, total)
    run_steps(tasks, own_pos, places, weights, total, tiles, skip=KEPT)
    start, once = packed[0:STARS, :], mid[1]
    twice = image_of(total, own_pos, once)
    products = (start * start, start * once, once * once, start * twice, once * twice)
    sums[...] = jnp.zeros(sums.shape, F32)
    for n, product in enumerate(products):
        sums[n : n + 1, :] = jnp.sum(product, axis=0, keepdims=True)
    top, middle, rest = (part.astype(F32) for part in split_three(fold(sums[...])))
    moments_ref[...] = jnp.where(left_half(8), top, middle)
    for n in range(3):
        pair = jnp.where(left_half(1), rest[2 * n : 2 * n + 1, :], rest[2 * n + 1 : 2 * n + 2, :])
        moments_ref[5 + n : 6 + n, :] = pair
    unsort(twice, rank, image_ref)


def unsort_kernel(x_ref, rank_ref, out_ref):
    unsort(x_ref[...], rank_ref, out_ref)


def two_sum(a, b):
    s = a + b
    back = s - a
    return s, (a - (s - back)) + (b - back)


def halves(a):
    scaled = 4097.0 * a
    top = scaled - (scaled - a)
    return top, a - top


def two_product(a, b):
    p = a * b
    a1, a2 = halves(a)
    b1, b2 = halves(b)
    return p, ((a1 * b1 - p) + a1 * b2 + a2 * b1) + a2 * b2


def pair_add(a, b):
    s, e = two_sum(a[0], b[0])
    return two_sum(s, e + (a[1] + b[1]))


def pair_mul(a, b):
    p, e = two_product(a[0], b[0])
    return two_sum(p, e + (a[0] * b[1] + a[1] * b[0]))


def final_kernel(moments_ref, start_ref, once_ref, twice_ref, solution_ref, residual_ref):
    gathered = moments_ref[...]
    rolled = pltpu.roll(gathered, WIDTH, axis=1)
    left = iota((1, LANES), 1) < WIDTH
    moments = []
    for n in range(5):
        source = gathered if n % 2 == 0 else rolled
        last = source[5 + n // 2 : 6 + n // 2, :]
        s, e = two_sum(gathered[n : n + 1, :], rolled[n : n + 1, :])
        s, e = two_sum(s, e + last)
        moments.append((jnp.where(left, s, 1.0), jnp.where(left, e, 0.0)))
    norm, curve, square, cross, cube = moments
    alpha = norm[0] / curve[0]
    step = (alpha, jnp.zeros_like(alpha))
    minus = (-alpha, jnp.zeros_like(alpha))
    step_sq = pair_mul(step, step)
    by_curve = pair_mul(minus, curve)
    norm_next = pair_add(pair_add(norm, pair_add(by_curve, by_curve)), pair_mul(step_sq, square))
    beta = norm_next[0] / norm[0]
    gamma = two_sum(jnp.ones_like(beta), beta)
    curve_next = pair_add(
        pair_mul(pair_mul(gamma, gamma), curve),
        pair_add(
            pair_mul(pair_mul(gamma, minus), pair_add(cross, square)),
            pair_mul(step_sq, cube),
        ),
    )
    alpha_next = norm_next[0] / curve_next[0]
    alpha, beta, alpha_next = (column(row)[0:WIDTH] for row in (alpha, beta, alpha_next))
    for o in range(BLOCKS):
        for ic in range(CHUNKS):
            at = (o, slice(None), lanes(ic))
            start, once, twice = start_ref[at], once_ref[at], twice_ref[at]
            residual = start - alpha * once
            direction = residual + beta * start
            image = (once - alpha * twice) + beta * once
            solution_ref[at] = alpha * start + alpha_next * direction
            residual_ref[at] = residual - alpha_next * image


def shape(*dims, dtype=F32):
    return jax.ShapeDtypeStruct(dims, dtype)


def call(kernel, out_shape, scratch=(), in_specs=None, count=None, out_specs=None, flops=0, nbytes=1 << 20):
    return pl.pallas_call(
        kernel,
        out_shape=out_shape,
        in_specs=in_specs if in_specs is not None else [VMEM] * count,
        out_specs=out_specs or jax.tree.map(lambda _: VMEM, out_shape),
        scratch_shapes=list(scratch),
        compiler_params=pltpu.CompilerParams(vmem_limit_bytes=LIMIT),
        cost_estimate=pl.CostEstimate(flops=flops, bytes_accessed=nbytes, transcendentals=0),
    )


BLOCK = shape(BLOCKS, WIDTH, STARS)
OWN_POS = shape(NOISE + 1, BLOCKS * PADDED, LANES)
OWN_SUM = shape(BLOCKS * STARS, LANES)
TASKS = shape(LISTS, dtype=jnp.int32)


def pairs_scratch(blocks):
    return [
        pltpu.VMEM((blocks * CHUNKS, LANES, LANES), BF16),
        pltpu.VMEM((BLOCKS * PADDED, LANES), F32),
        pltpu.VMEM((max(AT_ONCE.values()), LONG, 2 * LANES), BF16),
    ]


def table_scratch(rows):
    return [
        pltpu.VMEM((rows, STARS), F32),
        pltpu.VMEM((rows, LANES), F32),
        pltpu.VMEM((rows, LANES), F32),
        pltpu.VMEM((rows, LANES), jnp.int32),
        pltpu.SMEM((rows, LANES), jnp.int32),
        pltpu.SemaphoreType.DMA,
    ]


def apply_own(packed):
    return call(
        own_kernel,
        (OWN_POS, OWN_SUM, shape(BLOCKS * CHUNKS, META, LANES), TASKS),
        scratch=pairs_scratch(BLOCKS) + table_scratch(8),
        count=1,
        out_specs=(VMEM, VMEM, VMEM, SMEM),
        flops=1 << 30,
    )(packed)


def apply_first(low, mid, high, own_pos, own_sum):
    return call(
        first_kernel,
        (shape(STARS, LANES), shape(NEAR * CHUNKS, META, LANES), TASKS),
        scratch=pairs_scratch(NEAR) + table_scratch(24),
        count=5,
        out_specs=(VMEM, VMEM, SMEM),
    )(low, mid, high, own_pos, own_sum)


def apply_between(own_tasks, tasks, once, own_pos, own_places, places):
    return call(
        between_kernel,
        (
            OWN_SUM,
            shape(KEPT[LONG], LONG, 2 * LANES, dtype=BF16),
            shape(KEPT[SHORT], SHORT, 2 * LANES, dtype=BF16),
        ),
        scratch=pairs_scratch(BLOCKS),
        in_specs=[SMEM, SMEM] + [VMEM] * 4,
        flops=1 << 30,
    )(own_tasks, tasks, once, own_pos, own_places, places)


def apply_second(tasks, low, mid, high, own_pos, own_sum, places, kept_long, kept_short, packed, rank):
    return call(
        second_kernel,
        (BLOCK, shape(8, LANES)),
        scratch=pairs_scratch(NEAR) + [pltpu.VMEM((8, LANES), F32)],
        in_specs=[SMEM] + [VMEM] * 10,
    )(tasks, low, mid, high, own_pos, own_sum, places, kept_long, kept_short, packed, rank)


def shift(x, axis, by):
    count = lax.axis_size(axis)
    return lax.ppermute(x, axis, [(i, i + by) for i in range(count) if 0 <= i + by < count])


SKY = ("far", "near", "x", "core")


def sky_shift(x, by):
    count = lax.axis_size(SKY)
    return lax.ppermute(x, SKY, [(i, i + by) for i in range(count) if 0 <= i + by < count])


def with_halo(x):
    before, after = shift(x, "tm", 1), shift(x, "tm", -1)
    mid = jnp.stack([before, x, after])
    return sky_shift(mid, 1), mid, sky_shift(mid, -1)


def local(star_pos, noise_var, targets, pair_list):
    ident = (lax.axis_index(SKY) * lax.axis_size("tm") + lax.axis_index("tm")) * BLOCKS
    packed, rank = call(
        sort_kernel,
        (shape(ROWS, LANES), shape(BLOCKS, STARS)),
        scratch=[pltpu.VMEM((BLOCKS * WIDTH, STARS), F32), pltpu.VMEM((2 * META, STARS), F32)],
        in_specs=[SMEM, VMEM, VMEM, VMEM, VMEM],
    )(ident.reshape(1), star_pos, noise_var, targets, pair_list)
    low, mid, high = with_halo(packed)
    own_pos, own_sum, own_places, own_tasks = apply_own(packed)
    once, places, tasks = apply_first(low, mid, high, own_pos, own_sum)
    low, mid, high = with_halo(once)
    own_sum, *kept = apply_between(own_tasks, tasks, once, own_pos, own_places, places)
    once_back = call(unsort_kernel, BLOCK, count=2, flops=1 << 28)(once, rank)
    twice_back, moments = apply_second(
        tasks, low, mid, high, own_pos, own_sum, places, *kept, packed, rank
    )
    for axis in ("core", "x", "tm", "near", "far"):
        moments = lax.psum(moments, axis)
    return call(final_kernel, (BLOCK, BLOCK), count=4)(moments, targets, once_back, twice_back)


def solution(mesh):
    sky, tm = mesh.devices.shape
    near = 4 if sky % 32 == 0 else 1
    finer = Mesh(mesh.devices.reshape(sky // (8 * near), near, 4, 2, tm), SKY + ("tm",))
    both = SKY + ("tm",)
    in_specs = (P(both, None, None), P(both, None), P(both, None, None), P(both, None))
    out_specs = (P(both, None, None), P(both, None, None))
    return jax.shard_map(local, mesh=finer, in_specs=in_specs, out_specs=out_specs, check_vma=False)
```

time: 158 us -> 139 us (0.88)
  the two profiles are of different devices: /device:TPU:32 before, /device:TPU:8 now
where the time goes in v2:
time: 139 us
  blocking collectives  68 us (49%)
  starting transfers between devices  32.3 us (23%)
  Pallas kernels  23.6 us (17%)
  waiting for transfers between devices  10.6 us (8%)
  local copies, waits for them, and re-layouts  3.03 us (2%)
    psum x5, blocking collectives, local(): moments = lax.psum(moments, axis)  68 us
    ppermute x4, starting transfers between devices, sky_shift(): lax.ppermute(x, SKY, [(i, i + by) for i in range(count) if 0 <= i + by <...  17.4 us
    ppermute x4, starting transfers between devices, shift(): lax.ppermute(x, axis, [(i, i + by) for i in range(count) if 0 <= i + by <...  14.9 us
    ppermute x4, waiting for transfers between devices, shift(): lax.ppermute(x, axis, [(i, i + by) for i in range(count) if 0 <= i + by <...  10.6 us
    pallas_call x1, Pallas kernels, apply_first(): call(first_kernel, (shape(STARS, LANES), shape(NEAR * CHUNKS, META, LANES...  6.93 us
    pallas_call x1, Pallas kernels, apply_between(): call(between_kernel, (OWN_SUM, shape(KEPT[LONG], LONG, 2 * LANES, dtype=B...  5.4 us
    pallas_call x1, Pallas kernels, apply_own(): call(own_kernel, (OWN_POS, OWN_SUM, shape(BLOCKS * CHUNKS, META, LANES),...  5.06 us
    pallas_call x1, Pallas kernels, apply_second(): call(second_kernel, (BLOCK, shape(8, LANES)), scratch=pairs_scratch(NEAR)...  3.34 us
  transfers between devices with their start and end apart: 8, of which 4 were waited for; matrix products, arithmetic and copies ran while one was open for 0% of the time, Pallas kernels for 8%

profile of v2, /device:TPU:8, one launch (start us, length us, event | category | flops | bytes accessed | tf_op | source)
XLA Modules:
  0.0 138.5 jit_solution(17919410583488033830)
XLA Ops:
  0.6 0.7 copy.6.pos_ref
  1.4 0.0 copy-start
  1.4 0.9 copy-done
  2.3 0.0 copy-start.2
  2.3 0.7 copy-done.2
  3.0 0.0 copy-start.3
  3.0 0.7 copy-done.3
  3.7 1.3 shard_map.59
  5.0 3.5 %collective-permute-start = (f32[576,128]{1,0:T(8,128)S(1)}, f32[576,128]{1,0:T(8,128)S(1)}, u32[]{:S(2)}, u32[]{:S(2)}) collective-permute-start(f32[576,128]{1,0:T(8,128)S(1)} %get-tuple-element.16.packed), channel_id=1, source_target_pairs={{0,1},{1,2},{2,3},{4,5},{5,6},{6,7},{8,9},{9,10},{10,11},{12,13},{... | collective-permute-start | bytes 884744 | tf_op jit(solution)/shard_map/ppermute | solution.py:575
  8.4 5.6 %collective-permute-start.1 = (f32[576,128]{1,0:T(8,128)S(1)}, f32[576,128]{1,0:T(8,128)S(1)}, u32[]{:S(2)}, u32[]{:S(2)}) collective-permute-start(f32[576,128]{1,0:T(8,128)S(1)} %get-tuple-element.16.packed), channel_id=1, source_target_pairs={{1,0},{2,1},{3,2},{5,4},{6,5},{7,6},{9,8},{10,9},{11,10},{13,12},{... | collective-permute-start | bytes 884744 | tf_op jit(solution)/shard_map/ppermute | solution.py:575
  14.0 2.7 %collective-permute-done = f32[576,128]{1,0:T(8,128)S(1)} collective-permute-done((f32[576,128]{1,0:T(8,128)S(1)}, f32[576,128]{1,0:T(8,128)S(1)}, u32[]{:S(2)}, u32[]{:S(2)}) %collective-permute-start) | collective-permute-done | bytes 294944 | tf_op jit(solution)/shard_map/ppermute | solution.py:575
  16.8 2.0 %collective-permute-done.1 = f32[576,128]{1,0:T(8,128)S(1)} collective-permute-done((f32[576,128]{1,0:T(8,128)S(1)}, f32[576,128]{1,0:T(8,128)S(1)}, u32[]{:S(2)}, u32[]{:S(2)}) %collective-permute-start.1) | collective-permute-done | bytes 294944 | tf_op jit(solution)/shard_map/ppermute | solution.py:575
  18.8 0.1 pad_maximum_fusion.mid
  18.9 1.3 collective-permute-start.2
  20.2 1.3 collective-permute-start.3
  21.5 5.1 %shard_map.60 = (f32[4,1536,128]{2,1,0:T(8,128)S(1)}, f32[1024,128]{1,0:T(8,128)S(1)}, f32[8,8,128]{2,1,0:T(8,128)S(1)}, s32[512]{0:T(512)S(1)}) custom-call(f32[576,128]{1,0:T(8,128)S(1)} %get-tuple-element.16.packed), custom_call_target="tpu_custom_call" | custom-call | flops 1073741824 | bytes 1048576 | tf_op jit(solution)/shard_map/pallas_call | solution.py:530
  26.6 0.0 collective-permute-done.2.low
  26.6 0.0 collective-permute-done.3.high
  26.6 6.9 %shard_map.61 = (f32[512,128]{1,0:T(8,128)S(1)}, f32[72,8,128]{2,1,0:T(8,128)S(1)}, s32[512]{0:T(512)S(1)}) custom-call(f32[3,576,128]{2,1,0:T(8,128)S(1)} %collective-permute-done.2.low, f32[3,576,128]{2,1,0:T(8,128)S(1)} %pad_maximum_fusion.mid, f32[3,576,128]{2,1,0:T(8,128)S(1)} %collective-permute-done.3.high, ...), custom_call_target="tpu_custom_call" | custom-call | bytes 1048576 | tf_op jit(solution)/shard_map/pallas_call | solution.py:541
  33.5 3.4 %collective-permute-start.4 = (f32[512,128]{1,0:T(8,128)S(1)}, f32[512,128]{1,0:T(8,128)S(1)}, u32[]{:S(2)}, u32[]{:S(2)}) collective-permute-start(f32[512,128]{1,0:T(8,128)S(1)} %get-tuple-element.20.once.x_ref), channel_id=1, source_target_pairs={{0,1},{1,2},{2,3},{4,5},{5,6},{6,7},{8,9},{9,10},{10,11},{12,13},{... | collective-permute-start | bytes 786440 | tf_op jit(solution)/shard_map/ppermute | solution.py:575
  37.0 2.4 %collective-permute-start.5 = (f32[512,128]{1,0:T(8,128)S(1)}, f32[512,128]{1,0:T(8,128)S(1)}, u32[]{:S(2)}, u32[]{:S(2)}) collective-permute-start(f32[512,128]{1,0:T(8,128)S(1)} %get-tuple-element.20.once.x_ref), channel_id=1, source_target_pairs={{1,0},{2,1},{3,2},{5,4},{6,5},{7,6},{9,8},{10,9},{11,10},{13,12},{... | collective-permute-start | bytes 786440 | tf_op jit(solution)/shard_map/ppermute | solution.py:575
  39.4 2.4 %collective-permute-done.4 = f32[512,128]{1,0:T(8,128)S(1)} collective-permute-done((f32[512,128]{1,0:T(8,128)S(1)}, f32[512,128]{1,0:T(8,128)S(1)}, u32[]{:S(2)}, u32[]{:S(2)}) %collective-permute-start.4) | collective-permute-done | bytes 262176 | tf_op jit(solution)/shard_map/ppermute | solution.py:575
  41.8 3.4 %collective-permute-done.5 = f32[512,128]{1,0:T(8,128)S(1)} collective-permute-done((f32[512,128]{1,0:T(8,128)S(1)}, f32[512,128]{1,0:T(8,128)S(1)}, u32[]{:S(2)}, u32[]{:S(2)}) %collective-permute-start.5) | collective-permute-done | bytes 262176 | tf_op jit(solution)/shard_map/ppermute | solution.py:575
  45.3 0.1 pad_maximum_fusion.1.mid
  45.3 13.5 %collective-permute-start.6 = (f32[3,512,128]{2,1,0:T(8,128)S(1)}, f32[3,512,128]{2,1,0:T(8,128)S(1)}, u32[]{:S(2)}, u32[]{:S(2)}) collective-permute-start(f32[3,512,128]{2,1,0:T(8,128)S(1)} %pad_maximum_fusion.1.mid), channel_id=1, source_target_pairs={{0,4},{4,8},{8,12},{12,16},{16,20},{20,24},{24,28},{28,32},{32,36}... | collective-permute-start | bytes 2359304 | tf_op jit(solution)/shard_map/ppermute | solution.py:583
  58.8 1.3 collective-permute-start.7
  60.1 0.5 shard_map.64.once_ref
  60.6 5.4 %shard_map.62 = (f32[1024,128]{1,0:T(8,128)S(1)}, bf16[40,256,256]{2,1,0:T(8,128)(2,1)S(1)}, bf16[48,64,256]{2,1,0:T(8,128)(2,1)S(1)}) custom-call(s32[512]{0:T(512)S(1)} %get-tuple-element.21.own_tasks, s32[512]{0:T(512)S(1)} %get-tuple-element.19.tasks, f32[512,128]{1,0:T(8,128)S(1)} %get-tuple-element.20.once.x_ref, ...), custom_call_target="tpu_custom_call" | custom-call | flops 1073741824 | bytes 1048576 | tf_op jit(solution)/shard_map/pallas_call | solution.py:551
  66.0 0.0 collective-permute-done.6.low
  66.0 0.0 collective-permute-done.7.high
  66.0 0.0 copy-start.1
  66.0 3.3 %shard_map.63 = (f32[2,64,512]{2,1,0:T(8,128)S(1)}, f32[8,128]{1,0:T(8,128)S(1)}) custom-call(s32[512]{0:T(512)S(1)} %get-tuple-element.19.tasks, f32[3,512,128]{2,1,0:T(8,128)S(1)} %collective-permute-done.6.low, f32[3,512,128]{2,1,0:T(8,128)S(1)} %pad_maximum_fusion.1.mid, f32[3,512,128]{2,1,0:T(8,128)S(1)} %collective-permute-done.7.high, ...), custom_call_target="tpu_custom_call" | custom-call | bytes 1048576 | tf_op jit(solution)/shard_map/pallas_call | solution.py:565
  69.4 12.1 %psum.35 = f32[8,128]{1,0:T(8,128)S(1)} all-reduce(f32[8,128]{1,0:T(8,128)S(1)} %get-tuple-element.28), channel_id=1, replica_groups=mesh['far'=4,'near'=4,'x'=4,'core'=2,'tm'=4] {'core'}, use_global_device_ids=true, to_apply=%region_0.0 | all-reduce | flops 1024 | bytes 8192 | tf_op jit(solution)/shard_map/psum | solution.py:610
  81.5 14.4 %psum.36 = f32[8,128]{1,0:T(8,128)S(1)} all-reduce(f32[8,128]{1,0:T(8,128)S(1)} %psum.35), channel_id=1, replica_groups=mesh['far'=4,'near'=4,'x'=4,'core'=2,'tm'=4] {'x'}, use_global_device_ids=true, to_apply=%region_1.0 | all-reduce | flops 1024 | bytes 8192 | tf_op jit(solution)/shard_map/psum | solution.py:610
  95.9 7.9 %psum.37 = f32[8,128]{1,0:T(8,128)S(1)} all-reduce(f32[8,128]{1,0:T(8,128)S(1)} %psum.36), channel_id=1, replica_groups=mesh['far'=4,'near'=4,'x'=4,'core'=2,'tm'=4] {'tm'}, use_global_device_ids=true, to_apply=%region_2.0 | all-reduce | flops 1024 | bytes 8192 | tf_op jit(solution)/shard_map/psum | solution.py:610
  103.8 15.3 %psum.38 = f32[8,128]{1,0:T(8,128)S(1)} all-reduce(f32[8,128]{1,0:T(8,128)S(1)} %psum.37), channel_id=1, replica_groups=mesh['far'=4,'near'=4,'x'=4,'core'=2,'tm'=4] {'near'}, use_global_device_ids=true, to_apply=%region_3.0 | all-reduce | flops 1024 | bytes 8192 | tf_op jit(solution)/shard_map/psum | solution.py:610
  119.1 18.3 %psum.39.moments_ref = f32[8,128]{1,0:T(8,128)S(1)} all-reduce(f32[8,128]{1,0:T(8,128)S(1)} %psum.38), channel_id=1, replica_groups=mesh['far'=4,'near'=4,'x'=4,'core'=2,'tm'=4] {'far'}, use_global_device_ids=true, to_apply=%region_4.0 | all-reduce | flops 1024 | bytes 8192 | tf_op jit(solution)/shard_map/psum | solution.py:610
  137.4 0.0 copy-done.1
  137.4 1.1 shard_map.65
Async XLA Ops:
  1.4 0.9 copy-start
  2.3 0.7 copy-start.2
  3.0 0.7 copy-start.3
  5.0 11.8 %collective-permute-start = (f32[576,128]{1,0:T(8,128)S(1)}, f32[576,128]{1,0:T(8,128)S(1)}, u32[]{:S(2)}, u32[]{:S(2)}) collective-permute-start(f32[576,128]{1,0:T(8,128)S(1)} %get-tuple-element.16.packed), channel_id=1, source_target_pairs={{0,1},{1,2},{2,3},{4,5},{5,6},{6,7},{8,9},{9,10},{10,11},{12,13},{... | collective-permute-start | bytes 884744 | tf_op jit(solution)/shard_map/ppermute | solution.py:575
  8.4 10.4 %collective-permute-start.1 = (f32[576,128]{1,0:T(8,128)S(1)}, f32[576,128]{1,0:T(8,128)S(1)}, u32[]{:S(2)}, u32[]{:S(2)}) collective-permute-start(f32[576,128]{1,0:T(8,128)S(1)} %get-tuple-element.16.packed), channel_id=1, source_target_pairs={{1,0},{2,1},{3,2},{5,4},{6,5},{7,6},{9,8},{10,9},{11,10},{13,12},{... | collective-permute-start | bytes 884744 | tf_op jit(solution)/shard_map/ppermute | solution.py:575
  18.9 7.7 %collective-permute-start.2 = (f32[3,576,128]{2,1,0:T(8,128)S(1)}, f32[3,576,128]{2,1,0:T(8,128)S(1)}, u32[]{:S(2)}, u32[]{:S(2)}) collective-permute-start(f32[3,576,128]{2,1,0:T(8,128)S(1)} %pad_maximum_fusion.mid), channel_id=1, source_target_pairs={{0,4},{4,8},{8,12},{12,16},{16,20},{20,24},{24,28},{28,32},{32,36}... | collective-permute-start | bytes 2654216 | tf_op jit(solution)/shard_map/ppermute | solution.py:583
  20.2 6.4 %collective-permute-start.3 = (f32[3,576,128]{2,1,0:T(8,128)S(1)}, f32[3,576,128]{2,1,0:T(8,128)S(1)}, u32[]{:S(2)}, u32[]{:S(2)}) collective-permute-start(f32[3,576,128]{2,1,0:T(8,128)S(1)} %pad_maximum_fusion.mid), channel_id=1, source_target_pairs={{4,0},{8,4},{12,8},{16,12},{20,16},{24,20},{28,24},{32,28},{36,32}... | collective-permute-start | bytes 2654216 | tf_op jit(solution)/shard_map/ppermute | solution.py:583
  33.5 8.3 %collective-permute-start.4 = (f32[512,128]{1,0:T(8,128)S(1)}, f32[512,128]{1,0:T(8,128)S(1)}, u32[]{:S(2)}, u32[]{:S(2)}) collective-permute-start(f32[512,128]{1,0:T(8,128)S(1)} %get-tuple-element.20.once.x_ref), channel_id=1, source_target_pairs={{0,1},{1,2},{2,3},{4,5},{5,6},{6,7},{8,9},{9,10},{10,11},{12,13},{... | collective-permute-start | bytes 786440 | tf_op jit(solution)/shard_map/ppermute | solution.py:575
  37.0 8.3 %collective-permute-start.5 = (f32[512,128]{1,0:T(8,128)S(1)}, f32[512,128]{1,0:T(8,128)S(1)}, u32[]{:S(2)}, u32[]{:S(2)}) collective-permute-start(f32[512,128]{1,0:T(8,128)S(1)} %get-tuple-element.20.once.x_ref), channel_id=1, source_target_pairs={{1,0},{2,1},{3,2},{5,4},{6,5},{7,6},{9,8},{10,9},{11,10},{13,12},{... | collective-permute-start | bytes 786440 | tf_op jit(solution)/shard_map/ppermute | solution.py:575
  45.3 20.7 %collective-permute-start.6 = (f32[3,512,128]{2,1,0:T(8,128)S(1)}, f32[3,512,128]{2,1,0:T(8,128)S(1)}, u32[]{:S(2)}, u32[]{:S(2)}) collective-permute-start(f32[3,512,128]{2,1,0:T(8,128)S(1)} %pad_maximum_fusion.1.mid), channel_id=1, source_target_pairs={{0,4},{4,8},{8,12},{12,16},{16,20},{20,24},{24,28},{28,32},{32,36}... | collective-permute-start | bytes 2359304 | tf_op jit(solution)/shard_map/ppermute | solution.py:583
  58.8 7.2 %collective-permute-start.7 = (f32[3,512,128]{2,1,0:T(8,128)S(1)}, f32[3,512,128]{2,1,0:T(8,128)S(1)}, u32[]{:S(2)}, u32[]{:S(2)}) collective-permute-start(f32[3,512,128]{2,1,0:T(8,128)S(1)} %pad_maximum_fusion.1.mid), channel_id=1, source_target_pairs={{4,0},{8,4},{12,8},{16,12},{20,16},{24,20},{28,24},{32,28},{36,32}... | collective-permute-start | bytes 2359304 | tf_op jit(solution)/shard_map/ppermute | solution.py:583
  66.0 71.4 %copy-start.1 = (f32[2,64,512]{2,1,0:T(8,128)S(1)}, f32[2,64,512]{2,1,0:T(8,128)}, u32[]{:S(2)}) copy-start(f32[2,64,512]{2,1,0:T(8,128)} %start_ref.1) | copy-start | bytes 786436

commit v3 on v2

--- a/solution.py
+++ b/solution.py
@@ -12,7 +12,7 @@
 BLOCKS, WIDTH, STARS, LANES = 2, 64, 512, 128
 CHUNKS = STARS // LANES
 NOISE, LIST, IDENT, META = 3, 4, 5, 8
-COLUMNS = 16
+SLOTS = 16
 ROWS = STARS + CHUNKS * BLOCKS * META
 NEAR = 18
 OWN = 8
@@ -107,7 +107,7 @@
 def sort_kernel(ident_ref, pos_ref, noise_ref, targets_ref, list_ref, packed_ref, rank_ref, tall, small):
     values = jnp.zeros((STARS, LANES), F32)
     for b in range(BLOCKS):
-        rank = ranks(pos_ref[b, 2:3, :])
+        rank = ranks(pos_ref[2, b : b + 1, :])
         rank_ref[b : b + 1, :] = rank
         where_to = one_hot(rank)
         tall[...] = jnp.zeros(tall.shape, F32)
@@ -115,96 +115,86 @@
         parts = nt(where_to, jnp.concatenate(split_three(tall[...]), axis=0))
         values += (parts[:, lanes(0)] + parts[:, lanes(1)]) + parts[:, lanes(2)]
         small[...] = jnp.zeros(small.shape, F32)
-        small[0:3, :] = pos_ref[b]
+        for c in range(3):
+            small[c : c + 1, :] = pos_ref[c, b : b + 1, :]
         small[NOISE : NOISE + 1, :] = noise_ref[b : b + 1, :]
         parts = nt(jnp.concatenate(split_three(small[...]), axis=0), where_to)
         height = small.shape[0]
         meta = ((parts[:height] + parts[height : 2 * height]) + parts[2 * height :])[0:META]
+        listed = list_ref[b : b + 1, :].astype(F32) + 1.0
         for jc in range(CHUNKS):
             packed_ref[meta_rows(b, jc), :] = meta[:, lanes(jc)]
             first = STARS + (jc * BLOCKS + b) * META
             ident = jnp.full((1, LANES), (ident_ref[0] + b + 1).astype(F32))
             packed_ref[first + IDENT : first + IDENT + 1, :] = ident
-        listed = list_ref[b : b + 1, :].astype(F32) + 1.0
-        first = STARS + b * META + LIST
-        packed_ref[first : first + 1, 0 : listed.shape[1]] = listed
+            packed_ref[first + LIST : first + LIST + 1, 0 : listed.shape[1]] = listed
     packed_ref[0:STARS, :] = values
 
 
-def build_table(devices, own, chosen, table, times, lists, idents):
-    rows = table.shape[0]
-    for scratch in (times, lists, idents):
-        scratch[...] = jnp.zeros(scratch.shape, F32)
-    for d, device in enumerate(devices):
-        for b in range(BLOCKS):
-            k = BLOCKS * d + b
-            for jc in range(CHUNKS):
-                first = STARS + (jc * BLOCKS + b) * META
-                times[k : k + 1, lanes(jc)] = device[first + 2 : first + 3, :]
-            first = STARS + b * META
-            lists[k : k + 1, :] = device[first + LIST : first + LIST + 1, :]
-            idents[k : k + 1, :] = device[first + IDENT : first + IDENT + 1, :]
-    place = iota((rows, LANES), 1)
-    block = iota((rows, 1), 0)
-    out = jnp.full((rows, LANES), -1, jnp.int32)
-    ident = idents[:, 0:1]
+def build_table(places, blocks, own, own_times, chosen, table, turned):
+    entries = blocks * CHUNKS
+    turned[...] = jnp.zeros(turned.shape, F32)
+    flipped = []
+    for n, row in enumerate((2, LIST, IDENT)):
+        for at in range(entries):
+            turned[n, at : at + 1, :] = places[at, row : row + 1, :]
+        flipped.append(jnp.transpose(turned[n]))
+    times, lists, idents = flipped
+    first, last = times[0:1, :], times[LANES - 1 : LANES, :]
+    lists, ident = lists[0:SLOTS, :], idents[0:1, :]
+    entry = iota((1, LANES), 1)
+    rows = []
     for o in range(BLOCKS):
-        own_ident = idents[own + o : own + o + 1, 0:1]
-        own_list = lists[own + o : own + o + 1, :]
-        own_list = jnp.where(own_list == 0.0, -5.0, own_list)
-        hit = jnp.where((lists[...] == own_ident) | (own_list == ident), 1.0, 0.0)
-        linked = (jnp.max(hit, axis=1, keepdims=True) > 0.0) | (ident == own_ident)
-        linked = linked & chosen(block)
-        mine = times[own + o : own + o + 1, :]
-        twice = jnp.zeros((rows, 1), jnp.int32)
-        for jc in range(CHUNKS):
-            first = times[:, jc * LANES : jc * LANES + 1]
-            last = times[:, (jc + 1) * LANES - 1 : (jc + 1) * LANES]
-            skipped = jnp.sum(jnp.where(first - mine >= 1.0, 1.0, 0.0), axis=1, keepdims=True)
-            beyond = jnp.sum(jnp.where(mine - last >= 1.0, 1.0, 0.0), axis=1, keepdims=True)
-            start = skipped.astype(jnp.int32)
-            end = STARS - beyond.astype(jnp.int32)
-            start = start - (start & 7)
-            count = jnp.where(linked & (end > start), end - start, 0)
-            whole = (count + (LONG - SHORT - 1)) // LONG
-            twice = jnp.where(whole > 1, 1, twice)
-            code = (block * CHUNKS + jc) * 2048 + (o * PADDED + start)
-            steps = (
-                jnp.where(whole > 0, code, -1),
-                jnp.where(count > whole * LONG, code + whole * LONG, -1),
-                jnp.where(whole > 1, code + LONG, -1),
-            )
-            for n, step in enumerate(steps):
-                out = jnp.where(place == COLUMNS * o + n * CHUNKS + jc, step, out)
-        flag = linked.astype(jnp.int32) + twice
-        out = jnp.where(place == COLUMNS * o + 3 * CHUNKS, flag, out)
-    table[...] = out
+        at = (own + o) * CHUNKS
+        own_ident = turned[2, at : at + 1, :]
+        own_list = jnp.where(lists == 0.0, -5.0, lists)[:, at : at + 1]
+        hit = jnp.where((lists == own_ident) | (own_list == ident), 1.0, 0.0)
+        linked = (jnp.max(hit, axis=0, keepdims=True) > 0.0) | (ident == own_ident)
+        linked = linked & chosen(entry) & (entry < entries)
+        mine = own_times(o)
+        skipped = jnp.sum(jnp.where(first - mine >= 1.0, 1.0, 0.0), axis=0, keepdims=True)
+        beyond = jnp.sum(jnp.where(mine - last >= 1.0, 1.0, 0.0), axis=0, keepdims=True)
+        start = skipped.astype(jnp.int32)
+        end = STARS - beyond.astype(jnp.int32)
+        start = start - (start & 7)
+        count = jnp.where(linked & (end > start), end - start, 0)
+        whole = (count + (LONG - SHORT - 1)) // LONG
+        code = entry * 2048 + (o * PADDED + start)
+        rows += [
+            jnp.where(whole > 0, code, -1),
+            jnp.where(count > whole * LONG, code + whole * LONG, -1),
+            jnp.where(whole > 1, code + LONG, -1),
+            jnp.where(whole > 1, 2, jnp.where(linked, 1, 0)),
+        ]
+    for n, row in enumerate(rows):
+        table[n : n + 1, :] = row
 
 
 def list_steps(table, tasks, blocks):
     def per_block(k, counts):
         for o in range(BLOCKS):
-            flag = table[k, COLUMNS * o + 3 * CHUNKS]
+            flags = [table[4 * o + 3, CHUNKS * k + jc] for jc in range(CHUNKS)]
 
             def add(counts, o=o):
                 counts = list(counts)
+                codes = [[table[4 * o + n, CHUNKS * k + jc] for jc in range(CHUNKS)] for n in range(2)]
                 for jc in range(CHUNKS):
                     for n, rows in enumerate((LONG, SHORT)):
-                        code = table[k, COLUMNS * o + n * CHUNKS + jc]
-                        tasks[FIRST[rows] + counts[n]] = code
-                        counts[n] += (code >= 0).astype(jnp.int32)
+                        tasks[FIRST[rows] + counts[n]] = codes[n][jc]
+                        counts[n] += (codes[n][jc] >= 0).astype(jnp.int32)
                 return tuple(counts)
 
             def more(counts, o=o):
                 long, short = counts
                 for jc in range(CHUNKS):
-                    code = table[k, COLUMNS * o + 2 * CHUNKS + jc]
+                    code = table[4 * o + 2, CHUNKS * k + jc]
                     tasks[FIRST[LONG] + long] = code
                     long += (code >= 0).astype(jnp.int32)
                 return long, short
 
-            counts = lax.cond(flag > 0, add, lambda counts: counts, counts)
-            counts = lax.cond(flag > 1, more, lambda counts: counts, counts)
+            counts = lax.cond(flags[0] > 0, add, lambda counts: counts, counts)
+            most = jnp.maximum(jnp.maximum(flags[0], flags[1]), jnp.maximum(flags[2], flags[3]))
+            counts = lax.cond(most > 1, more, lambda counts: counts, counts)
         return counts
 
     counts = lax.fori_loop(0, blocks, per_block, (jnp.int32(0), jnp.int32(0)))
@@ -257,10 +247,13 @@
 
         def some(i, _):
             picked = [decode(tasks[FIRST[rows] + width * i + n]) for n in range(width)]
-            for n, (at, row) in enumerate(picked):
-                eval_tile(at, row, rows, own_pos, places, tiles.at[n, 0:rows])
-            for n, (at, row) in enumerate(picked):
-                add_product(at, row, rows, tiles[n, 0:rows], weights, total)
+            for n in range(width + 1):
+                if n < width:
+                    at, row = picked[n]
+                    eval_tile(at, row, rows, own_pos, places, tiles.at[n, 0:rows])
+                if n > 0:
+                    at, row = picked[n - 1]
+                    add_product(at, row, rows, tiles[n - 1, 0:rows], weights, total)
             return 0
 
         lax.fori_loop(begin, (tasks[COUNT[rows]] + (width - 1)) // width, some, 0)
@@ -321,18 +314,18 @@
 
 
 def own_kernel(packed, own_pos, own_sum, places, own_tasks, weights, total, tiles, *scratch):
-    times, lists, idents, table, scalars, sem = scratch
-    build_table([packed], 0, lambda k: k < BLOCKS, table, times, lists, idents)
-    copy = pltpu.make_async_copy(table, scalars, sem)
-    copy.start()
+    turned, table, scalars, sem = scratch
     stage_places(packed, 0, places)
-    stage_weights(packed, 0, weights)
     for o in range(BLOCKS):
         for c in range(NOISE + 1):
             for ic in range(CHUNKS):
                 first = o * PADDED + ic * LANES
                 own_pos[c, first : first + LANES, :] = column(places[o * CHUNKS + ic, c : c + 1, :])
             own_pos[c, padding(o), :] = jnp.zeros((PADDED - STARS, LANES), F32)
+    build_table(places, BLOCKS, 0, lambda o: own_pos[2, own_rows(o), :], lambda e: e >= 0, table, turned)
+    copy = pltpu.make_async_copy(table, scalars, sem)
+    copy.start()
+    stage_weights(packed, 0, weights)
     total[...] = jnp.zeros(total.shape, F32)
     copy.wait()
     list_steps(scalars, own_tasks, BLOCKS)
@@ -342,23 +335,41 @@
 
 
 def first_kernel(
-    low, mid, high, own_pos, own_sum, image_ref, places, tasks, weights, total, tiles, *scratch
+    low_pair,
+    low,
+    mid_pair,
+    high_pair,
+    high,
+    own,
+    own_pos,
+    own_sum,
+    image_ref,
+    places,
+    tasks,
+    weights,
+    total,
+    tiles,
+    *scratch,
 ):
-    times, lists, idents, table, scalars, sem = scratch
-    groups = (low, mid, high)
-    devices = [groups[d // 3].at[d % 3] for d in range(9)]
-    build_table(devices, OWN, lambda k: (k < OWN) | (k >= OWN + BLOCKS), table, times, lists, idents)
+    turned, table, scalars, sem = scratch
+    devices = nine(low_pair, low, mid_pair, high_pair, high, own)
+    for d, device in enumerate(devices):
+        stage_places(device, d, places)
+
+    def others(entry):
+        return (entry < OWN * CHUNKS) | (entry >= (OWN + BLOCKS) * CHUNKS)
+
+    build_table(places, NEAR, OWN, lambda o: own_pos[2, own_rows(o), :], others, table, turned)
     copy = pltpu.make_async_copy(table, scalars, sem)
     copy.start()
     for d, device in enumerate(devices):
         if d != OWN // BLOCKS:
-            stage_places(device, d, places)
             stage_weights(device, d, weights)
     stage_own_sum(own_sum, total)
     copy.wait()
     list_steps(scalars, tasks, NEAR)
     run_steps(tasks, own_pos, places, weights, total, tiles)
-    image_ref[...] = image_of(total, own_pos, mid[1, 0:STARS, :])
+    image_ref[...] = image_of(total, own_pos, own[0:STARS, :])
 
 
 def between_kernel(
@@ -374,9 +385,12 @@
 
 def second_kernel(
     tasks,
+    low_pair,
     low,
-    mid,
+    mid_pair,
+    high_pair,
     high,
+    once,
     own_pos,
     own_sum,
     places,
@@ -391,14 +405,13 @@
     tiles,
     sums,
 ):
-    groups = (low, mid, high)
-    for d in range(9):
+    for d, device in enumerate(nine(low_pair, low, mid_pair, high_pair, high, once)):
         if d != OWN // BLOCKS:
-            stage_weights(groups[d // 3].at[d % 3], d, weights)
+            stage_weights(device, d, weights)
     stage_own_sum(own_sum, total)
     run_kept(tasks, {LONG: kept_long, SHORT: kept_short}, weights, total)
     run_steps(tasks, own_pos, places, weights, total, tiles, skip=KEPT)
-    start, once = packed[0:STARS, :], mid[1]
+    start, once = packed[0:STARS, :], once[...]
     twice = image_of(total, own_pos, once)
     products = (start * start, start * once, once * once, start * twice, once * twice)
     sums[...] = jnp.zeros(sums.shape, F32)
@@ -515,36 +528,33 @@
     ]
 
 
-def table_scratch(rows):
-    return [
-        pltpu.VMEM((rows, STARS), F32),
-        pltpu.VMEM((rows, LANES), F32),
-        pltpu.VMEM((rows, LANES), F32),
-        pltpu.VMEM((rows, LANES), jnp.int32),
-        pltpu.SMEM((rows, LANES), jnp.int32),
-        pltpu.SemaphoreType.DMA,
-    ]
+TABLE_SCRATCH = [
+    pltpu.VMEM((3, LANES, LANES), F32),
+    pltpu.VMEM((8, LANES), jnp.int32),
+    pltpu.SMEM((8, LANES), jnp.int32),
+    pltpu.SemaphoreType.DMA,
+]
 
 
 def apply_own(packed):
     return call(
         own_kernel,
         (OWN_POS, OWN_SUM, shape(BLOCKS * CHUNKS, META, LANES), TASKS),
-        scratch=pairs_scratch(BLOCKS) + table_scratch(8),
+        scratch=pairs_scratch(BLOCKS) + TABLE_SCRATCH,
         count=1,
         out_specs=(VMEM, VMEM, VMEM, SMEM),
         flops=1 << 30,
     )(packed)
 
 
-def apply_first(low, mid, high, own_pos, own_sum):
+def apply_first(near, own, own_pos, own_sum):
     return call(
         first_kernel,
         (shape(STARS, LANES), shape(NEAR * CHUNKS, META, LANES), TASKS),
-        scratch=pairs_scratch(NEAR) + table_scratch(24),
-        count=5,
+        scratch=pairs_scratch(NEAR) + TABLE_SCRATCH,
+        count=8,
         out_specs=(VMEM, VMEM, SMEM),
-    )(low, mid, high, own_pos, own_sum)
+    )(*near, own, own_pos, own_sum)
 
 
 def apply_between(own_tasks, tasks, once, own_pos, own_places, places):
@@ -561,13 +571,13 @@
     )(own_tasks, tasks, once, own_pos, own_places, places)
 
 
-def apply_second(tasks, low, mid, high, own_pos, own_sum, places, kept_long, kept_short, packed, rank):
+def apply_second(tasks, near, once, own_pos, own_sum, places, kept_long, kept_short, packed, rank):
     return call(
         second_kernel,
         (BLOCK, shape(8, LANES)),
         scratch=pairs_scratch(NEAR) + [pltpu.VMEM((8, LANES), F32)],
-        in_specs=[SMEM] + [VMEM] * 10,
-    )(tasks, low, mid, high, own_pos, own_sum, places, kept_long, kept_short, packed, rank)
+        in_specs=[SMEM] + [VMEM] * 13,
+    )(tasks, *near, once, own_pos, own_sum, places, kept_long, kept_short, packed, rank)
 
 
 def shift(x, axis, by):
@@ -584,9 +594,24 @@
 
 
 def with_halo(x):
-    before, after = shift(x, "tm", 1), shift(x, "tm", -1)
-    mid = jnp.stack([before, x, after])
-    return sky_shift(mid, 1), mid, sky_shift(mid, -1)
+    beside = shift(x, "tm", 1), shift(x, "tm", -1), sky_shift(x, 1), sky_shift(x, -1)
+    before, after, low, high = lax.optimization_barrier(beside)
+    mid = jnp.stack([before, after])
+    return sky_shift(mid, 1), low, mid, sky_shift(mid, -1), high
+
+
+def nine(low_pair, low, mid_pair, high_pair, high, own):
+    return [
+        low_pair.at[0],
+        low,
+        low_pair.at[1],
+        mid_pair.at[0],
+        own,
+        mid_pair.at[1],
+        high_pair.at[0],
+        high,
+        high_pair.at[1],
+    ]
 
 
 def local(star_pos, noise_var, targets, pair_list):
@@ -596,15 +621,15 @@
         (shape(ROWS, LANES), shape(BLOCKS, STARS)),
         scratch=[pltpu.VMEM((BLOCKS * WIDTH, STARS), F32), pltpu.VMEM((2 * META, STARS), F32)],
         in_specs=[SMEM, VMEM, VMEM, VMEM, VMEM],
-    )(ident.reshape(1), star_pos, noise_var, targets, pair_list)
-    low, mid, high = with_halo(packed)
+    )(ident.reshape(1), jnp.swapaxes(star_pos, 0, 1), noise_var, targets, pair_list)
+    near = with_halo(packed)
     own_pos, own_sum, own_places, own_tasks = apply_own(packed)
-    once, places, tasks = apply_first(low, mid, high, own_pos, own_sum)
-    low, mid, high = with_halo(once)
+    once, places, tasks = apply_first(near, packed, own_pos, own_sum)
+    near = with_halo(once)
     own_sum, *kept = apply_between(own_tasks, tasks, once, own_pos, own_places, places)
     once_back = call(unsort_kernel, BLOCK, count=2, flops=1 << 28)(once, rank)
     twice_back, moments = apply_second(
-        tasks, low, mid, high, own_pos, own_sum, places, *kept, packed, rank
+        tasks, near, once, own_pos, own_sum, places, *kept, packed, rank
     )
     for axis in ("core", "x", "tm", "near", "far"):
         moments = lax.psum(moments, axis)

time: 139 us -> 146 us (1.050)
  the two profiles are of different devices: /device:TPU:8 before, /device:TPU:4 now
where the time goes in v3:
time: 146 us; the launch traced here: 145 us
  blocking collectives  66.1 us (45%)
  starting transfers between devices  35.1 us (24%)
  Pallas kernels  30 us (21%)
  waiting for transfers between devices  9.98 us (7%)
  local copies, waits for them, and re-layouts  3.02 us (2%)
    psum x5, blocking collectives, local(): moments = lax.psum(moments, axis)  66.1 us
    ppermute x8, starting transfers between devices, sky_shift(): lax.ppermute(x, SKY, [(i, i + by) for i in range(count) if 0 <= i + by <...  24.4 us
    ppermute x4, starting transfers between devices, shift(): lax.ppermute(x, axis, [(i, i + by) for i in range(count) if 0 <= i + by <...  10.8 us
    pallas_call x1, Pallas kernels, apply_first(): call(first_kernel, (shape(STARS, LANES), shape(NEAR * CHUNKS, META, LANES...  9.82 us
    pallas_call x1, Pallas kernels, apply_between(): call(between_kernel, (OWN_SUM, shape(KEPT[LONG], LONG, 2 * LANES, dtype=B...  7.19 us
    ppermute x8, waiting for transfers between devices, sky_shift(): lax.ppermute(x, SKY, [(i, i + by) for i in range(count) if 0 <= i + by <...  6.5 us
    pallas_call x1, Pallas kernels, apply_own(): call(own_kernel, (OWN_POS, OWN_SUM, shape(BLOCKS * CHUNKS, META, LANES),...  5.46 us
    pallas_call x1, Pallas kernels, apply_second(): call(second_kernel, (BLOCK, shape(8, LANES)), scratch=pairs_scratch(NEAR)...  4.61 us
  transfers between devices with their start and end apart: 12, of which 6 were waited for; matrix products, arithmetic and copies ran while one was open for 0% of the time, Pallas kernels for 9%

profile of v3, /device:TPU:4, one launch (start us, length us, event | category | flops | bytes accessed | tf_op | source)
XLA Modules:
  0.0 145.2 jit_solution(6141475896243915489)
XLA Ops:
  0.6 0.0 copy-start
  0.7 0.9 copy-done
  1.6 0.0 copy-start.2
  1.6 0.7 copy-done.2
  2.3 0.0 copy-start.3
  2.3 0.7 copy-done.3
  3.0 0.0 copy-start.4
  3.0 0.7 copy-done.4
  3.7 1.3 shard_map.59
  4.9 3.5 %collective-permute-start = (f32[576,128]{1,0:T(8,128)S(1)}, f32[576,128]{1,0:T(8,128)S(1)}, u32[]{:S(2)}, u32[]{:S(2)}) collective-permute-start(f32[576,128]{1,0:T(8,128)S(1)} %get-tuple-element.24.packed.own), channel_id=1, source_target_pairs={{0,1},{1,2},{2,3},{4,5},{5,6},{6,7},{8,9},{9,10},{10,11},{12,13},{... | collective-permute-start | bytes 884744 | tf_op jit(solution)/shard_map/ppermute | solution.py:585
  8.4 1.3 collective-permute-start.1
  9.7 1.9 %collective-permute-start.2 = (f32[576,128]{1,0:T(8,128)S(1)}, f32[576,128]{1,0:T(8,128)S(1)}, u32[]{:S(2)}, u32[]{:S(2)}) collective-permute-start(f32[576,128]{1,0:T(8,128)S(1)} %get-tuple-element.24.packed.own), channel_id=1, source_target_pairs={{0,4},{4,8},{8,12},{12,16},{16,20},{20,24},{24,28},{28,32},{32,36}... | collective-permute-start | bytes 884744 | tf_op jit(solution)/shard_map/ppermute | solution.py:593
  11.7 3.6 %collective-permute-start.3 = (f32[576,128]{1,0:T(8,128)S(1)}, f32[576,128]{1,0:T(8,128)S(1)}, u32[]{:S(2)}, u32[]{:S(2)}) collective-permute-start(f32[576,128]{1,0:T(8,128)S(1)} %get-tuple-element.24.packed.own), channel_id=1, source_target_pairs={{4,0},{8,4},{12,8},{16,12},{20,16},{24,20},{28,24},{32,28},{36,32}... | collective-permute-start | bytes 884744 | tf_op jit(solution)/shard_map/ppermute | solution.py:593
  15.3 0.0 collective-permute-done
  15.3 3.5 %collective-permute-done.1 = f32[576,128]{1,0:T(8,128)S(1)} collective-permute-done((f32[576,128]{1,0:T(8,128)S(1)}, f32[576,128]{1,0:T(8,128)S(1)}, u32[]{:S(2)}, u32[]{:S(2)}) %collective-permute-start.1) | collective-permute-done | bytes 294944 | tf_op jit(solution)/shard_map/ppermute | solution.py:585
  18.8 0.0 collective-permute-done.2.low
  18.8 0.7 collective-permute-done.3.high
  19.6 3.4 %collective-permute-start.4 = (f32[2,576,128]{2,1,0:T(8,128)S(1)}, f32[2,576,128]{2,1,0:T(8,128)S(1)}, u32[]{:S(2)}, u32[]{:S(2)}) collective-permute-start(f32[2,576,128]{2,1,0:T(8,128)S(1)} %pad_maximum_fusion.mid_pair), channel_id=1, source_target_pairs={{0,4},{4,8},{8,12},{12,16},{16,20},{20,24},{24,28},{28,32},{32,36}... | collective-permute-start | bytes 1769480 | tf_op jit(solution)/shard_map/ppermute | solution.py:593
  23.0 2.4 %collective-permute-start.5 = (f32[2,576,128]{2,1,0:T(8,128)S(1)}, f32[2,576,128]{2,1,0:T(8,128)S(1)}, u32[]{:S(2)}, u32[]{:S(2)}) collective-permute-start(f32[2,576,128]{2,1,0:T(8,128)S(1)} %pad_maximum_fusion.mid_pair), channel_id=1, source_target_pairs={{4,0},{8,4},{12,8},{16,12},{20,16},{24,20},{28,24},{32,28},{36,32}... | collective-permute-start | bytes 1769480 | tf_op jit(solution)/shard_map/ppermute | solution.py:593
  25.3 5.5 %shard_map.60 = (f32[4,1536,128]{2,1,0:T(8,128)S(1)}, f32[1024,128]{1,0:T(8,128)S(1)}, f32[8,8,128]{2,1,0:T(8,128)S(1)}, s32[512]{0:T(512)S(1)}) custom-call(f32[576,128]{1,0:T(8,128)S(1)} %get-tuple-element.24.packed.own), custom_call_target="tpu_custom_call" | custom-call | flops 1073741824 | bytes 1048576 | tf_op jit(solution)/shard_map/pallas_call | solution.py:540
  30.8 0.2 collective-permute-done.4.low_pair
  31.0 1.8 %collective-permute-done.5.high_pair = f32[2,576,128]{2,1,0:T(8,128)S(1)} collective-permute-done((f32[2,576,128]{2,1,0:T(8,128)S(1)}, f32[2,576,128]{2,1,0:T(8,128)S(1)}, u32[]{:S(2)}, u32[]{:S(2)}) %collective-permute-start.5) | collective-permute-done | bytes 589856 | tf_op jit(solution)/shard_map/ppermute | solution.py:593
  32.7 9.8 %shard_map.61 = (f32[512,128]{1,0:T(8,128)S(1)}, f32[72,8,128]{2,1,0:T(8,128)S(1)}, s32[512]{0:T(512)S(1)}) custom-call(f32[2,576,128]{2,1,0:T(8,128)S(1)} %collective-permute-done.4.low_pair, f32[576,128]{1,0:T(8,128)S(1)} %collective-permute-done.2.low, f32[2,576,128]{2,1,0:T(8,128)S(1)} %pad_maximum_fusion.mid_pair, ...), custom_call_target="tpu_custom_call" | custom-call | bytes 1048576 | tf_op jit(solution)/shard_map/pallas_call | solution.py:551
  42.6 4.7 %collective-permute-start.6 = (f32[512,128]{1,0:T(8,128)S(1)}, f32[512,128]{1,0:T(8,128)S(1)}, u32[]{:S(2)}, u32[]{:S(2)}) collective-permute-start(f32[512,128]{1,0:T(8,128)S(1)} %get-tuple-element.32.once.x_ref), channel_id=1, source_target_pairs={{0,1},{1,2},{2,3},{4,5},{5,6},{6,7},{8,9},{9,10},{10,11},{12,13},{... | collective-permute-start | bytes 786440 | tf_op jit(solution)/shard_map/ppermute | solution.py:585
  47.2 1.3 collective-permute-start.7
  48.5 5.4 %collective-permute-start.8 = (f32[512,128]{1,0:T(8,128)S(1)}, f32[512,128]{1,0:T(8,128)S(1)}, u32[]{:S(2)}, u32[]{:S(2)}) collective-permute-start(f32[512,128]{1,0:T(8,128)S(1)} %get-tuple-element.32.once.x_ref), channel_id=1, source_target_pairs={{0,4},{4,8},{8,12},{12,16},{16,20},{20,24},{24,28},{28,32},{32,36}... | collective-permute-start | bytes 786440 | tf_op jit(solution)/shard_map/ppermute | solution.py:593
  54.0 1.9 %collective-permute-start.9 = (f32[512,128]{1,0:T(8,128)S(1)}, f32[512,128]{1,0:T(8,128)S(1)}, u32[]{:S(2)}, u32[]{:S(2)}) collective-permute-start(f32[512,128]{1,0:T(8,128)S(1)} %get-tuple-element.32.once.x_ref), channel_id=1, source_target_pairs={{4,0},{8,4},{12,8},{16,12},{20,16},{24,20},{28,24},{32,28},{36,32}... | collective-permute-start | bytes 786440 | tf_op jit(solution)/shard_map/ppermute | solution.py:593
  55.9 0.0 collective-permute-done.6
  55.9 0.0 collective-permute-done.7
  55.9 0.3 collective-permute-done.8.low
  56.2 3.5 %collective-permute-done.9.high = f32[512,128]{1,0:T(8,128)S(1)} collective-permute-done((f32[512,128]{1,0:T(8,128)S(1)}, f32[512,128]{1,0:T(8,128)S(1)}, u32[]{:S(2)}, u32[]{:S(2)}) %collective-permute-start.9) | collective-permute-done | bytes 262176 | tf_op jit(solution)/shard_map/ppermute | solution.py:593
  59.8 0.1 pad_maximum_fusion.1.mid_pair
  59.8 3.8 %collective-permute-start.10 = (f32[2,512,128]{2,1,0:T(8,128)S(1)}, f32[2,512,128]{2,1,0:T(8,128)S(1)}, u32[]{:S(2)}, u32[]{:S(2)}) collective-permute-start(f32[2,512,128]{2,1,0:T(8,128)S(1)} %pad_maximum_fusion.1.mid_pair), channel_id=1, source_target_pairs={{0,4},{4,8},{8,12},{12,16},{16,20},{20,24},{24,28},{28,32},{32,36}... | collective-permute-start | bytes 1572872 | tf_op jit(solution)/shard_map/ppermute | solution.py:593
  63.6 1.9 %collective-permute-start.11 = (f32[2,512,128]{2,1,0:T(8,128)S(1)}, f32[2,512,128]{2,1,0:T(8,128)S(1)}, u32[]{:S(2)}, u32[]{:S(2)}) collective-permute-start(f32[2,512,128]{2,1,0:T(8,128)S(1)} %pad_maximum_fusion.1.mid_pair), channel_id=1, source_target_pairs={{4,0},{8,4},{12,8},{16,12},{20,16},{24,20},{28,24},{32,28},{36,32}... | collective-permute-start | bytes 1572872 | tf_op jit(solution)/shard_map/ppermute | solution.py:593
  65.6 0.5 shard_map.64.once_ref
  66.1 7.2 %shard_map.62 = (f32[1024,128]{1,0:T(8,128)S(1)}, bf16[40,256,256]{2,1,0:T(8,128)(2,1)S(1)}, bf16[48,64,256]{2,1,0:T(8,128)(2,1)S(1)}) custom-call(s32[512]{0:T(512)S(1)} %get-tuple-element.37.own_tasks, s32[512]{0:T(512)S(1)} %get-tuple-element.31.tasks, f32[512,128]{1,0:T(8,128)S(1)} %get-tuple-element.32.once.x_ref, ...), custom_call_target="tpu_custom_call" | custom-call | flops 1073741824 | bytes 1048576 | tf_op jit(solution)/shard_map/pallas_call | solution.py:561
  73.2 0.0 collective-permute-done.10.low_pair
  73.3 0.0 collective-permute-done.11.high_pair
  73.3 0.0 copy-start.1
  73.3 4.6 %shard_map.63 = (f32[2,64,512]{2,1,0:T(8,128)S(1)}, f32[8,128]{1,0:T(8,128)S(1)}) custom-call(s32[512]{0:T(512)S(1)} %get-tuple-element.31.tasks, f32[2,512,128]{2,1,0:T(8,128)S(1)} %collective-permute-done.10.low_pair, f32[512,128]{1,0:T(8,128)S(1)} %collective-permute-done.8.low, f32[2,512,128]{2,1,0:T(8,128)S(1)} %pad_maximum_fusion.1.mid_pair, ...), custom_call_target="tpu_custom_call" | custom-call | bytes 1048576 | tf_op jit(solution)/shard_map/pallas_call | solution.py:575
  77.9 6.7 %psum.35 = f32[8,128]{1,0:T(8,128)S(1)} all-reduce(f32[8,128]{1,0:T(8,128)S(1)} %get-tuple-element.44), channel_id=1, replica_groups=mesh['far'=4,'near'=4,'x'=4,'core'=2,'tm'=4] {'core'}, use_global_device_ids=true, to_apply=%region_0.0 | all-reduce | flops 1024 | bytes 8192 | tf_op jit(solution)/shard_map/psum | solution.py:635
  84.6 10.2 %psum.36 = f32[8,128]{1,0:T(8,128)S(1)} all-reduce(f32[8,128]{1,0:T(8,128)S(1)} %psum.35), channel_id=1, replica_groups=mesh['far'=4,'near'=4,'x'=4,'core'=2,'tm'=4] {'x'}, use_global_device_ids=true, to_apply=%region_1.0 | all-reduce | flops 1024 | bytes 8192 | tf_op jit(solution)/shard_map/psum | solution.py:635
  94.8 11.3 %psum.37 = f32[8,128]{1,0:T(8,128)S(1)} all-reduce(f32[8,128]{1,0:T(8,128)S(1)} %psum.36), channel_id=1, replica_groups=mesh['far'=4,'near'=4,'x'=4,'core'=2,'tm'=4] {'tm'}, use_global_device_ids=true, to_apply=%region_2.0 | all-reduce | flops 1024 | bytes 8192 | tf_op jit(solution)/shard_map/psum | solution.py:635
  106.0 19.9 %psum.38 = f32[8,128]{1,0:T(8,128)S(1)} all-reduce(f32[8,128]{1,0:T(8,128)S(1)} %psum.37), channel_id=1, replica_groups=mesh['far'=4,'near'=4,'x'=4,'core'=2,'tm'=4] {'near'}, use_global_device_ids=true, to_apply=%region_3.0 | all-reduce | flops 1024 | bytes 8192 | tf_op jit(solution)/shard_map/psum | solution.py:635
  126.0 18.0 %psum.39.moments_ref = f32[8,128]{1,0:T(8,128)S(1)} all-reduce(f32[8,128]{1,0:T(8,128)S(1)} %psum.38), channel_id=1, replica_groups=mesh['far'=4,'near'=4,'x'=4,'core'=2,'tm'=4] {'far'}, use_global_device_ids=true, to_apply=%region_4.0 | all-reduce | flops 1024 | bytes 8192 | tf_op jit(solution)/shard_map/psum | solution.py:635
  144.0 0.0 copy-done.1
  144.0 1.1 shard_map.65
  (1 shorter events, 0.0 us)
Async XLA Ops:
  0.6 1.0 copy-start
  1.6 0.7 copy-start.2
  2.3 0.7 copy-start.3
  3.0 0.7 copy-start.4
  4.9 10.4 %collective-permute-start = (f32[576,128]{1,0:T(8,128)S(1)}, f32[576,128]{1,0:T(8,128)S(1)}, u32[]{:S(2)}, u32[]{:S(2)}) collective-permute-start(f32[576,128]{1,0:T(8,128)S(1)} %get-tuple-element.24.packed.own), channel_id=1, source_target_pairs={{0,1},{1,2},{2,3},{4,5},{5,6},{6,7},{8,9},{9,10},{10,11},{12,13},{... | collective-permute-start | bytes 884744 | tf_op jit(solution)/shard_map/ppermute | solution.py:585
  8.4 10.4 %collective-permute-start.1 = (f32[576,128]{1,0:T(8,128)S(1)}, f32[576,128]{1,0:T(8,128)S(1)}, u32[]{:S(2)}, u32[]{:S(2)}) collective-permute-start(f32[576,128]{1,0:T(8,128)S(1)} %get-tuple-element.24.packed.own), channel_id=1, source_target_pairs={{1,0},{2,1},{3,2},{5,4},{6,5},{7,6},{9,8},{10,9},{11,10},{13,12},{... | collective-permute-start | bytes 884744 | tf_op jit(solution)/shard_map/ppermute | solution.py:585
  9.7 9.1 %collective-permute-start.2 = (f32[576,128]{1,0:T(8,128)S(1)}, f32[576,128]{1,0:T(8,128)S(1)}, u32[]{:S(2)}, u32[]{:S(2)}) collective-permute-start(f32[576,128]{1,0:T(8,128)S(1)} %get-tuple-element.24.packed.own), channel_id=1, source_target_pairs={{0,4},{4,8},{8,12},{12,16},{16,20},{20,24},{24,28},{28,32},{32,36}... | collective-permute-start | bytes 884744 | tf_op jit(solution)/shard_map/ppermute | solution.py:593
  11.7 7.9 %collective-permute-start.3 = (f32[576,128]{1,0:T(8,128)S(1)}, f32[576,128]{1,0:T(8,128)S(1)}, u32[]{:S(2)}, u32[]{:S(2)}) collective-permute-start(f32[576,128]{1,0:T(8,128)S(1)} %get-tuple-element.24.packed.own), channel_id=1, source_target_pairs={{4,0},{8,4},{12,8},{16,12},{20,16},{24,20},{28,24},{32,28},{36,32}... | collective-permute-start | bytes 884744 | tf_op jit(solution)/shard_map/ppermute | solution.py:593
  19.6 11.4 %collective-permute-start.4 = (f32[2,576,128]{2,1,0:T(8,128)S(1)}, f32[2,576,128]{2,1,0:T(8,128)S(1)}, u32[]{:S(2)}, u32[]{:S(2)}) collective-permute-start(f32[2,576,128]{2,1,0:T(8,128)S(1)} %pad_maximum_fusion.mid_pair), channel_id=1, source_target_pairs={{0,4},{4,8},{8,12},{12,16},{16,20},{20,24},{24,28},{28,32},{32,36}... | collective-permute-start | bytes 1769480 | tf_op jit(solution)/shard_map/ppermute | solution.py:593
  23.0 9.7 %collective-permute-start.5 = (f32[2,576,128]{2,1,0:T(8,128)S(1)}, f32[2,576,128]{2,1,0:T(8,128)S(1)}, u32[]{:S(2)}, u32[]{:S(2)}) collective-permute-start(f32[2,576,128]{2,1,0:T(8,128)S(1)} %pad_maximum_fusion.mid_pair), channel_id=1, source_target_pairs={{4,0},{8,4},{12,8},{16,12},{20,16},{24,20},{28,24},{32,28},{36,32}... | collective-permute-start | bytes 1769480 | tf_op jit(solution)/shard_map/ppermute | solution.py:593
  42.6 13.3 %collective-permute-start.6 = (f32[512,128]{1,0:T(8,128)S(1)}, f32[512,128]{1,0:T(8,128)S(1)}, u32[]{:S(2)}, u32[]{:S(2)}) collective-permute-start(f32[512,128]{1,0:T(8,128)S(1)} %get-tuple-element.32.once.x_ref), channel_id=1, source_target_pairs={{0,1},{1,2},{2,3},{4,5},{5,6},{6,7},{8,9},{9,10},{10,11},{12,13},{... | collective-permute-start | bytes 786440 | tf_op jit(solution)/shard_map/ppermute | solution.py:585
  47.2 8.7 %collective-permute-start.7 = (f32[512,128]{1,0:T(8,128)S(1)}, f32[512,128]{1,0:T(8,128)S(1)}, u32[]{:S(2)}, u32[]{:S(2)}) collective-permute-start(f32[512,128]{1,0:T(8,128)S(1)} %get-tuple-element.32.once.x_ref), channel_id=1, source_target_pairs={{1,0},{2,1},{3,2},{5,4},{6,5},{7,6},{9,8},{10,9},{11,10},{13,12},{... | collective-permute-start | bytes 786440 | tf_op jit(solution)/shard_map/ppermute | solution.py:585
  48.5 7.7 %collective-permute-start.8 = (f32[512,128]{1,0:T(8,128)S(1)}, f32[512,128]{1,0:T(8,128)S(1)}, u32[]{:S(2)}, u32[]{:S(2)}) collective-permute-start(f32[512,128]{1,0:T(8,128)S(1)} %get-tuple-element.32.once.x_ref), channel_id=1, source_target_pairs={{0,4},{4,8},{8,12},{12,16},{16,20},{20,24},{24,28},{28,32},{32,36}... | collective-permute-start | bytes 786440 | tf_op jit(solution)/shard_map/ppermute | solution.py:593
  54.0 5.8 %collective-permute-start.9 = (f32[512,128]{1,0:T(8,128)S(1)}, f32[512,128]{1,0:T(8,128)S(1)}, u32[]{:S(2)}, u32[]{:S(2)}) collective-permute-start(f32[512,128]{1,0:T(8,128)S(1)} %get-tuple-element.32.once.x_ref), channel_id=1, source_target_pairs={{4,0},{8,4},{12,8},{16,12},{20,16},{24,20},{28,24},{32,28},{36,32}... | collective-permute-start | bytes 786440 | tf_op jit(solution)/shard_map/ppermute | solution.py:593
  59.8 13.4 %collective-permute-start.10 = (f32[2,512,128]{2,1,0:T(8,128)S(1)}, f32[2,512,128]{2,1,0:T(8,128)S(1)}, u32[]{:S(2)}, u32[]{:S(2)}) collective-permute-start(f32[2,512,128]{2,1,0:T(8,128)S(1)} %pad_maximum_fusion.1.mid_pair), channel_id=1, source_target_pairs={{0,4},{4,8},{8,12},{12,16},{16,20},{20,24},{24,28},{28,32},{32,36}... | collective-permute-start | bytes 1572872 | tf_op jit(solution)/shard_map/ppermute | solution.py:593
  63.6 9.6 %collective-permute-start.11 = (f32[2,512,128]{2,1,0:T(8,128)S(1)}, f32[2,512,128]{2,1,0:T(8,128)S(1)}, u32[]{:S(2)}, u32[]{:S(2)}) collective-permute-start(f32[2,512,128]{2,1,0:T(8,128)S(1)} %pad_maximum_fusion.1.mid_pair), channel_id=1, source_target_pairs={{4,0},{8,4},{12,8},{16,12},{20,16},{24,20},{28,24},{32,28},{36,32}... | collective-permute-start | bytes 1572872 | tf_op jit(solution)/shard_map/ppermute | solution.py:593
  73.3 70.8 %copy-start.1 = (f32[2,64,512]{2,1,0:T(8,128)S(1)}, f32[2,64,512]{2,1,0:T(8,128)}, u32[]{:S(2)}) copy-start(f32[2,64,512]{2,1,0:T(8,128)} %start_ref.1) | copy-start | bytes 786436

commit v4 on v3

--- a/solution.py
+++ b/solution.py
@@ -11,7 +11,8 @@
 BF16 = jnp.bfloat16
 BLOCKS, WIDTH, STARS, LANES = 2, 64, 512, 128
 CHUNKS = STARS // LANES
-NOISE, LIST, IDENT, META = 3, 4, 5, 8
+NOISE = 3
+LIST, IDENT, META = 3, 64, 4
 SLOTS = 16
 ROWS = STARS + CHUNKS * BLOCKS * META
 NEAR = 18
@@ -26,6 +27,7 @@
 LISTS = 512
 VMEM = pl.BlockSpec(memory_space=pltpu.VMEM)
 SMEM = pl.BlockSpec(memory_space=pltpu.SMEM)
+FULL = 64 * 1024 * 1024
 LIMIT = 32 * 1024 * 1024
 
 
@@ -104,12 +106,22 @@
     return slice(first, first + META)
 
 
-def sort_kernel(ident_ref, pos_ref, noise_ref, targets_ref, list_ref, packed_ref, rank_ref, tall, small):
+def sort_kernel(
+    ident_ref, pos_hbm, noise_hbm, targets_hbm, list_hbm, packed_ref, rank_ref, noise_out, tall, small, *scratch
+):
+    pos_ref, noise_ref, targets_ref, list_ref, sems = scratch
+    pairs = ((pos_hbm, pos_ref), (noise_hbm, noise_ref), (targets_hbm, targets_ref), (list_hbm, list_ref))
+    copies = [pltpu.make_async_copy(a, b, sems.at[n]) for n, (a, b) in enumerate(pairs)]
+    for copy in copies:
+        copy.start()
+    copies[0].wait()
+    for b in range(BLOCKS):
+        rank_ref[b : b + 1, :] = ranks(pos_ref[2, b : b + 1, :])
+    for copy in copies[1:]:
+        copy.wait()
     values = jnp.zeros((STARS, LANES), F32)
     for b in range(BLOCKS):
-        rank = ranks(pos_ref[2, b : b + 1, :])
-        rank_ref[b : b + 1, :] = rank
-        where_to = one_hot(rank)
+        where_to = one_hot(rank_ref[b : b + 1, :])
         tall[...] = jnp.zeros(tall.shape, F32)
         tall[b * WIDTH : (b + 1) * WIDTH, :] = targets_ref[b]
         parts = nt(where_to, jnp.concatenate(split_three(tall[...]), axis=0))
@@ -120,13 +132,15 @@
         small[NOISE : NOISE + 1, :] = noise_ref[b : b + 1, :]
         parts = nt(jnp.concatenate(split_three(small[...]), axis=0), where_to)
         height = small.shape[0]
-        meta = ((parts[:height] + parts[height : 2 * height]) + parts[2 * height :])[0:META]
+        meta = (parts[:height] + parts[height : 2 * height]) + parts[2 * height :]
         listed = list_ref[b : b + 1, :].astype(F32) + 1.0
+        ident = jnp.full((1, LANES), (ident_ref[0] + b + 1).astype(F32))
+        ident = jnp.where(iota((1, LANES), 1) < IDENT, 0.0, ident)
         for jc in range(CHUNKS):
-            packed_ref[meta_rows(b, jc), :] = meta[:, lanes(jc)]
-            first = STARS + (jc * BLOCKS + b) * META
-            ident = jnp.full((1, LANES), (ident_ref[0] + b + 1).astype(F32))
-            packed_ref[first + IDENT : first + IDENT + 1, :] = ident
+            first = meta_rows(b, jc).start
+            packed_ref[first : first + 3, :] = meta[0:3, lanes(jc)]
+            noise_out[b * CHUNKS + jc : b * CHUNKS + jc + 1, :] = meta[NOISE : NOISE + 1, lanes(jc)]
+            packed_ref[first + LIST : first + LIST + 1, :] = ident
             packed_ref[first + LIST : first + LIST + 1, 0 : listed.shape[1]] = listed
     packed_ref[0:STARS, :] = values
 
@@ -135,18 +149,18 @@
     entries = blocks * CHUNKS
     turned[...] = jnp.zeros(turned.shape, F32)
     flipped = []
-    for n, row in enumerate((2, LIST, IDENT)):
+    for n, row in enumerate((2, LIST)):
         for at in range(entries):
             turned[n, at : at + 1, :] = places[at, row : row + 1, :]
         flipped.append(jnp.transpose(turned[n]))
-    times, lists, idents = flipped
+    times, lists = flipped
     first, last = times[0:1, :], times[LANES - 1 : LANES, :]
-    lists, ident = lists[0:SLOTS, :], idents[0:1, :]
+    lists, ident = lists[0:SLOTS, :], lists[IDENT : IDENT + 1, :]
     entry = iota((1, LANES), 1)
     rows = []
     for o in range(BLOCKS):
         at = (own + o) * CHUNKS
-        own_ident = turned[2, at : at + 1, :]
+        own_ident = turned[1, at : at + 1, IDENT : IDENT + 1]
         own_list = jnp.where(lists == 0.0, -5.0, lists)[:, at : at + 1]
         hit = jnp.where((lists == own_ident) | (own_list == ident), 1.0, 0.0)
         linked = (jnp.max(hit, axis=0, keepdims=True) > 0.0) | (ident == own_ident)
@@ -310,17 +324,19 @@
 def stage_places(device, d, places):
     for b in range(BLOCKS):
         for jc in range(CHUNKS):
-            places[(BLOCKS * d + b) * CHUNKS + jc] = device[meta_rows(b, jc), :]
-
-
-def own_kernel(packed, own_pos, own_sum, places, own_tasks, weights, total, tiles, *scratch):
+            places[(BLOCKS * d + b) * CHUNKS + jc, 0:META, :] = device[meta_rows(b, jc), :]
+
+
+def own_kernel(packed, noise, own_pos, own_sum, places, own_tasks, weights, total, tiles, *scratch):
     turned, table, scalars, sem = scratch
     stage_places(packed, 0, places)
     for o in range(BLOCKS):
         for c in range(NOISE + 1):
             for ic in range(CHUNKS):
                 first = o * PADDED + ic * LANES
-                own_pos[c, first : first + LANES, :] = column(places[o * CHUNKS + ic, c : c + 1, :])
+                at = o * CHUNKS + ic
+                row = noise[at : at + 1, :] if c == NOISE else places[at, c : c + 1, :]
+                own_pos[c, first : first + LANES, :] = column(row)
             own_pos[c, padding(o), :] = jnp.zeros((PADDED - STARS, LANES), F32)
     build_table(places, BLOCKS, 0, lambda o: own_pos[2, own_rows(o), :], lambda e: e >= 0, table, turned)
     copy = pltpu.make_async_copy(table, scalars, sem)
@@ -335,24 +351,11 @@
 
 
 def first_kernel(
-    low_pair,
-    low,
-    mid_pair,
-    high_pair,
-    high,
-    own,
-    own_pos,
-    own_sum,
-    image_ref,
-    places,
-    tasks,
-    weights,
-    total,
-    tiles,
-    *scratch,
+    low, mid, high, own_pos, own_sum, image_ref, places, tasks, weights, total, tiles, *scratch
 ):
     turned, table, scalars, sem = scratch
-    devices = nine(low_pair, low, mid_pair, high_pair, high, own)
+    groups = (low, mid, high)
+    devices = [groups[d // 3].at[d % 3] for d in range(9)]
     for d, device in enumerate(devices):
         stage_places(device, d, places)
 
@@ -369,7 +372,7 @@
     copy.wait()
     list_steps(scalars, tasks, NEAR)
     run_steps(tasks, own_pos, places, weights, total, tiles)
-    image_ref[...] = image_of(total, own_pos, own[0:STARS, :])
+    image_ref[...] = image_of(total, own_pos, mid[1, 0:STARS, :])
 
 
 def between_kernel(
@@ -385,12 +388,9 @@
 
 def second_kernel(
     tasks,
-    low_pair,
     low,
-    mid_pair,
-    high_pair,
+    mid,
     high,
-    once,
     own_pos,
     own_sum,
     places,
@@ -405,13 +405,14 @@
     tiles,
     sums,
 ):
-    for d, device in enumerate(nine(low_pair, low, mid_pair, high_pair, high, once)):
+    groups = (low, mid, high)
+    for d in range(9):
         if d != OWN // BLOCKS:
-            stage_weights(device, d, weights)
+            stage_weights(groups[d // 3].at[d % 3], d, weights)
     stage_own_sum(own_sum, total)
     run_kept(tasks, {LONG: kept_long, SHORT: kept_short}, weights, total)
     run_steps(tasks, own_pos, places, weights, total, tiles, skip=KEPT)
-    start, once = packed[0:STARS, :], once[...]
+    start, once = packed[0:STARS, :], mid[1]
     twice = image_of(total, own_pos, once)
     products = (start * start, start * once, once * once, start * twice, once * twice)
     sums[...] = jnp.zeros(sums.shape, F32)
@@ -502,14 +503,14 @@
     return jax.ShapeDtypeStruct(dims, dtype)
 
 
-def call(kernel, out_shape, scratch=(), in_specs=None, count=None, out_specs=None, flops=0, nbytes=1 << 20):
+def call(kernel, out_shape, scratch=(), in_specs=None, count=None, out_specs=None, limit=LIMIT, flops=0, nbytes=1 << 20):
     return pl.pallas_call(
         kernel,
         out_shape=out_shape,
         in_specs=in_specs if in_specs is not None else [VMEM] * count,
         out_specs=out_specs or jax.tree.map(lambda _: VMEM, out_shape),
         scratch_shapes=list(scratch),
-        compiler_params=pltpu.CompilerParams(vmem_limit_bytes=LIMIT),
+        compiler_params=pltpu.CompilerParams(vmem_limit_bytes=limit),
         cost_estimate=pl.CostEstimate(flops=flops, bytes_accessed=nbytes, transcendentals=0),
     )
 
@@ -529,32 +530,32 @@
 
 
 TABLE_SCRATCH = [
-    pltpu.VMEM((3, LANES, LANES), F32),
+    pltpu.VMEM((2, LANES, LANES), F32),
     pltpu.VMEM((8, LANES), jnp.int32),
     pltpu.SMEM((8, LANES), jnp.int32),
     pltpu.SemaphoreType.DMA,
 ]
 
 
-def apply_own(packed):
+def apply_own(packed, noise):
     return call(
         own_kernel,
-        (OWN_POS, OWN_SUM, shape(BLOCKS * CHUNKS, META, LANES), TASKS),
+        (OWN_POS, OWN_SUM, shape(BLOCKS * CHUNKS, 8, LANES), TASKS),
         scratch=pairs_scratch(BLOCKS) + TABLE_SCRATCH,
-        count=1,
+        count=2,
         out_specs=(VMEM, VMEM, VMEM, SMEM),
         flops=1 << 30,
-    )(packed)
-
-
-def apply_first(near, own, own_pos, own_sum):
+    )(packed, noise)
+
+
+def apply_first(low, mid, high, own_pos, own_sum):
     return call(
         first_kernel,
-        (shape(STARS, LANES), shape(NEAR * CHUNKS, META, LANES), TASKS),
+        (shape(STARS, LANES), shape(NEAR * CHUNKS, 8, LANES), TASKS),
         scratch=pairs_scratch(NEAR) + TABLE_SCRATCH,
-        count=8,
+        count=5,
         out_specs=(VMEM, VMEM, SMEM),
-    )(*near, own, own_pos, own_sum)
+    )(low, mid, high, own_pos, own_sum)
 
 
 def apply_between(own_tasks, tasks, once, own_pos, own_places, places):
@@ -571,13 +572,13 @@
     )(own_tasks, tasks, once, own_pos, own_places, places)
 
 
-def apply_second(tasks, near, once, own_pos, own_sum, places, kept_long, kept_short, packed, rank):
+def apply_second(tasks, low, mid, high, own_pos, own_sum, places, kept_long, kept_short, packed, rank):
     return call(
         second_kernel,
         (BLOCK, shape(8, LANES)),
         scratch=pairs_scratch(NEAR) + [pltpu.VMEM((8, LANES), F32)],
-        in_specs=[SMEM] + [VMEM] * 13,
-    )(tasks, *near, once, own_pos, own_sum, places, kept_long, kept_short, packed, rank)
+        in_specs=[SMEM] + [VMEM] * 10,
+    )(tasks, low, mid, high, own_pos, own_sum, places, kept_long, kept_short, packed, rank)
 
 
 def shift(x, axis, by):
@@ -594,42 +595,38 @@
 
 
 def with_halo(x):
-    beside = shift(x, "tm", 1), shift(x, "tm", -1), sky_shift(x, 1), sky_shift(x, -1)
-    before, after, low, high = lax.optimization_barrier(beside)
-    mid = jnp.stack([before, after])
-    return sky_shift(mid, 1), low, mid, sky_shift(mid, -1), high
-
-
-def nine(low_pair, low, mid_pair, high_pair, high, own):
-    return [
-        low_pair.at[0],
-        low,
-        low_pair.at[1],
-        mid_pair.at[0],
-        own,
-        mid_pair.at[1],
-        high_pair.at[0],
-        high,
-        high_pair.at[1],
-    ]
+    before, after = shift(x, "tm", 1), shift(x, "tm", -1)
+    mid = jnp.stack([before, x, after])
+    return sky_shift(mid, 1), mid, sky_shift(mid, -1)
 
 
 def local(star_pos, noise_var, targets, pair_list):
     ident = (lax.axis_index(SKY) * lax.axis_size("tm") + lax.axis_index("tm")) * BLOCKS
-    packed, rank = call(
+    hbm = pl.BlockSpec(memory_space=pltpu.HBM)
+    stars = (BLOCKS, STARS)
+    packed, rank, noise = call(
         sort_kernel,
-        (shape(ROWS, LANES), shape(BLOCKS, STARS)),
-        scratch=[pltpu.VMEM((BLOCKS * WIDTH, STARS), F32), pltpu.VMEM((2 * META, STARS), F32)],
-        in_specs=[SMEM, VMEM, VMEM, VMEM, VMEM],
+        (shape(ROWS, LANES), shape(*stars), shape(BLOCKS * CHUNKS, LANES)),
+        scratch=[
+            pltpu.VMEM((BLOCKS * WIDTH, STARS), F32),
+            pltpu.VMEM((16, STARS), F32),
+            pltpu.VMEM((3,) + stars, F32),
+            pltpu.VMEM(stars, F32),
+            pltpu.VMEM((BLOCKS, WIDTH, STARS), F32),
+            pltpu.VMEM(pair_list.shape, jnp.int32),
+            pltpu.SemaphoreType.DMA((4,)),
+        ],
+        in_specs=[SMEM] + [hbm] * 4,
+        limit=FULL - 512 * 1024,
     )(ident.reshape(1), jnp.swapaxes(star_pos, 0, 1), noise_var, targets, pair_list)
-    near = with_halo(packed)
-    own_pos, own_sum, own_places, own_tasks = apply_own(packed)
-    once, places, tasks = apply_first(near, packed, own_pos, own_sum)
-    near = with_halo(once)
+    low, mid, high = with_halo(packed)
+    own_pos, own_sum, own_places, own_tasks = apply_own(packed, noise)
+    once, places, tasks = apply_first(low, mid, high, own_pos, own_sum)
+    low, mid, high = with_halo(once)
     own_sum, *kept = apply_between(own_tasks, tasks, once, own_pos, own_places, places)
     once_back = call(unsort_kernel, BLOCK, count=2, flops=1 << 28)(once, rank)
     twice_back, moments = apply_second(
-        tasks, near, once, own_pos, own_sum, places, *kept, packed, rank
+        tasks, low, mid, high, own_pos, own_sum, places, *kept, packed, rank
     )
     for axis in ("core", "x", "tm", "near", "far"):
         moments = lax.psum(moments, axis)

time: 146 us -> 138 us (0.945)
  the two profiles are of different devices: /device:TPU:4 before, /device:TPU:8 now
where the time goes in v4:
time: 138 us; the launch traced here: 137 us
  blocking collectives  66.2 us (48%)
  starting transfers between devices  30.1 us (22%)
  Pallas kernels  25.5 us (18%)
  waiting for transfers between devices  12 us (9%)
  local copies, waits for them, and re-layouts  1.65 us (1%)
    psum x5, blocking collectives, local(): moments = lax.psum(moments, axis)  66.2 us
    ppermute x4, starting transfers between devices, sky_shift(): lax.ppermute(x, SKY, [(i, i + by) for i in range(count) if 0 <= i + by <...  15.2 us
    ppermute x4, starting transfers between devices, shift(): lax.ppermute(x, axis, [(i, i + by) for i in range(count) if 0 <= i + by <...  14.9 us
    ppermute x4, waiting for transfers between devices, shift(): lax.ppermute(x, axis, [(i, i + by) for i in range(count) if 0 <= i + by <...  9.59 us
    pallas_call x1, Pallas kernels, apply_first(): call(first_kernel, (shape(STARS, LANES), shape(NEAR * CHUNKS, 8, LANES),...  6.92 us
    pallas_call x1, Pallas kernels, apply_own(): call(own_kernel, (OWN_POS, OWN_SUM, shape(BLOCKS * CHUNKS, 8, LANES), TAS...  5.45 us
    pallas_call x1, Pallas kernels, apply_between(): call(between_kernel, (OWN_SUM, shape(KEPT[LONG], LONG, 2 * LANES, dtype=B...  5.4 us
    pallas_call x1, Pallas kernels, apply_second(): call(second_kernel, (BLOCK, shape(8, LANES)), scratch=pairs_scratch(NEAR)...  3.33 us
  transfers between devices with their start and end apart: 8, of which 5 were waited for; matrix products, arithmetic and copies ran while one was open for 0% of the time, Pallas kernels for 8%

profile of v4, /device:TPU:8, one launch (start us, length us, event | category | flops | bytes accessed | tf_op | source)
XLA Modules:
  0.0 137.2 jit_solution(8286236591570653956)
XLA Ops:
  0.6 2.8 %shard_map.59 = (f32[544,128]{1,0:T(8,128)}, f32[2,512]{1,0:T(2,128)}, f32[8,128]{1,0:T(8,128)}) custom-call(s32[1]{0:T(128)} %bitcast.ident_ref, f32[3,2,512]{2,1,0:T(2,128)} %bitcast.14, f32[2,512]{1,0:T(2,128)} %noise_hbm.1, f32[2,64,512]{2,1,0:T(8,128)} %start_ref.1, s32[2,14]{1,0:T(2,128)} %list_hbm.1), custom_call_target="tpu_custom_call" | custom-call | bytes 1048576 | tf_op jit(solution)/shard_map/pallas_call | solution.py:607
  3.4 3.5 %collective-permute-start = (f32[544,128]{1,0:T(8,128)}, f32[544,128]{1,0:T(8,128)S(1)}, u32[]{:S(2)}, u32[]{:S(2)}) collective-permute-start(f32[544,128]{1,0:T(8,128)} %get-tuple-element.17.packed), channel_id=1, source_target_pairs={{0,1},{1,2},{2,3},{4,5},{5,6},{6,7},{8,9},{9,10},{10,11},{12,13},{... | collective-permute-start | bytes 835592 | tf_op jit(solution)/shard_map/ppermute | solution.py:586
  6.9 5.6 %collective-permute-start.1 = (f32[544,128]{1,0:T(8,128)}, f32[544,128]{1,0:T(8,128)S(1)}, u32[]{:S(2)}, u32[]{:S(2)}) collective-permute-start(f32[544,128]{1,0:T(8,128)} %get-tuple-element.17.packed), channel_id=1, source_target_pairs={{1,0},{2,1},{3,2},{5,4},{6,5},{7,6},{9,8},{10,9},{11,10},{13,12},{... | collective-permute-start | bytes 835592 | tf_op jit(solution)/shard_map/ppermute | solution.py:586
  12.5 2.8 %collective-permute-done = f32[544,128]{1,0:T(8,128)S(1)} collective-permute-done((f32[544,128]{1,0:T(8,128)}, f32[544,128]{1,0:T(8,128)S(1)}, u32[]{:S(2)}, u32[]{:S(2)}) %collective-permute-start) | collective-permute-done | bytes 278560 | tf_op jit(solution)/shard_map/ppermute | solution.py:586
  15.3 1.9 %collective-permute-done.1 = f32[544,128]{1,0:T(8,128)S(1)} collective-permute-done((f32[544,128]{1,0:T(8,128)}, f32[544,128]{1,0:T(8,128)S(1)}, u32[]{:S(2)}, u32[]{:S(2)}) %collective-permute-start.1) | collective-permute-done | bytes 278560 | tf_op jit(solution)/shard_map/ppermute | solution.py:586
  17.1 1.0 pad_maximum_fusion.mid
  18.1 1.3 collective-permute-start.2
  19.5 1.3 collective-permute-start.3
  20.8 0.0 copy-start
  20.8 0.9 copy-done
  21.8 0.0 copy-start.4
  21.8 0.7 copy-done.4
  22.4 5.5 %shard_map.60 = (f32[4,1536,128]{2,1,0:T(8,128)S(1)}, f32[1024,128]{1,0:T(8,128)S(1)}, f32[8,8,128]{2,1,0:T(8,128)S(1)}, s32[512]{0:T(512)S(1)}) custom-call(f32[544,128]{1,0:T(8,128)S(1)} %copy-done, f32[8,128]{1,0:T(8,128)S(1)} %copy-done.4), custom_call_target="tpu_custom_call" | custom-call | flops 1073741824 | bytes 1048576 | tf_op jit(solution)/shard_map/pallas_call | solution.py:541
  27.9 0.0 collective-permute-done.2.low
  27.9 0.0 collective-permute-done.3.high
  27.9 0.0 copy-start.3
  27.9 6.9 %shard_map.61 = (f32[512,128]{1,0:T(8,128)S(1)}, f32[72,8,128]{2,1,0:T(8,128)S(1)}, s32[512]{0:T(512)S(1)}) custom-call(f32[3,544,128]{2,1,0:T(8,128)S(1)} %collective-permute-done.2.low, f32[3,544,128]{2,1,0:T(8,128)S(1)} %pad_maximum_fusion.mid, f32[3,544,128]{2,1,0:T(8,128)S(1)} %collective-permute-done.3.high, ...), custom_call_target="tpu_custom_call" | custom-call | bytes 1048576 | tf_op jit(solution)/shard_map/pallas_call | solution.py:552
  34.9 2.5 %collective-permute-start.4 = (f32[512,128]{1,0:T(8,128)S(1)}, f32[512,128]{1,0:T(8,128)S(1)}, u32[]{:S(2)}, u32[]{:S(2)}) collective-permute-start(f32[512,128]{1,0:T(8,128)S(1)} %get-tuple-element.22.once.x_ref), channel_id=1, source_target_pairs={{0,1},{1,2},{2,3},{4,5},{5,6},{6,7},{8,9},{9,10},{10,11},{12,13},{... | collective-permute-start | bytes 786440 | tf_op jit(solution)/shard_map/ppermute | solution.py:586
  37.4 3.3 %collective-permute-start.5 = (f32[512,128]{1,0:T(8,128)S(1)}, f32[512,128]{1,0:T(8,128)S(1)}, u32[]{:S(2)}, u32[]{:S(2)}) collective-permute-start(f32[512,128]{1,0:T(8,128)S(1)} %get-tuple-element.22.once.x_ref), channel_id=1, source_target_pairs={{1,0},{2,1},{3,2},{5,4},{6,5},{7,6},{9,8},{10,9},{11,10},{13,12},{... | collective-permute-start | bytes 786440 | tf_op jit(solution)/shard_map/ppermute | solution.py:586
  40.7 2.4 %collective-permute-done.4 = f32[512,128]{1,0:T(8,128)S(1)} collective-permute-done((f32[512,128]{1,0:T(8,128)S(1)}, f32[512,128]{1,0:T(8,128)S(1)}, u32[]{:S(2)}, u32[]{:S(2)}) %collective-permute-start.4) | collective-permute-done | bytes 262176 | tf_op jit(solution)/shard_map/ppermute | solution.py:586
  43.1 2.5 %collective-permute-done.5 = f32[512,128]{1,0:T(8,128)S(1)} collective-permute-done((f32[512,128]{1,0:T(8,128)S(1)}, f32[512,128]{1,0:T(8,128)S(1)}, u32[]{:S(2)}, u32[]{:S(2)}) %collective-permute-start.5) | collective-permute-done | bytes 262176 | tf_op jit(solution)/shard_map/ppermute | solution.py:586
  45.7 0.0 copy-start.1
  45.7 0.1 pad_maximum_fusion.1.mid
  45.7 11.3 %collective-permute-start.6 = (f32[3,512,128]{2,1,0:T(8,128)S(1)}, f32[3,512,128]{2,1,0:T(8,128)S(1)}, u32[]{:S(2)}, u32[]{:S(2)}) collective-permute-start(f32[3,512,128]{2,1,0:T(8,128)S(1)} %pad_maximum_fusion.1.mid), channel_id=1, source_target_pairs={{0,4},{4,8},{8,12},{12,16},{16,20},{20,24},{24,28},{28,32},{32,36}... | collective-permute-start | bytes 2359304 | tf_op jit(solution)/shard_map/ppermute | solution.py:594
  57.0 1.3 collective-permute-start.7
  58.3 0.0 copy-done.3
  58.3 0.5 shard_map.64.once_ref
  58.8 5.4 %shard_map.62 = (f32[1024,128]{1,0:T(8,128)S(1)}, bf16[40,256,256]{2,1,0:T(8,128)(2,1)S(1)}, bf16[48,64,256]{2,1,0:T(8,128)(2,1)S(1)}) custom-call(s32[512]{0:T(512)S(1)} %get-tuple-element.23.own_tasks, s32[512]{0:T(512)S(1)} %get-tuple-element.21.tasks, f32[512,128]{1,0:T(8,128)S(1)} %get-tuple-element.22.once.x_ref, ...), custom_call_target="tpu_custom_call" | custom-call | flops 1073741824 | bytes 1048576 | tf_op jit(solution)/shard_map/pallas_call | solution.py:562
  64.2 0.0 collective-permute-done.6.low
  64.2 2.4 %collective-permute-done.7.high = f32[3,512,128]{2,1,0:T(8,128)S(1)} collective-permute-done((f32[3,512,128]{2,1,0:T(8,128)S(1)}, f32[3,512,128]{2,1,0:T(8,128)S(1)}, u32[]{:S(2)}, u32[]{:S(2)}) %collective-permute-start.7) | collective-permute-done | bytes 786464 | tf_op jit(solution)/shard_map/ppermute | solution.py:594
  66.6 0.0 copy-done.1
  66.6 0.0 copy-start.2
  66.6 3.3 %shard_map.63 = (f32[2,64,512]{2,1,0:T(8,128)S(1)}, f32[8,128]{1,0:T(8,128)S(1)}) custom-call(s32[512]{0:T(512)S(1)} %get-tuple-element.21.tasks, f32[3,512,128]{2,1,0:T(8,128)S(1)} %collective-permute-done.6.low, f32[3,512,128]{2,1,0:T(8,128)S(1)} %pad_maximum_fusion.1.mid, f32[3,512,128]{2,1,0:T(8,128)S(1)} %collective-permute-done.7.high, ...), custom_call_target="tpu_custom_call" | custom-call | bytes 1048576 | tf_op jit(solution)/shard_map/pallas_call | solution.py:576
  69.9 12.7 %psum.35 = f32[8,128]{1,0:T(8,128)S(1)} all-reduce(f32[8,128]{1,0:T(8,128)S(1)} %get-tuple-element.30), channel_id=1, replica_groups=mesh['far'=4,'near'=4,'x'=4,'core'=2,'tm'=4] {'core'}, use_global_device_ids=true, to_apply=%region_0.0 | all-reduce | flops 1024 | bytes 8192 | tf_op jit(solution)/shard_map/psum | solution.py:632
  82.6 13.0 %psum.36 = f32[8,128]{1,0:T(8,128)S(1)} all-reduce(f32[8,128]{1,0:T(8,128)S(1)} %psum.35), channel_id=1, replica_groups=mesh['far'=4,'near'=4,'x'=4,'core'=2,'tm'=4] {'x'}, use_global_device_ids=true, to_apply=%region_1.0 | all-reduce | flops 1024 | bytes 8192 | tf_op jit(solution)/shard_map/psum | solution.py:632
  95.6 7.1 %psum.37 = f32[8,128]{1,0:T(8,128)S(1)} all-reduce(f32[8,128]{1,0:T(8,128)S(1)} %psum.36), channel_id=1, replica_groups=mesh['far'=4,'near'=4,'x'=4,'core'=2,'tm'=4] {'tm'}, use_global_device_ids=true, to_apply=%region_2.0 | all-reduce | flops 1024 | bytes 8192 | tf_op jit(solution)/shard_map/psum | solution.py:632
  102.7 15.6 %psum.38 = f32[8,128]{1,0:T(8,128)S(1)} all-reduce(f32[8,128]{1,0:T(8,128)S(1)} %psum.37), channel_id=1, replica_groups=mesh['far'=4,'near'=4,'x'=4,'core'=2,'tm'=4] {'near'}, use_global_device_ids=true, to_apply=%region_3.0 | all-reduce | flops 1024 | bytes 8192 | tf_op jit(solution)/shard_map/psum | solution.py:632
  118.4 17.7 %psum.39.moments_ref = f32[8,128]{1,0:T(8,128)S(1)} all-reduce(f32[8,128]{1,0:T(8,128)S(1)} %psum.38), channel_id=1, replica_groups=mesh['far'=4,'near'=4,'x'=4,'core'=2,'tm'=4] {'far'}, use_global_device_ids=true, to_apply=%region_4.0 | all-reduce | flops 1024 | bytes 8192 | tf_op jit(solution)/shard_map/psum | solution.py:632
  136.1 0.0 copy-done.2
  136.1 1.1 shard_map.65
Async XLA Ops:
  3.4 11.8 %collective-permute-start = (f32[544,128]{1,0:T(8,128)}, f32[544,128]{1,0:T(8,128)S(1)}, u32[]{:S(2)}, u32[]{:S(2)}) collective-permute-start(f32[544,128]{1,0:T(8,128)} %get-tuple-element.17.packed), channel_id=1, source_target_pairs={{0,1},{1,2},{2,3},{4,5},{5,6},{6,7},{8,9},{9,10},{10,11},{12,13},{... | collective-permute-start | bytes 835592 | tf_op jit(solution)/shard_map/ppermute | solution.py:586
  6.9 10.2 %collective-permute-start.1 = (f32[544,128]{1,0:T(8,128)}, f32[544,128]{1,0:T(8,128)S(1)}, u32[]{:S(2)}, u32[]{:S(2)}) collective-permute-start(f32[544,128]{1,0:T(8,128)} %get-tuple-element.17.packed), channel_id=1, source_target_pairs={{1,0},{2,1},{3,2},{5,4},{6,5},{7,6},{9,8},{10,9},{11,10},{13,12},{... | collective-permute-start | bytes 835592 | tf_op jit(solution)/shard_map/ppermute | solution.py:586
  18.1 9.8 %collective-permute-start.2 = (f32[3,544,128]{2,1,0:T(8,128)S(1)}, f32[3,544,128]{2,1,0:T(8,128)S(1)}, u32[]{:S(2)}, u32[]{:S(2)}) collective-permute-start(f32[3,544,128]{2,1,0:T(8,128)S(1)} %pad_maximum_fusion.mid), channel_id=1, source_target_pairs={{0,4},{4,8},{8,12},{12,16},{16,20},{20,24},{24,28},{28,32},{32,36}... | collective-permute-start | bytes 2506760 | tf_op jit(solution)/shard_map/ppermute | solution.py:594
  19.5 8.4 %collective-permute-start.3 = (f32[3,544,128]{2,1,0:T(8,128)S(1)}, f32[3,544,128]{2,1,0:T(8,128)S(1)}, u32[]{:S(2)}, u32[]{:S(2)}) collective-permute-start(f32[3,544,128]{2,1,0:T(8,128)S(1)} %pad_maximum_fusion.mid), channel_id=1, source_target_pairs={{4,0},{8,4},{12,8},{16,12},{20,16},{24,20},{28,24},{32,28},{36,32}... | collective-permute-start | bytes 2506760 | tf_op jit(solution)/shard_map/ppermute | solution.py:594
  20.8 1.0 copy-start
  21.8 0.7 copy-start.4
  27.9 30.4 %copy-start.3 = (f32[2,512]{1,0:T(2,128)S(1)}, f32[2,512]{1,0:T(2,128)}, u32[]{:S(2)}) copy-start(f32[2,512]{1,0:T(2,128)} %get-tuple-element.29.rank.rank_ref) | copy-start | bytes 12292
  34.9 8.3 %collective-permute-start.4 = (f32[512,128]{1,0:T(8,128)S(1)}, f32[512,128]{1,0:T(8,128)S(1)}, u32[]{:S(2)}, u32[]{:S(2)}) collective-permute-start(f32[512,128]{1,0:T(8,128)S(1)} %get-tuple-element.22.once.x_ref), channel_id=1, source_target_pairs={{0,1},{1,2},{2,3},{4,5},{5,6},{6,7},{8,9},{9,10},{10,11},{12,13},{... | collective-permute-start | bytes 786440 | tf_op jit(solution)/shard_map/ppermute | solution.py:586
  37.4 8.3 %collective-permute-start.5 = (f32[512,128]{1,0:T(8,128)S(1)}, f32[512,128]{1,0:T(8,128)S(1)}, u32[]{:S(2)}, u32[]{:S(2)}) collective-permute-start(f32[512,128]{1,0:T(8,128)S(1)} %get-tuple-element.22.once.x_ref), channel_id=1, source_target_pairs={{1,0},{2,1},{3,2},{5,4},{6,5},{7,6},{9,8},{10,9},{11,10},{13,12},{... | collective-permute-start | bytes 786440 | tf_op jit(solution)/shard_map/ppermute | solution.py:586
  45.7 20.9 %copy-start.1 = (f32[544,128]{1,0:T(8,128)S(1)}, f32[544,128]{1,0:T(8,128)}, u32[]{:S(2)}) copy-start(f32[544,128]{1,0:T(8,128)} %get-tuple-element.17.packed) | copy-start | bytes 835588
  45.7 18.5 %collective-permute-start.6 = (f32[3,512,128]{2,1,0:T(8,128)S(1)}, f32[3,512,128]{2,1,0:T(8,128)S(1)}, u32[]{:S(2)}, u32[]{:S(2)}) collective-permute-start(f32[3,512,128]{2,1,0:T(8,128)S(1)} %pad_maximum_fusion.1.mid), channel_id=1, source_target_pairs={{0,4},{4,8},{8,12},{12,16},{16,20},{20,24},{24,28},{28,32},{32,36}... | collective-permute-start | bytes 2359304 | tf_op jit(solution)/shard_map/ppermute | solution.py:594
  57.0 9.6 %collective-permute-start.7 = (f32[3,512,128]{2,1,0:T(8,128)S(1)}, f32[3,512,128]{2,1,0:T(8,128)S(1)}, u32[]{:S(2)}, u32[]{:S(2)}) collective-permute-start(f32[3,512,128]{2,1,0:T(8,128)S(1)} %pad_maximum_fusion.1.mid), channel_id=1, source_target_pairs={{4,0},{8,4},{12,8},{16,12},{20,16},{24,20},{28,24},{32,28},{36,32}... | collective-permute-start | bytes 2359304 | tf_op jit(solution)/shard_map/ppermute | solution.py:594
  66.6 69.5 %copy-start.2 = (f32[2,64,512]{2,1,0:T(8,128)S(1)}, f32[2,64,512]{2,1,0:T(8,128)}, u32[]{:S(2)}) copy-start(f32[2,64,512]{2,1,0:T(8,128)} %start_ref.1) | copy-start | bytes 786436

commit v5 on v4

--- a/solution.py
+++ b/solution.py
@@ -22,9 +22,9 @@
 KEPT = {LONG: 40, SHORT: 48}
 PADDED = STARS + LONG
 NOTHING = STARS
-FIRST = {LONG: 8, SHORT: 320}
 COUNT = {LONG: 0, SHORT: 1}
-LISTS = 512
+FIRST = {LONG: 1, SHORT: 4}
+LIST_ROWS = {LONG: 3, SHORT: 2}
 VMEM = pl.BlockSpec(memory_space=pltpu.VMEM)
 SMEM = pl.BlockSpec(memory_space=pltpu.SMEM)
 FULL = 64 * 1024 * 1024
@@ -145,7 +145,7 @@
     packed_ref[0:STARS, :] = values
 
 
-def build_table(places, blocks, own, own_times, chosen, table, turned):
+def build_lists(places, blocks, own, own_times, chosen, lists_out, turned):
     entries = blocks * CHUNKS
     turned[...] = jnp.zeros(turned.shape, F32)
     flipped = []
@@ -157,7 +157,7 @@
     first, last = times[0:1, :], times[LANES - 1 : LANES, :]
     lists, ident = lists[0:SLOTS, :], lists[IDENT : IDENT + 1, :]
     entry = iota((1, LANES), 1)
-    rows = []
+    rows = {LONG: [], SHORT: []}
     for o in range(BLOCKS):
         at = (own + o) * CHUNKS
         own_ident = turned[1, at : at + 1, IDENT : IDENT + 1]
@@ -174,48 +174,42 @@
         count = jnp.where(linked & (end > start), end - start, 0)
         whole = (count + (LONG - SHORT - 1)) // LONG
         code = entry * 2048 + (o * PADDED + start)
-        rows += [
-            jnp.where(whole > 0, code, -1),
-            jnp.where(count > whole * LONG, code + whole * LONG, -1),
-            jnp.where(whole > 1, code + LONG, -1),
-            jnp.where(whole > 1, 2, jnp.where(linked, 1, 0)),
-        ]
-    for n, row in enumerate(rows):
-        table[n : n + 1, :] = row
-
-
-def list_steps(table, tasks, blocks):
-    def per_block(k, counts):
-        for o in range(BLOCKS):
-            flags = [table[4 * o + 3, CHUNKS * k + jc] for jc in range(CHUNKS)]
-
-            def add(counts, o=o):
-                counts = list(counts)
-                codes = [[table[4 * o + n, CHUNKS * k + jc] for jc in range(CHUNKS)] for n in range(2)]
-                for jc in range(CHUNKS):
-                    for n, rows in enumerate((LONG, SHORT)):
-                        tasks[FIRST[rows] + counts[n]] = codes[n][jc]
-                        counts[n] += (codes[n][jc] >= 0).astype(jnp.int32)
-                return tuple(counts)
-
-            def more(counts, o=o):
-                long, short = counts
-                for jc in range(CHUNKS):
-                    code = table[4 * o + 2, CHUNKS * k + jc]
-                    tasks[FIRST[LONG] + long] = code
-                    long += (code >= 0).astype(jnp.int32)
-                return long, short
-
-            counts = lax.cond(flags[0] > 0, add, lambda counts: counts, counts)
-            most = jnp.maximum(jnp.maximum(flags[0], flags[1]), jnp.maximum(flags[2], flags[3]))
-            counts = lax.cond(most > 1, more, lambda counts: counts, counts)
-        return counts
-
-    counts = lax.fori_loop(0, blocks, per_block, (jnp.int32(0), jnp.int32(0)))
-    for rows, count in zip((LONG, SHORT), counts):
-        tasks[COUNT[rows]] = count
-        for n in range(AT_ONCE[rows]):
-            tasks[FIRST[rows] + count + n] = NOTHING
+        rows[LONG].append(jnp.where(whole > 0, code, -1))
+        rows[LONG].append(jnp.where(whole > 1, code + LONG, -1))
+        rows[SHORT].append(jnp.where(count > whole * LONG, code + whole * LONG, -1))
+    codes = [row.astype(F32) for row in rows[LONG] + rows[SHORT]]
+    turned[0] = jnp.full((LANES, LANES), -1.0, F32)
+    for n, row in enumerate(codes):
+        turned[0, n : n + 1, :] = row
+    flags = jnp.where(turned[0, 0:8, :] >= 0.0, 1.0, 0.0)
+    earlier = jnp.where(iota((LANES, LANES), 0) < iota((LANES, LANES), 1), 1.0, 0.0)
+    before = nn(flags.astype(BF16), earlier.astype(BF16))
+    held = before[:, LANES - 1 :] + flags[:, LANES - 1 :]
+    totals = {}
+    n = 0
+    for size in (LONG, SHORT):
+        total = jnp.zeros((1, 1), F32)
+        for _ in rows[size]:
+            row = turned[0, n : n + 1, :]
+            turned[0, 8 + n : 9 + n, :] = jnp.where(row >= 0.0, before[n : n + 1, :] + total, -1.0)
+            total = total + held[n : n + 1, :]
+            n += 1
+        totals[size] = total
+    columns = jnp.transpose(turned[0])
+    lengths = jnp.where(entry == COUNT[LONG], totals[LONG], totals[SHORT])
+    lists_out[0:1, :] = lengths.astype(jnp.int32)
+    n = 0
+    for size in (LONG, SHORT):
+        picked = range(n, n + len(rows[size]))
+        n += len(rows[size])
+        for chunk in range(LIST_ROWS[size]):
+            place = (iota((LANES, LANES), 1) + chunk * LANES).astype(F32)
+            found = jnp.zeros((LANES, LANES), F32)
+            for r in picked:
+                found += jnp.where(columns[:, 8 + r : 9 + r] == place, columns[:, r : r + 1], 0.0)
+            row = jnp.sum(found, axis=0, keepdims=True)
+            row = jnp.where(place[0:1, :] < totals[size], row, float(NOTHING))
+            lists_out[FIRST[size] + chunk : FIRST[size] + chunk + 1, :] = row.astype(jnp.int32)
 
 
 def stage_weights(device, d, weights):
@@ -245,8 +239,13 @@
         tile[piece * step : (piece + 1) * step, LANES:] = rest
 
 
-def decode(code):
+def step_at(tasks, rows, n):
+    code = tasks[FIRST[rows] + (n >> 7), n & 127]
     return code >> 11, pl.multiple_of(code & 2047, 8)
+
+
+def length(tasks, rows):
+    return tasks[0, COUNT[rows]]
 
 
 def add_product(at, row, rows, tile, weights, total):
@@ -260,7 +259,7 @@
         begin = skip[rows] // width if skip else 0
 
         def some(i, _):
-            picked = [decode(tasks[FIRST[rows] + width * i + n]) for n in range(width)]
+            picked = [step_at(tasks, rows, width * i + n) for n in range(width)]
             for n in range(width + 1):
                 if n < width:
                     at, row = picked[n]
@@ -270,7 +269,7 @@
                     add_product(at, row, rows, tiles[n - 1, 0:rows], weights, total)
             return 0
 
-        lax.fori_loop(begin, (tasks[COUNT[rows]] + (width - 1)) // width, some, 0)
+        lax.fori_loop(begin, (length(tasks, rows) + (width - 1)) // width, some, 0)
 
 
 def keep_tiles(tasks, own_pos, places, kept):
@@ -279,11 +278,11 @@
 
         def some(i, _):
             for n in range(width):
-                at, row = decode(tasks[FIRST[rows] + width * i + n])
+                at, row = step_at(tasks, rows, width * i + n)
                 eval_tile(at, row, rows, own_pos, places, kept[rows].at[width * i + n])
             return 0
 
-        batches = (tasks[COUNT[rows]] + (width - 1)) // width
+        batches = (length(tasks, rows) + (width - 1)) // width
         lax.fori_loop(0, jnp.minimum(batches, KEPT[rows] // width), some, 0)
 
 
@@ -293,11 +292,11 @@
 
         def some(i, _):
             for n in range(width):
-                at, row = decode(tasks[FIRST[rows] + width * i + n])
+                at, row = step_at(tasks, rows, width * i + n)
                 add_product(at, row, rows, kept[rows][width * i + n], weights, total)
             return 0
 
-        batches = (tasks[COUNT[rows]] + (width - 1)) // width
+        batches = (length(tasks, rows) + (width - 1)) // width
         lax.fori_loop(0, jnp.minimum(batches, KEPT[rows] // width), some, 0)
 
 
@@ -328,7 +327,7 @@
 
 
 def own_kernel(packed, noise, own_pos, own_sum, places, own_tasks, weights, total, tiles, *scratch):
-    turned, table, scalars, sem = scratch
+    turned, lists, sem = scratch
     stage_places(packed, 0, places)
     for o in range(BLOCKS):
         for c in range(NOISE + 1):
@@ -338,13 +337,12 @@
                 row = noise[at : at + 1, :] if c == NOISE else places[at, c : c + 1, :]
                 own_pos[c, first : first + LANES, :] = column(row)
             own_pos[c, padding(o), :] = jnp.zeros((PADDED - STARS, LANES), F32)
-    build_table(places, BLOCKS, 0, lambda o: own_pos[2, own_rows(o), :], lambda e: e >= 0, table, turned)
-    copy = pltpu.make_async_copy(table, scalars, sem)
+    build_lists(places, BLOCKS, 0, lambda o: own_pos[2, own_rows(o), :], lambda e: e >= 0, lists, turned)
+    copy = pltpu.make_async_copy(lists, own_tasks, sem)
     copy.start()
     stage_weights(packed, 0, weights)
     total[...] = jnp.zeros(total.shape, F32)
     copy.wait()
-    list_steps(scalars, own_tasks, BLOCKS)
     run_steps(own_tasks, own_pos, places, weights, total, tiles)
     for o in range(BLOCKS):
         own_sum[o * STARS : (o + 1) * STARS, :] = total[own_rows(o), :]
@@ -353,7 +351,7 @@
 def first_kernel(
     low, mid, high, own_pos, own_sum, image_ref, places, tasks, weights, total, tiles, *scratch
 ):
-    turned, table, scalars, sem = scratch
+    turned, lists, sem = scratch
     groups = (low, mid, high)
     devices = [groups[d // 3].at[d % 3] for d in range(9)]
     for d, device in enumerate(devices):
@@ -362,15 +360,14 @@
     def others(entry):
         return (entry < OWN * CHUNKS) | (entry >= (OWN + BLOCKS) * CHUNKS)
 
-    build_table(places, NEAR, OWN, lambda o: own_pos[2, own_rows(o), :], others, table, turned)
-    copy = pltpu.make_async_copy(table, scalars, sem)
+    build_lists(places, NEAR, OWN, lambda o: own_pos[2, own_rows(o), :], others, lists, turned)
+    copy = pltpu.make_async_copy(lists, tasks, sem)
     copy.start()
     for d, device in enumerate(devices):
         if d != OWN // BLOCKS:
             stage_weights(device, d, weights)
     stage_own_sum(own_sum, total)
     copy.wait()
-    list_steps(scalars, tasks, NEAR)
     run_steps(tasks, own_pos, places, weights, total, tiles)
     image_ref[...] = image_of(total, own_pos, mid[1, 0:STARS, :])
 
@@ -518,7 +515,7 @@
 BLOCK = shape(BLOCKS, WIDTH, STARS)
 OWN_POS = shape(NOISE + 1, BLOCKS * PADDED, LANES)
 OWN_SUM = shape(BLOCKS * STARS, LANES)
-TASKS = shape(LISTS, dtype=jnp.int32)
+TASKS = shape(8, LANES, dtype=jnp.int32)
 
 
 def pairs_scratch(blocks):
@@ -529,10 +526,9 @@
     ]
 
 
-TABLE_SCRATCH = [
+LIST_SCRATCH = [
     pltpu.VMEM((2, LANES, LANES), F32),
     pltpu.VMEM((8, LANES), jnp.int32),
-    pltpu.SMEM((8, LANES), jnp.int32),
     pltpu.SemaphoreType.DMA,
 ]
 
@@ -541,7 +537,7 @@
     return call(
         own_kernel,
         (OWN_POS, OWN_SUM, shape(BLOCKS * CHUNKS, 8, LANES), TASKS),
-        scratch=pairs_scratch(BLOCKS) + TABLE_SCRATCH,
+        scratch=pairs_scratch(BLOCKS) + LIST_SCRATCH,
         count=2,
         out_specs=(VMEM, VMEM, VMEM, SMEM),
         flops=1 << 30,
@@ -552,7 +548,7 @@
     return call(
         first_kernel,
         (shape(STARS, LANES), shape(NEAR * CHUNKS, 8, LANES), TASKS),
-        scratch=pairs_scratch(NEAR) + TABLE_SCRATCH,
+        scratch=pairs_scratch(NEAR) + LIST_SCRATCH,
         count=5,
         out_specs=(VMEM, VMEM, SMEM),
     )(low, mid, high, own_pos, own_sum)
@@ -596,7 +592,8 @@
 
 def with_halo(x):
     before, after = shift(x, "tm", 1), shift(x, "tm", -1)
-    mid = jnp.stack([before, x, after])
+    mid = lax.optimization_barrier(jnp.zeros((3,) + x.shape, F32).at[1].set(x))
+    mid = mid.at[0].set(before).at[2].set(after)
     return sky_shift(mid, 1), mid, sky_shift(mid, -1)
 
 

time: 138 us -> 135 us (0.978)
  the two profiles are of different devices: /device:TPU:8 before, /device:TPU:4 now
where the time goes in v5:
time: 135 us
  blocking collectives  59.8 us (44%)
  Pallas kernels  26.4 us (20%)
  waiting for transfers between devices  22.8 us (17%)
  starting transfers between devices  22.1 us (16%)
  local copies, waits for them, and re-layouts  2.79 us (2%)
    psum x5, blocking collectives, local(): moments = lax.psum(moments, axis)  59.8 us
    ppermute x4, waiting for transfers between devices, shift(): lax.ppermute(x, axis, [(i, i + by) for i in range(count) if 0 <= i + by <...  17.4 us
    ppermute x4, starting transfers between devices, sky_shift(): lax.ppermute(x, SKY, [(i, i + by) for i in range(count) if 0 <= i + by <...  11.1 us
    ppermute x4, starting transfers between devices, shift(): lax.ppermute(x, axis, [(i, i + by) for i in range(count) if 0 <= i + by <...  11 us
    pallas_call x1, Pallas kernels, apply_first(): call(first_kernel, (shape(STARS, LANES), shape(NEAR * CHUNKS, 8, LANES),...  6.41 us
    pallas_call x1, Pallas kernels, apply_between(): call(between_kernel, (OWN_SUM, shape(KEPT[LONG], LONG, 2 * LANES, dtype=B...  6.09 us
    pallas_call x1, Pallas kernels, apply_own(): call(own_kernel, (OWN_POS, OWN_SUM, shape(BLOCKS * CHUNKS, 8, LANES), TAS...  5.82 us
    ppermute x4, waiting for transfers between devices, sky_shift(): lax.ppermute(x, SKY, [(i, i + by) for i in range(count) if 0 <= i + by <...  5.44 us
  transfers between devices with their start and end apart: 8, of which 8 were waited for; matrix products, arithmetic and copies ran while one was open for 1% of the time, Pallas kernels for 9%

profile of v5, /device:TPU:4, one launch (start us, length us, event | category | flops | bytes accessed | tf_op | source)
XLA Modules:
  0.0 134.7 jit_solution(1327569061675158673)
XLA Ops:
  0.6 2.8 %shard_map.59 = (f32[544,128]{1,0:T(8,128)}, f32[2,512]{1,0:T(2,128)}, f32[8,128]{1,0:T(8,128)}) custom-call(s32[1]{0:T(128)} %bitcast.ident_ref, f32[3,2,512]{2,1,0:T(2,128)} %bitcast.14, f32[2,512]{1,0:T(2,128)} %noise_hbm.1, f32[2,64,512]{2,1,0:T(8,128)} %start_ref.1, s32[2,14]{1,0:T(2,128)} %list_hbm.1), custom_call_target="tpu_custom_call" | custom-call | bytes 1048576 | tf_op jit(solution)/shard_map/pallas_call | solution.py:604
  3.4 3.5 %collective-permute-start = (f32[544,128]{1,0:T(8,128)}, f32[544,128]{1,0:T(8,128)S(1)}, u32[]{:S(2)}, u32[]{:S(2)}) collective-permute-start(f32[544,128]{1,0:T(8,128)} %get-tuple-element.89.packed), channel_id=1, source_target_pairs={{0,1},{1,2},{2,3},{4,5},{5,6},{6,7},{8,9},{9,10},{10,11},{12,13},{... | collective-permute-start | bytes 835592 | tf_op jit(solution)/shard_map/ppermute | solution.py:582
  6.9 1.3 collective-permute-start.1
  8.2 1.0 scatter.20
  9.2 3.9 %collective-permute-done = f32[544,128]{1,0:T(8,128)S(1)} collective-permute-done((f32[544,128]{1,0:T(8,128)}, f32[544,128]{1,0:T(8,128)S(1)}, u32[]{:S(2)}, u32[]{:S(2)}) %collective-permute-start) | collective-permute-done | bytes 278560 | tf_op jit(solution)/shard_map/ppermute | solution.py:582
  13.1 4.0 %collective-permute-done.1 = f32[544,128]{1,0:T(8,128)S(1)} collective-permute-done((f32[544,128]{1,0:T(8,128)}, f32[544,128]{1,0:T(8,128)S(1)}, u32[]{:S(2)}, u32[]{:S(2)}) %collective-permute-start.1) | collective-permute-done | bytes 278560 | tf_op jit(solution)/shard_map/ppermute | solution.py:582
  17.2 1.9 %collective-permute-start.2 = (f32[3,544,128]{2,1,0:T(8,128)S(1)}, f32[3,544,128]{2,1,0:T(8,128)S(1)}, u32[]{:S(2)}, u32[]{:S(2)}) collective-permute-start(f32[3,544,128]{2,1,0:T(8,128)S(1)} %bitcast_dynamic-update-slice_fusion.mid), channel_id=1, source_target_pairs={{0,4},{4,8},{8,12},{12,16},{16,20},{20,24},{24,28},{28,32},{32,36}... | collective-permute-start | bytes 2506760 | tf_op jit(solution)/shard_map/ppermute | solution.py:590
  19.1 3.6 %collective-permute-start.3 = (f32[3,544,128]{2,1,0:T(8,128)S(1)}, f32[3,544,128]{2,1,0:T(8,128)S(1)}, u32[]{:S(2)}, u32[]{:S(2)}) collective-permute-start(f32[3,544,128]{2,1,0:T(8,128)S(1)} %bitcast_dynamic-update-slice_fusion.mid), channel_id=1, source_target_pairs={{4,0},{8,4},{12,8},{16,12},{20,16},{24,20},{28,24},{32,28},{36,32}... | collective-permute-start | bytes 2506760 | tf_op jit(solution)/shard_map/ppermute | solution.py:590
  22.8 0.0 copy-start
  22.8 0.9 copy-done
  23.7 0.0 copy-start.4
  23.7 0.7 copy-done.4
  24.4 5.8 %shard_map.60 = (f32[4,1536,128]{2,1,0:T(8,128)S(1)}, f32[1024,128]{1,0:T(8,128)S(1)}, f32[8,8,128]{2,1,0:T(8,128)S(1)}, s32[8,128]{1,0:T(8,128)S(1)}) custom-call(f32[544,128]{1,0:T(8,128)S(1)} %copy-done, f32[8,128]{1,0:T(8,128)S(1)} %copy-done.4), custom_call_target="tpu_custom_call" | custom-call | flops 1073741824 | bytes 1048576 | tf_op jit(solution)/shard_map/pallas_call | solution.py:537
  30.2 0.8 collective-permute-done.2.low
  31.0 1.8 %collective-permute-done.3.high = f32[3,544,128]{2,1,0:T(8,128)S(1)} collective-permute-done((f32[3,544,128]{2,1,0:T(8,128)S(1)}, f32[3,544,128]{2,1,0:T(8,128)S(1)}, u32[]{:S(2)}, u32[]{:S(2)}) %collective-permute-start.3) | collective-permute-done | bytes 835616 | tf_op jit(solution)/shard_map/ppermute | solution.py:590
  32.8 0.0 copy-start.3
  32.8 6.4 %shard_map.61 = (f32[512,128]{1,0:T(8,128)S(1)}, f32[72,8,128]{2,1,0:T(8,128)S(1)}, s32[8,128]{1,0:T(8,128)S(1)}) custom-call(f32[3,544,128]{2,1,0:T(8,128)S(1)} %collective-permute-done.2.low, f32[3,544,128]{2,1,0:T(8,128)S(1)} %bitcast_dynamic-update-slice_fusion.mid, f32[3,544,128]{2,1,0:T(8,128)S(1)} %collective-permute-done.3.high, ...), custom_call_target="tpu_custom_call" | custom-call | bytes 1048576 | tf_op jit(solution)/shard_map/pallas_call | solution.py:548
  39.2 4.9 %collective-permute-start.4 = (f32[512,128]{1,0:T(8,128)S(1)}, f32[512,128]{1,0:T(8,128)S(1)}, u32[]{:S(2)}, u32[]{:S(2)}) collective-permute-start(f32[512,128]{1,0:T(8,128)S(1)} %get-tuple-element.94.once.x_ref), channel_id=1, source_target_pairs={{0,1},{1,2},{2,3},{4,5},{5,6},{6,7},{8,9},{9,10},{10,11},{12,13},{... | collective-permute-start | bytes 786440 | tf_op jit(solution)/shard_map/ppermute | solution.py:582
  44.1 1.3 collective-permute-start.5
  45.4 0.1 scatter.25
  45.5 0.0 copy-start.1
  45.5 4.5 %collective-permute-done.4 = f32[512,128]{1,0:T(8,128)S(1)} collective-permute-done((f32[512,128]{1,0:T(8,128)S(1)}, f32[512,128]{1,0:T(8,128)S(1)}, u32[]{:S(2)}, u32[]{:S(2)}) %collective-permute-start.4) | collective-permute-done | bytes 262176 | tf_op jit(solution)/shard_map/ppermute | solution.py:582
  50.0 5.0 %collective-permute-done.5 = f32[512,128]{1,0:T(8,128)S(1)} collective-permute-done((f32[512,128]{1,0:T(8,128)S(1)}, f32[512,128]{1,0:T(8,128)S(1)}, u32[]{:S(2)}, u32[]{:S(2)}) %collective-permute-start.5) | collective-permute-done | bytes 262176 | tf_op jit(solution)/shard_map/ppermute | solution.py:582
  55.0 1.9 %collective-permute-start.6 = (f32[3,512,128]{2,1,0:T(8,128)S(1)}, f32[3,512,128]{2,1,0:T(8,128)S(1)}, u32[]{:S(2)}, u32[]{:S(2)}) collective-permute-start(f32[3,512,128]{2,1,0:T(8,128)S(1)} %bitcast_dynamic-update-slice_fusion.2.mid), channel_id=1, source_target_pairs={{0,4},{4,8},{8,12},{12,16},{16,20},{20,24},{24,28},{28,32},{32,36}... | collective-permute-start | bytes 2359304 | tf_op jit(solution)/shard_map/ppermute | solution.py:590
  56.9 3.6 %collective-permute-start.7 = (f32[3,512,128]{2,1,0:T(8,128)S(1)}, f32[3,512,128]{2,1,0:T(8,128)S(1)}, u32[]{:S(2)}, u32[]{:S(2)}) collective-permute-start(f32[3,512,128]{2,1,0:T(8,128)S(1)} %bitcast_dynamic-update-slice_fusion.2.mid), channel_id=1, source_target_pairs={{4,0},{8,4},{12,8},{16,12},{20,16},{24,20},{28,24},{32,28},{36,32}... | collective-permute-start | bytes 2359304 | tf_op jit(solution)/shard_map/ppermute | solution.py:590
  60.6 0.0 copy-done.3
  60.6 0.5 shard_map.64.once_ref
  61.1 6.1 %shard_map.62 = (f32[1024,128]{1,0:T(8,128)S(1)}, bf16[40,256,256]{2,1,0:T(8,128)(2,1)S(1)}, bf16[48,64,256]{2,1,0:T(8,128)(2,1)S(1)}) custom-call(s32[8,128]{1,0:T(8,128)S(1)} %get-tuple-element.95.own_tasks, s32[8,128]{1,0:T(8,128)S(1)} %get-tuple-element.93.tasks, f32[512,128]{1,0:T(8,128)S(1)} %get-tuple-element.94.once.x_ref, ...), custom_call_target="tpu_custom_call" | custom-call | flops 1073741824 | bytes 1048576 | tf_op jit(solution)/shard_map/pallas_call | solution.py:558
  67.1 1.2 collective-permute-done.6.low
  68.3 1.8 %collective-permute-done.7.high = f32[3,512,128]{2,1,0:T(8,128)S(1)} collective-permute-done((f32[3,512,128]{2,1,0:T(8,128)S(1)}, f32[3,512,128]{2,1,0:T(8,128)S(1)}, u32[]{:S(2)}, u32[]{:S(2)}) %collective-permute-start.7) | collective-permute-done | bytes 786464 | tf_op jit(solution)/shard_map/ppermute | solution.py:590
  70.1 0.0 copy-done.1
  70.1 0.0 copy-start.2
  70.1 3.7 %shard_map.63 = (f32[2,64,512]{2,1,0:T(8,128)S(1)}, f32[8,128]{1,0:T(8,128)S(1)}) custom-call(s32[8,128]{1,0:T(8,128)S(1)} %get-tuple-element.93.tasks, f32[3,512,128]{2,1,0:T(8,128)S(1)} %collective-permute-done.6.low, f32[3,512,128]{2,1,0:T(8,128)S(1)} %bitcast_dynamic-update-slice_fusion.2.mid, f32[3,512,128]{2,1,0:T(8,128)S(1)} %collective-permute-done.7.high, ...), custom_call_target="tpu_custom_call" | custom-call | bytes 1048576 | tf_op jit(solution)/shard_map/pallas_call | solution.py:572
  73.8 2.5 %psum.35 = f32[8,128]{1,0:T(8,128)S(1)} all-reduce(f32[8,128]{1,0:T(8,128)S(1)} %get-tuple-element.102), channel_id=1, replica_groups=mesh['far'=4,'near'=4,'x'=4,'core'=2,'tm'=4] {'core'}, use_global_device_ids=true, to_apply=%region_0.0 | all-reduce | flops 1024 | bytes 8192 | tf_op jit(solution)/shard_map/psum | solution.py:629
  76.3 14.4 %psum.36 = f32[8,128]{1,0:T(8,128)S(1)} all-reduce(f32[8,128]{1,0:T(8,128)S(1)} %psum.35), channel_id=1, replica_groups=mesh['far'=4,'near'=4,'x'=4,'core'=2,'tm'=4] {'x'}, use_global_device_ids=true, to_apply=%region_1.0 | all-reduce | flops 1024 | bytes 8192 | tf_op jit(solution)/shard_map/psum | solution.py:629
  90.7 7.9 %psum.37 = f32[8,128]{1,0:T(8,128)S(1)} all-reduce(f32[8,128]{1,0:T(8,128)S(1)} %psum.36), channel_id=1, replica_groups=mesh['far'=4,'near'=4,'x'=4,'core'=2,'tm'=4] {'tm'}, use_global_device_ids=true, to_apply=%region_2.0 | all-reduce | flops 1024 | bytes 8192 | tf_op jit(solution)/shard_map/psum | solution.py:629
  98.6 18.1 %psum.38 = f32[8,128]{1,0:T(8,128)S(1)} all-reduce(f32[8,128]{1,0:T(8,128)S(1)} %psum.37), channel_id=1, replica_groups=mesh['far'=4,'near'=4,'x'=4,'core'=2,'tm'=4] {'near'}, use_global_device_ids=true, to_apply=%region_3.0 | all-reduce | flops 1024 | bytes 8192 | tf_op jit(solution)/shard_map/psum | solution.py:629
  116.7 16.9 %psum.39.moments_ref = f32[8,128]{1,0:T(8,128)S(1)} all-reduce(f32[8,128]{1,0:T(8,128)S(1)} %psum.38), channel_id=1, replica_groups=mesh['far'=4,'near'=4,'x'=4,'core'=2,'tm'=4] {'far'}, use_global_device_ids=true, to_apply=%region_4.0 | all-reduce | flops 1024 | bytes 8192 | tf_op jit(solution)/shard_map/psum | solution.py:629
  133.6 0.0 copy-done.2
  133.6 1.1 shard_map.65
  (4 shorter events, 0.1 us)
Async XLA Ops:
  3.4 9.7 %collective-permute-start = (f32[544,128]{1,0:T(8,128)}, f32[544,128]{1,0:T(8,128)S(1)}, u32[]{:S(2)}, u32[]{:S(2)}) collective-permute-start(f32[544,128]{1,0:T(8,128)} %get-tuple-element.89.packed), channel_id=1, source_target_pairs={{0,1},{1,2},{2,3},{4,5},{5,6},{6,7},{8,9},{9,10},{10,11},{12,13},{... | collective-permute-start | bytes 835592 | tf_op jit(solution)/shard_map/ppermute | solution.py:582
  6.9 10.2 %collective-permute-start.1 = (f32[544,128]{1,0:T(8,128)}, f32[544,128]{1,0:T(8,128)S(1)}, u32[]{:S(2)}, u32[]{:S(2)}) collective-permute-start(f32[544,128]{1,0:T(8,128)} %get-tuple-element.89.packed), channel_id=1, source_target_pairs={{1,0},{2,1},{3,2},{5,4},{6,5},{7,6},{9,8},{10,9},{11,10},{13,12},{... | collective-permute-start | bytes 835592 | tf_op jit(solution)/shard_map/ppermute | solution.py:582
  17.2 13.8 %collective-permute-start.2 = (f32[3,544,128]{2,1,0:T(8,128)S(1)}, f32[3,544,128]{2,1,0:T(8,128)S(1)}, u32[]{:S(2)}, u32[]{:S(2)}) collective-permute-start(f32[3,544,128]{2,1,0:T(8,128)S(1)} %bitcast_dynamic-update-slice_fusion.mid), channel_id=1, source_target_pairs={{0,4},{4,8},{8,12},{12,16},{16,20},{20,24},{24,28},{28,32},{32,36}... | collective-permute-start | bytes 2506760 | tf_op jit(solution)/shard_map/ppermute | solution.py:590
  19.1 13.7 %collective-permute-start.3 = (f32[3,544,128]{2,1,0:T(8,128)S(1)}, f32[3,544,128]{2,1,0:T(8,128)S(1)}, u32[]{:S(2)}, u32[]{:S(2)}) collective-permute-start(f32[3,544,128]{2,1,0:T(8,128)S(1)} %bitcast_dynamic-update-slice_fusion.mid), channel_id=1, source_target_pairs={{4,0},{8,4},{12,8},{16,12},{20,16},{24,20},{28,24},{32,28},{36,32}... | collective-permute-start | bytes 2506760 | tf_op jit(solution)/shard_map/ppermute | solution.py:590
  22.8 1.0 copy-start
  23.7 0.7 copy-start.4
  32.8 27.8 %copy-start.3 = (f32[2,512]{1,0:T(2,128)S(1)}, f32[2,512]{1,0:T(2,128)}, u32[]{:S(2)}) copy-start(f32[2,512]{1,0:T(2,128)} %get-tuple-element.101.rank.rank_ref) | copy-start | bytes 12292
  39.2 10.8 %collective-permute-start.4 = (f32[512,128]{1,0:T(8,128)S(1)}, f32[512,128]{1,0:T(8,128)S(1)}, u32[]{:S(2)}, u32[]{:S(2)}) collective-permute-start(f32[512,128]{1,0:T(8,128)S(1)} %get-tuple-element.94.once.x_ref), channel_id=1, source_target_pairs={{0,1},{1,2},{2,3},{4,5},{5,6},{6,7},{8,9},{9,10},{10,11},{12,13},{... | collective-permute-start | bytes 786440 | tf_op jit(solution)/shard_map/ppermute | solution.py:582
  44.1 10.9 %collective-permute-start.5 = (f32[512,128]{1,0:T(8,128)S(1)}, f32[512,128]{1,0:T(8,128)S(1)}, u32[]{:S(2)}, u32[]{:S(2)}) collective-permute-start(f32[512,128]{1,0:T(8,128)S(1)} %get-tuple-element.94.once.x_ref), channel_id=1, source_target_pairs={{1,0},{2,1},{3,2},{5,4},{6,5},{7,6},{9,8},{10,9},{11,10},{13,12},{... | collective-permute-start | bytes 786440 | tf_op jit(solution)/shard_map/ppermute | solution.py:582
  45.5 24.6 %copy-start.1 = (f32[544,128]{1,0:T(8,128)S(1)}, f32[544,128]{1,0:T(8,128)}, u32[]{:S(2)}) copy-start(f32[544,128]{1,0:T(8,128)} %get-tuple-element.89.packed) | copy-start | bytes 835588
  55.0 13.3 %collective-permute-start.6 = (f32[3,512,128]{2,1,0:T(8,128)S(1)}, f32[3,512,128]{2,1,0:T(8,128)S(1)}, u32[]{:S(2)}, u32[]{:S(2)}) collective-permute-start(f32[3,512,128]{2,1,0:T(8,128)S(1)} %bitcast_dynamic-update-slice_fusion.2.mid), channel_id=1, source_target_pairs={{0,4},{4,8},{8,12},{12,16},{16,20},{20,24},{24,28},{28,32},{32,36}... | collective-permute-start | bytes 2359304 | tf_op jit(solution)/shard_map/ppermute | solution.py:590
  56.9 13.1 %collective-permute-start.7 = (f32[3,512,128]{2,1,0:T(8,128)S(1)}, f32[3,512,128]{2,1,0:T(8,128)S(1)}, u32[]{:S(2)}, u32[]{:S(2)}) collective-permute-start(f32[3,512,128]{2,1,0:T(8,128)S(1)} %bitcast_dynamic-update-slice_fusion.2.mid), channel_id=1, source_target_pairs={{4,0},{8,4},{12,8},{16,12},{20,16},{24,20},{28,24},{32,28},{36,32}... | collective-permute-start | bytes 2359304 | tf_op jit(solution)/shard_map/ppermute | solution.py:590
  70.1 63.5 %copy-start.2 = (f32[2,64,512]{2,1,0:T(8,128)S(1)}, f32[2,64,512]{2,1,0:T(8,128)}, u32[]{:S(2)}) copy-start(f32[2,64,512]{2,1,0:T(8,128)} %start_ref.1) | copy-start | bytes 786436

commit v6 on v5

--- a/solution.py
+++ b/solution.py
@@ -19,6 +19,8 @@
 OWN = 8
 LONG, SHORT = 256, 64
 AT_ONCE = {LONG: 4, SHORT: 8}
+AT_END = {LONG: 1, SHORT: 4}
+FEW = {LONG: 2, SHORT: 4}
 KEPT = {LONG: 40, SHORT: 48}
 PADDED = STARS + LONG
 NOTHING = STARS
@@ -253,13 +255,30 @@
     total[pl.ds(row, rows), :] += nn(tile, both)
 
 
+def in_batches(tasks, rows, first, last, some):
+    width, narrow = AT_ONCE[rows], AT_END[rows]
+    shift_wide, shift_narrow = width.bit_length() - 1, narrow.bit_length() - 1
+
+    def wide(i, _):
+        some(first + width * i, width)
+        return 0
+
+    whole = (jnp.maximum(last - first, 0) + (width - 1 - FEW[rows])) >> shift_wide
+    lax.fori_loop(0, whole, wide, 0)
+    rest = first + width * whole
+
+    def few(i, _):
+        some(rest + narrow * i, narrow)
+        return 0
+
+    lax.fori_loop(0, (jnp.maximum(last - rest, 0) + (narrow - 1)) >> shift_narrow, few, 0)
+
+
 def run_steps(tasks, own_pos, places, weights, total, tiles, skip=None):
     for rows in (LONG, SHORT):
-        width = AT_ONCE[rows]
-        begin = skip[rows] // width if skip else 0
-
-        def some(i, _):
-            picked = [step_at(tasks, rows, width * i + n) for n in range(width)]
+
+        def some(first, width, rows=rows):
+            picked = [step_at(tasks, rows, first + n) for n in range(width)]
             for n in range(width + 1):
                 if n < width:
                     at, row = picked[n]
@@ -267,37 +286,30 @@
                 if n > 0:
                     at, row = picked[n - 1]
                     add_product(at, row, rows, tiles[n - 1, 0:rows], weights, total)
-            return 0
-
-        lax.fori_loop(begin, (length(tasks, rows) + (width - 1)) // width, some, 0)
+
+        in_batches(tasks, rows, skip[rows] if skip else 0, length(tasks, rows), some)
 
 
 def keep_tiles(tasks, own_pos, places, kept):
     for rows in (LONG, SHORT):
-        width = AT_ONCE[rows]
-
-        def some(i, _):
+
+        def some(first, width, rows=rows):
             for n in range(width):
-                at, row = step_at(tasks, rows, width * i + n)
-                eval_tile(at, row, rows, own_pos, places, kept[rows].at[width * i + n])
-            return 0
-
-        batches = (length(tasks, rows) + (width - 1)) // width
-        lax.fori_loop(0, jnp.minimum(batches, KEPT[rows] // width), some, 0)
+                at, row = step_at(tasks, rows, first + n)
+                eval_tile(at, row, rows, own_pos, places, kept[rows].at[first + n])
+
+        in_batches(tasks, rows, 0, jnp.minimum(length(tasks, rows), KEPT[rows]), some)
 
 
 def run_kept(tasks, kept, weights, total):
     for rows in (LONG, SHORT):
-        width = AT_ONCE[rows]
-
-        def some(i, _):
+
+        def some(first, width, rows=rows):
             for n in range(width):
-                at, row = step_at(tasks, rows, width * i + n)
-                add_product(at, row, rows, kept[rows][width * i + n], weights, total)
-            return 0
-
-        batches = (length(tasks, rows) + (width - 1)) // width
-        lax.fori_loop(0, jnp.minimum(batches, KEPT[rows] // width), some, 0)
+                at, row = step_at(tasks, rows, first + n)
+                add_product(at, row, rows, kept[rows][first + n], weights, total)
+
+        in_batches(tasks, rows, 0, jnp.minimum(length(tasks, rows), KEPT[rows]), some)
 
 
 def own_rows(o):

time: 135 us -> 135 us (level)
  the two profiles are of different devices: /device:TPU:4 before, /device:TPU:8 now
where the time goes in v6:
time: 135 us
  blocking collectives  69.8 us (52%)
  starting transfers between devices  28.4 us (21%)
  Pallas kernels  23.8 us (18%)
  waiting for transfers between devices  9.25 us (7%)
  local copies, waits for them, and re-layouts  2.8 us (2%)
    psum x5, blocking collectives, local(): moments = lax.psum(moments, axis)  69.8 us
    ppermute x4, starting transfers between devices, shift(): lax.ppermute(x, axis, [(i, i + by) for i in range(count) if 0 <= i + by <...  14.9 us
    ppermute x4, starting transfers between devices, sky_shift(): lax.ppermute(x, SKY, [(i, i + by) for i in range(count) if 0 <= i + by <...  13.5 us
    ppermute x4, waiting for transfers between devices, shift(): lax.ppermute(x, axis, [(i, i + by) for i in range(count) if 0 <= i + by <...  9.24 us
    pallas_call x1, Pallas kernels, apply_own(): call(own_kernel, (OWN_POS, OWN_SUM, shape(BLOCKS * CHUNKS, 8, LANES), TAS...  5.71 us
    pallas_call x1, Pallas kernels, apply_first(): call(first_kernel, (shape(STARS, LANES), shape(NEAR * CHUNKS, 8, LANES),...  5.21 us
    pallas_call x1, Pallas kernels, apply_between(): call(between_kernel, (OWN_SUM, shape(KEPT[LONG], LONG, 2 * LANES, dtype=B...  5.12 us
    pallas_call x1, Pallas kernels, apply_second(): call(second_kernel, (BLOCK, shape(8, LANES)), scratch=pairs_scratch(NEAR)...  3.39 us
  transfers between devices with their start and end apart: 8, of which 4 were waited for; matrix products, arithmetic and copies ran while one was open for 1% of the time, Pallas kernels for 8%

profile of v6, /device:TPU:8, one launch (start us, length us, event | category | flops | bytes accessed | tf_op | source)
XLA Modules:
  0.0 134.9 jit_solution(9563097016679915769)
XLA Ops:
  0.6 2.8 %shard_map.59 = (f32[544,128]{1,0:T(8,128)}, f32[2,512]{1,0:T(2,128)}, f32[8,128]{1,0:T(8,128)}) custom-call(s32[1]{0:T(128)} %bitcast.ident_ref, f32[3,2,512]{2,1,0:T(2,128)} %bitcast.14, f32[2,512]{1,0:T(2,128)} %noise_hbm.1, f32[2,64,512]{2,1,0:T(8,128)} %start_ref.1, s32[2,14]{1,0:T(2,128)} %list_hbm.1), custom_call_target="tpu_custom_call" | custom-call | bytes 1048576 | tf_op jit(solution)/shard_map/pallas_call | solution.py:616
  3.4 3.5 %collective-permute-start = (f32[544,128]{1,0:T(8,128)}, f32[544,128]{1,0:T(8,128)S(1)}, u32[]{:S(2)}, u32[]{:S(2)}) collective-permute-start(f32[544,128]{1,0:T(8,128)} %get-tuple-element.89.packed), channel_id=1, source_target_pairs={{0,1},{1,2},{2,3},{4,5},{5,6},{6,7},{8,9},{9,10},{10,11},{12,13},{... | collective-permute-start | bytes 835592 | tf_op jit(solution)/shard_map/ppermute | solution.py:594
  6.9 5.6 %collective-permute-start.1 = (f32[544,128]{1,0:T(8,128)}, f32[544,128]{1,0:T(8,128)S(1)}, u32[]{:S(2)}, u32[]{:S(2)}) collective-permute-start(f32[544,128]{1,0:T(8,128)} %get-tuple-element.89.packed), channel_id=1, source_target_pairs={{1,0},{2,1},{3,2},{5,4},{6,5},{7,6},{9,8},{10,9},{11,10},{13,12},{... | collective-permute-start | bytes 835592 | tf_op jit(solution)/shard_map/ppermute | solution.py:594
  12.5 1.0 scatter.20
  13.5 1.8 %collective-permute-done = f32[544,128]{1,0:T(8,128)S(1)} collective-permute-done((f32[544,128]{1,0:T(8,128)}, f32[544,128]{1,0:T(8,128)S(1)}, u32[]{:S(2)}, u32[]{:S(2)}) %collective-permute-start) | collective-permute-done | bytes 278560 | tf_op jit(solution)/shard_map/ppermute | solution.py:594
  15.3 1.8 %collective-permute-done.1 = f32[544,128]{1,0:T(8,128)S(1)} collective-permute-done((f32[544,128]{1,0:T(8,128)}, f32[544,128]{1,0:T(8,128)S(1)}, u32[]{:S(2)}, u32[]{:S(2)}) %collective-permute-start.1) | collective-permute-done | bytes 278560 | tf_op jit(solution)/shard_map/ppermute | solution.py:594
  17.2 1.3 collective-permute-start.2
  18.5 1.3 collective-permute-start.3
  19.8 0.0 copy-start
  19.8 0.9 copy-done
  20.8 0.0 copy-start.4
  20.8 0.7 copy-done.4
  21.5 5.7 %shard_map.60 = (f32[4,1536,128]{2,1,0:T(8,128)S(1)}, f32[1024,128]{1,0:T(8,128)S(1)}, f32[8,8,128]{2,1,0:T(8,128)S(1)}, s32[8,128]{1,0:T(8,128)S(1)}) custom-call(f32[544,128]{1,0:T(8,128)S(1)} %copy-done, f32[8,128]{1,0:T(8,128)S(1)} %copy-done.4), custom_call_target="tpu_custom_call" | custom-call | flops 1073741824 | bytes 1048576 | tf_op jit(solution)/shard_map/pallas_call | solution.py:549
  27.2 0.0 collective-permute-done.2.low
  27.2 0.0 collective-permute-done.3.high
  27.2 0.0 copy-start.3
  27.2 5.2 %shard_map.61 = (f32[512,128]{1,0:T(8,128)S(1)}, f32[72,8,128]{2,1,0:T(8,128)S(1)}, s32[8,128]{1,0:T(8,128)S(1)}) custom-call(f32[3,544,128]{2,1,0:T(8,128)S(1)} %collective-permute-done.2.low, f32[3,544,128]{2,1,0:T(8,128)S(1)} %bitcast_dynamic-update-slice_fusion.mid, f32[3,544,128]{2,1,0:T(8,128)S(1)} %collective-permute-done.3.high, ...), custom_call_target="tpu_custom_call" | custom-call | bytes 1048576 | tf_op jit(solution)/shard_map/pallas_call | solution.py:560
  32.4 3.3 %collective-permute-start.4 = (f32[512,128]{1,0:T(8,128)S(1)}, f32[512,128]{1,0:T(8,128)S(1)}, u32[]{:S(2)}, u32[]{:S(2)}) collective-permute-start(f32[512,128]{1,0:T(8,128)S(1)} %get-tuple-element.94.once.x_ref), channel_id=1, source_target_pairs={{0,1},{1,2},{2,3},{4,5},{5,6},{6,7},{8,9},{9,10},{10,11},{12,13},{... | collective-permute-start | bytes 786440 | tf_op jit(solution)/shard_map/ppermute | solution.py:594
  35.8 2.5 %collective-permute-start.5 = (f32[512,128]{1,0:T(8,128)S(1)}, f32[512,128]{1,0:T(8,128)S(1)}, u32[]{:S(2)}, u32[]{:S(2)}) collective-permute-start(f32[512,128]{1,0:T(8,128)S(1)} %get-tuple-element.94.once.x_ref), channel_id=1, source_target_pairs={{1,0},{2,1},{3,2},{5,4},{6,5},{7,6},{9,8},{10,9},{11,10},{13,12},{... | collective-permute-start | bytes 786440 | tf_op jit(solution)/shard_map/ppermute | solution.py:594
  38.3 0.1 scatter.25
  38.4 0.0 copy-start.1
  38.4 2.3 %collective-permute-done.4 = f32[512,128]{1,0:T(8,128)S(1)} collective-permute-done((f32[512,128]{1,0:T(8,128)S(1)}, f32[512,128]{1,0:T(8,128)S(1)}, u32[]{:S(2)}, u32[]{:S(2)}) %collective-permute-start.4) | collective-permute-done | bytes 262176 | tf_op jit(solution)/shard_map/ppermute | solution.py:594
  40.7 3.3 %collective-permute-done.5 = f32[512,128]{1,0:T(8,128)S(1)} collective-permute-done((f32[512,128]{1,0:T(8,128)S(1)}, f32[512,128]{1,0:T(8,128)S(1)}, u32[]{:S(2)}, u32[]{:S(2)}) %collective-permute-start.5) | collective-permute-done | bytes 262176 | tf_op jit(solution)/shard_map/ppermute | solution.py:594
  44.0 9.6 %collective-permute-start.6 = (f32[3,512,128]{2,1,0:T(8,128)S(1)}, f32[3,512,128]{2,1,0:T(8,128)S(1)}, u32[]{:S(2)}, u32[]{:S(2)}) collective-permute-start(f32[3,512,128]{2,1,0:T(8,128)S(1)} %bitcast_dynamic-update-slice_fusion.2.mid), channel_id=1, source_target_pairs={{0,4},{4,8},{8,12},{12,16},{16,20},{20,24},{24,28},{28,32},{32,36}... | collective-permute-start | bytes 2359304 | tf_op jit(solution)/shard_map/ppermute | solution.py:602
  53.6 1.3 collective-permute-start.7
  54.9 0.0 copy-done.3
  54.9 0.5 shard_map.64.once_ref
  55.4 5.1 %shard_map.62 = (f32[1024,128]{1,0:T(8,128)S(1)}, bf16[40,256,256]{2,1,0:T(8,128)(2,1)S(1)}, bf16[48,64,256]{2,1,0:T(8,128)(2,1)S(1)}) custom-call(s32[8,128]{1,0:T(8,128)S(1)} %get-tuple-element.95.own_tasks, s32[8,128]{1,0:T(8,128)S(1)} %get-tuple-element.93.tasks, f32[512,128]{1,0:T(8,128)S(1)} %get-tuple-element.94.once.x_ref, ...), custom_call_target="tpu_custom_call" | custom-call | flops 1073741824 | bytes 1048576 | tf_op jit(solution)/shard_map/pallas_call | solution.py:570
  60.5 0.0 collective-permute-done.6.low
  60.5 0.0 collective-permute-done.7.high
  60.6 0.0 copy-done.1
  60.6 0.0 copy-start.2
  60.6 3.4 %shard_map.63 = (f32[2,64,512]{2,1,0:T(8,128)S(1)}, f32[8,128]{1,0:T(8,128)S(1)}) custom-call(s32[8,128]{1,0:T(8,128)S(1)} %get-tuple-element.93.tasks, f32[3,512,128]{2,1,0:T(8,128)S(1)} %collective-permute-done.6.low, f32[3,512,128]{2,1,0:T(8,128)S(1)} %bitcast_dynamic-update-slice_fusion.2.mid, f32[3,512,128]{2,1,0:T(8,128)S(1)} %collective-permute-done.7.high, ...), custom_call_target="tpu_custom_call" | custom-call | bytes 1048576 | tf_op jit(solution)/shard_map/pallas_call | solution.py:584
  64.0 12.3 %psum.35 = f32[8,128]{1,0:T(8,128)S(1)} all-reduce(f32[8,128]{1,0:T(8,128)S(1)} %get-tuple-element.102), channel_id=1, replica_groups=mesh['far'=4,'near'=4,'x'=4,'core'=2,'tm'=4] {'core'}, use_global_device_ids=true, to_apply=%region_0.0 | all-reduce | flops 1024 | bytes 8192 | tf_op jit(solution)/shard_map/psum | solution.py:641
  76.3 14.7 %psum.36 = f32[8,128]{1,0:T(8,128)S(1)} all-reduce(f32[8,128]{1,0:T(8,128)S(1)} %psum.35), channel_id=1, replica_groups=mesh['far'=4,'near'=4,'x'=4,'core'=2,'tm'=4] {'x'}, use_global_device_ids=true, to_apply=%region_1.0 | all-reduce | flops 1024 | bytes 8192 | tf_op jit(solution)/shard_map/psum | solution.py:641
  91.0 8.4 %psum.37 = f32[8,128]{1,0:T(8,128)S(1)} all-reduce(f32[8,128]{1,0:T(8,128)S(1)} %psum.36), channel_id=1, replica_groups=mesh['far'=4,'near'=4,'x'=4,'core'=2,'tm'=4] {'tm'}, use_global_device_ids=true, to_apply=%region_2.0 | all-reduce | flops 1024 | bytes 8192 | tf_op jit(solution)/shard_map/psum | solution.py:641
  99.4 15.9 %psum.38 = f32[8,128]{1,0:T(8,128)S(1)} all-reduce(f32[8,128]{1,0:T(8,128)S(1)} %psum.37), channel_id=1, replica_groups=mesh['far'=4,'near'=4,'x'=4,'core'=2,'tm'=4] {'near'}, use_global_device_ids=true, to_apply=%region_3.0 | all-reduce | flops 1024 | bytes 8192 | tf_op jit(solution)/shard_map/psum | solution.py:641
  115.3 18.5 %psum.39.moments_ref = f32[8,128]{1,0:T(8,128)S(1)} all-reduce(f32[8,128]{1,0:T(8,128)S(1)} %psum.38), channel_id=1, replica_groups=mesh['far'=4,'near'=4,'x'=4,'core'=2,'tm'=4] {'far'}, use_global_device_ids=true, to_apply=%region_4.0 | all-reduce | flops 1024 | bytes 8192 | tf_op jit(solution)/shard_map/psum | solution.py:641
  133.8 0.0 copy-done.2
  133.8 1.1 shard_map.65
  (4 shorter events, 0.1 us)
Async XLA Ops:
  3.4 11.8 %collective-permute-start = (f32[544,128]{1,0:T(8,128)}, f32[544,128]{1,0:T(8,128)S(1)}, u32[]{:S(2)}, u32[]{:S(2)}) collective-permute-start(f32[544,128]{1,0:T(8,128)} %get-tuple-element.89.packed), channel_id=1, source_target_pairs={{0,1},{1,2},{2,3},{4,5},{5,6},{6,7},{8,9},{9,10},{10,11},{12,13},{... | collective-permute-start | bytes 835592 | tf_op jit(solution)/shard_map/ppermute | solution.py:594
  6.9 10.2 %collective-permute-start.1 = (f32[544,128]{1,0:T(8,128)}, f32[544,128]{1,0:T(8,128)S(1)}, u32[]{:S(2)}, u32[]{:S(2)}) collective-permute-start(f32[544,128]{1,0:T(8,128)} %get-tuple-element.89.packed), channel_id=1, source_target_pairs={{1,0},{2,1},{3,2},{5,4},{6,5},{7,6},{9,8},{10,9},{11,10},{13,12},{... | collective-permute-start | bytes 835592 | tf_op jit(solution)/shard_map/ppermute | solution.py:594
  17.2 10.0 %collective-permute-start.2 = (f32[3,544,128]{2,1,0:T(8,128)S(1)}, f32[3,544,128]{2,1,0:T(8,128)S(1)}, u32[]{:S(2)}, u32[]{:S(2)}) collective-permute-start(f32[3,544,128]{2,1,0:T(8,128)S(1)} %bitcast_dynamic-update-slice_fusion.mid), channel_id=1, source_target_pairs={{0,4},{4,8},{8,12},{12,16},{16,20},{20,24},{24,28},{28,32},{32,36}... | collective-permute-start | bytes 2506760 | tf_op jit(solution)/shard_map/ppermute | solution.py:602
  18.5 8.7 %collective-permute-start.3 = (f32[3,544,128]{2,1,0:T(8,128)S(1)}, f32[3,544,128]{2,1,0:T(8,128)S(1)}, u32[]{:S(2)}, u32[]{:S(2)}) collective-permute-start(f32[3,544,128]{2,1,0:T(8,128)S(1)} %bitcast_dynamic-update-slice_fusion.mid), channel_id=1, source_target_pairs={{4,0},{8,4},{12,8},{16,12},{20,16},{24,20},{28,24},{32,28},{36,32}... | collective-permute-start | bytes 2506760 | tf_op jit(solution)/shard_map/ppermute | solution.py:602
  19.8 1.0 copy-start
  20.8 0.7 copy-start.4
  27.2 27.7 %copy-start.3 = (f32[2,512]{1,0:T(2,128)S(1)}, f32[2,512]{1,0:T(2,128)}, u32[]{:S(2)}) copy-start(f32[2,512]{1,0:T(2,128)} %get-tuple-element.101.rank.rank_ref) | copy-start | bytes 12292
  32.4 8.3 %collective-permute-start.4 = (f32[512,128]{1,0:T(8,128)S(1)}, f32[512,128]{1,0:T(8,128)S(1)}, u32[]{:S(2)}, u32[]{:S(2)}) collective-permute-start(f32[512,128]{1,0:T(8,128)S(1)} %get-tuple-element.94.once.x_ref), channel_id=1, source_target_pairs={{0,1},{1,2},{2,3},{4,5},{5,6},{6,7},{8,9},{9,10},{10,11},{12,13},{... | collective-permute-start | bytes 786440 | tf_op jit(solution)/shard_map/ppermute | solution.py:594
  35.8 8.3 %collective-permute-start.5 = (f32[512,128]{1,0:T(8,128)S(1)}, f32[512,128]{1,0:T(8,128)S(1)}, u32[]{:S(2)}, u32[]{:S(2)}) collective-permute-start(f32[512,128]{1,0:T(8,128)S(1)} %get-tuple-element.94.once.x_ref), channel_id=1, source_target_pairs={{1,0},{2,1},{3,2},{5,4},{6,5},{7,6},{9,8},{10,9},{11,10},{13,12},{... | collective-permute-start | bytes 786440 | tf_op jit(solution)/shard_map/ppermute | solution.py:594
  38.4 22.2 %copy-start.1 = (f32[544,128]{1,0:T(8,128)S(1)}, f32[544,128]{1,0:T(8,128)}, u32[]{:S(2)}) copy-start(f32[544,128]{1,0:T(8,128)} %get-tuple-element.89.packed) | copy-start | bytes 835588
  44.0 16.5 %collective-permute-start.6 = (f32[3,512,128]{2,1,0:T(8,128)S(1)}, f32[3,512,128]{2,1,0:T(8,128)S(1)}, u32[]{:S(2)}, u32[]{:S(2)}) collective-permute-start(f32[3,512,128]{2,1,0:T(8,128)S(1)} %bitcast_dynamic-update-slice_fusion.2.mid), channel_id=1, source_target_pairs={{0,4},{4,8},{8,12},{12,16},{16,20},{20,24},{24,28},{28,32},{32,36}... | collective-permute-start | bytes 2359304 | tf_op jit(solution)/shard_map/ppermute | solution.py:602
  53.6 6.9 %collective-permute-start.7 = (f32[3,512,128]{2,1,0:T(8,128)S(1)}, f32[3,512,128]{2,1,0:T(8,128)S(1)}, u32[]{:S(2)}, u32[]{:S(2)}) collective-permute-start(f32[3,512,128]{2,1,0:T(8,128)S(1)} %bitcast_dynamic-update-slice_fusion.2.mid), channel_id=1, source_target_pairs={{4,0},{8,4},{12,8},{16,12},{20,16},{24,20},{28,24},{32,28},{36,32}... | collective-permute-start | bytes 2359304 | tf_op jit(solution)/shard_map/ppermute | solution.py:602
  60.6 73.2 %copy-start.2 = (f32[2,64,512]{2,1,0:T(8,128)S(1)}, f32[2,64,512]{2,1,0:T(8,128)}, u32[]{:S(2)}) copy-start(f32[2,64,512]{2,1,0:T(8,128)} %start_ref.1) | copy-start | bytes 786436
